TPU v7x, 512 devices: a whole 4x4x16 slice. The times are simulated.
512 devices in a mesh: member: 16 (over y, z_hi), dp: 32 (over x, z_lo, core).
Axes of the slice: x: 4, y: 4, z: 16 (z_hi: 4, z_lo: 4; z = z_hi * 4 + z_lo), core: 2. Of those that a mesh axis runs over, the one named last changes fastest.
Arguments:
- features: bfloat16 [16, 512, 49, 1024], P('member', 'dp'), may hold values from -8 to 8
- labels: int32 [512], replicated, may hold values from 0 to 24575
- norm_gain: float32 [16, 1024], P('member'), may hold values from 0.75 to 1.25
- norm_bias: float32 [16, 1024], P('member'), may hold values from -0.25 to 0.25
- head_weight: bfloat16 [16, 1024, 24576], P('member', None, 'dp'), may hold values from -3 to 3
- head_bias: float32 [16, 24576], P('member', 'dp'), may hold values from -1.25 to 1.25
Outputs:
- mean_loss: float32 [], replicated
- grad_pooled: float32 [16, 512, 1024], P('member', 'dp')
- grad_gain: float32 [16, 1024], P('member')
- grad_bias: float32 [16, 1024], P('member')
- grad_head_weight: bfloat16 [16, 1024, 24576], P('member', None, 'dp')
- grad_head_bias: float32 [16, 24576], P('member', 'dp')
All inputs are finite; a program needn't handle non-finite values.
Results may differ from a plain program's by a relative error of at most 0.025.
Values may be sent and summed in bfloat16 or wider, within the bound.
No kernel may reach another device: no remote copies, remote signals or barrier semaphores. Data moves between devices by JAX's collectives and lax.ppermute only.
A program may use at most 64 MiB of HBM per device.

v0:
```python
import math

import jax
import jax.numpy as jnp
from jax import lax
from jax.sharding import PartitionSpec as P

norm_eps = 1e-06
loss_scale = 16.0


def merged(x, axis, combine):
    everything = jax.tree.map(lambda part: lax.all_gather(part, axis), x)
    initial = jax.tree.map(lambda part: part[0], everything)

    def hop(k, so_far):
        return combine(so_far, jax.tree.map(lambda part: part[k], everything))

    return lax.fori_loop(1, lax.axis_size(axis), hop, initial)


def layer_norm(pooled, norm_gain, norm_shift):
    center = pooled - jnp.mean(pooled, axis=-1, keepdims=True)
    inverse = lax.rsqrt(jnp.mean(center * center, axis=-1, keepdims=True) + norm_eps)
    normed = center * inverse
    return (normed, inverse, (normed * norm_gain + norm_shift).astype(jnp.bfloat16))


def norm_backward(upstream, normed, inverse, norm_gain):
    scaled = upstream * norm_gain
    return inverse * (
        scaled
        - jnp.mean(scaled, axis=-1, keepdims=True)
        - normed * jnp.mean(scaled * normed, axis=-1, keepdims=True)
    )


def member_join(former, latter):
    highest = jnp.maximum(former[0], latter[0])
    return (
        highest,
        former[1] * jnp.exp(former[0] - highest) + latter[1] * jnp.exp(latter[0] - highest),
    )


def per_device(features, labels, norm_gain, norm_bias, head_weight, head_bias):
    weight = head_weight[0]
    classes_here = weight.shape[1]
    gain_row = norm_gain[0]
    shift_row = norm_bias[0]
    position = lax.axis_index("dp")
    pooled = jnp.sum(features[0], axis=1, dtype=jnp.float32) / features.shape[2]
    normed, inverse, act = layer_norm(pooled, gain_row, shift_row)
    act_all = lax.all_gather(act, "dp", axis=0, tiled=True)
    logits = jnp.dot(act_all, weight, preferred_element_type=jnp.float32) + head_bias[0]
    local_class = labels - position * classes_here
    onehot = (local_class[:, None] == jnp.arange(classes_here, dtype=jnp.int32)[None, :]).astype(
        jnp.float32
    )
    label_part = jnp.sum(logits * onehot, axis=1)
    top_part = jnp.max(logits, axis=1)
    sum_part = jnp.sum(jnp.exp(logits - top_part[:, None]), axis=1)
    top_all = lax.pmax(top_part, "dp")
    sum_all, label_logit = lax.psum((sum_part * jnp.exp(top_part - top_all), label_part), "dp")
    log_total = top_all + jnp.log(sum_all)
    label_logp = label_logit - log_total
    mix_top, mix_sum = merged((label_logp, jnp.ones_like(label_logp)), "member", member_join)
    log_joint = mix_top + jnp.log(mix_sum)
    mean_loss = math.log(lax.axis_size("member")) - jnp.mean(log_joint)
    respons = jnp.exp(label_logp - log_joint)
    probabilities = jnp.exp(logits - log_total[:, None])
    grad_logits = (loss_scale * respons)[:, None] * (probabilities - onehot)
    grad_low = grad_logits.astype(jnp.bfloat16)
    grad_head_bias = jnp.sum(grad_logits, axis=0)
    grad_head_weight = lax.dot_general(
        act_all, grad_low, (((0,), (0,)), ((), ())), preferred_element_type=jnp.float32
    ).astype(jnp.bfloat16)
    upstream = lax.psum_scatter(
        lax.dot_general(
            grad_low, weight, (((1,), (1,)), ((), ())), preferred_element_type=jnp.float32
        ),
        "dp",
        scatter_dimension=0,
        tiled=True,
    )
    grad_gain, grad_shift = lax.psum(
        (jnp.sum(upstream * normed, axis=0), jnp.sum(upstream, axis=0)), "dp"
    )
    grad_pooled = norm_backward(upstream, normed, inverse, gain_row)
    return (
        mean_loss,
        grad_pooled[None],
        grad_gain[None],
        grad_shift[None],
        grad_head_weight[None],
        grad_head_bias[None],
    )


def solution(mesh):
    in_specs = (
        P("member", "dp", None, None),
        P(),
        P("member", None),
        P("member", None),
        P("member", None, "dp"),
        P("member", "dp"),
    )
    out_specs = (
        P(),
        P("member", "dp", None),
        P("member", None),
        P("member", None),
        P("member", None, "dp"),
        P("member", "dp"),
    )
    return jax.shard_map(
        per_device, mesh=mesh, in_specs=in_specs, out_specs=out_specs, check_vma=False
    )
```

profile of v0, /device:TPU:1, one launch (start us, length us, event | category | flops | bytes accessed | tf_op | source)
XLA Modules:
  0.0 497.9 jit_solution(16176686166835715571)
XLA Ops:
  7.2 0.0 copy-start
  7.2 0.0 copy-start.2
  7.2 0.0 copy-start.1
  7.2 0.0 copy-start.3
  7.2 0.0 copy-start.4
  7.2 0.0 all-gather.4.cloned.1.call-start
  7.3 1.8 convert_reduce_fusion
  9.0 0.1 multiply_reduce_fusion.4
  9.2 0.2 multiply_reduce_fusion.2
  9.4 0.0 copy-done.2
  9.4 0.0 copy-done.1
  9.4 0.7 add_convert_fusion
  10.1 0.0 all-gather.4.cloned.1.call-update
  10.1 0.0 reduce-scatter.2.cloned.1.call-start
  10.2 0.0 copy-done.3
  10.2 0.0 copy-done.4
  10.2 70.3 %all-gather.4.cloned.1.call-done = bf16[512,1024]{1,0:T(8,128)(2,1)} async-done(((bf16[16,1024]{1,0:T(8,128)(2,1)}), bf16[512,1024]{1,0:T(8,128)(2,1)}) %all-gather.4.cloned.1.call-update) | async-done | bytes 1048592 | tf_op jit(solution)/shard_map/all_gather | solution.py:54
  80.5 0.0 copy-done
  80.5 2.3 fusion.15
  82.8 67.0 %pmax.7 = f32[512]{0:T(512)S(1)} all-reduce(f32[512]{0:T(512)S(1)} %get-tuple-element.169), channel_id=1, replica_groups=mesh['member'=16,'dp'=32] {'dp'}, use_global_device_ids=true, to_apply=%region_6.0 | all-reduce | flops 512 | bytes 4096 | tf_op jit(solution)/shard_map/pmax | solution.py:63
  149.8 0.6 exponential_reduce_fusion
  150.4 70.2 %all-reduce.1 = (f32[512]{0:T(512)S(1)}, f32[512]{0:T(512)S(1)}) all-reduce(f32[512]{0:T(512)S(1)} %get-tuple-element.146, f32[512]{0:T(512)S(1)} %exponential_multiply_fusion.1), channel_id=1, replica_groups=mesh['member'=16,'dp'=32] {'dp'}, use_global_device_ids=true, to_apply=%region_4.0 | all-reduce | flops 1024 | bytes 8192 | tf_op jit(solution)/shard_map/psum | solution.py:64
  220.6 45.5 %all-gather.1 = f32[16,1,512]{2,1,0:T(1,128)S(1)} all-gather(f32[1,1,512]{2,1,0:T(1,128)S(1)} %bitcast.33), channel_id=2, replica_groups=mesh['member'=16,'dp'=32] {'member'}, dimensions={0}, use_global_device_ids=true | all-gather | bytes 34816 | tf_op jit(solution)/shard_map/all_gather | solution.py:13
  266.1 0.9 while.18
  267.0 0.6 exponential_multiply_fusion
  267.6 2.5 fusion.1
  270.1 0.0 reduce-scatter.2.cloned.1.call-update
  270.2 0.5 fusion.9
  270.7 0.6 broadcast_in_dim.28
  271.9 3.7 fusion.8
  275.6 138.1 %reduce-scatter.2.cloned.1.call-done = f32[16,1024]{1,0:T(8,128)} async-done(((f32[512,1024]{1,0:T(8,128)}), f32[16,1024]{1,0:T(8,128)}) %reduce-scatter.2.cloned.1.call-update) | async-done | bytes 65552 | tf_op jit(solution)/shard_map/reduce_scatter | solution.py:78
  413.7 1.0 multiply_reduce_fusion
  414.8 73.6 %all-reduce = (f32[1,1024]{1,0:T(1,128)}, f32[1,1024]{1,0:T(1,128)}) all-reduce(f32[1,1024]{1,0:T(1,128)S(1)} %bitcast.34, f32[1,1024]{1,0:T(1,128)S(1)} %bitcast.35), channel_id=1, replica_groups=mesh['member'=16,'dp'=32] {'dp'}, use_global_device_ids=true, to_apply=%region_16.0 | all-reduce | flops 2048 | bytes 16384 | tf_op jit(solution)/shard_map/psum | solution.py:86
  488.4 1.6 multiply_bitcast_fusion
  (40 shorter events, 0.5 us)
Async XLA Ops:
  7.2 73.4 %copy-start = (bf16[1,1024,768]{2,1,0:T(8,128)(2,1)S(1)}, bf16[1,1024,768]{2,1,0:T(8,128)(2,1)}, u32[]{:S(2)}) copy-start(bf16[1,1024,768]{2,1,0:T(8,128)(2,1)} %param.12) | copy-start | bytes 4718596
  7.2 2.2 copy-start.2
  7.2 2.2 copy-start.1
  7.2 3.0 copy-start.3
  7.2 3.0 copy-start.4
  7.2 73.3 %all-gather.4.cloned.1.call-start = ((), (), s32[]{:S(2)}) async-start(), calls=%async_computation.1 | async-start | bytes 1081344 | tf_op jit(solution)/shard_map/all_gather | solution.py:54
  10.1 403.6 %reduce-scatter.2.cloned.1.call-start = ((), (), s32[]{:S(2)}) async-start(), calls=%async_computation.2 | async-start | bytes 2162688 | tf_op jit(solution)/shard_map/reduce_scatter | solution.py:78
Sparse Core Ops, SparseCore 0:
  10.8 69.6 all-gather.3
  270.3 143.3 reduce-scatter.1
where the time goes:
time: 498 us
  blocking collectives  256 us (51%)
  waiting for transfers between devices  208 us (42%)
  between operations  16 us (3%)
  matrix products  8.5 us (2%)
  other arithmetic  7.42 us (1%)
    reduce_scatter x1, waiting for transfers between devices, per_device(): lax.psum_scatter(lax.dot_general(grad_low, weight, (((1,), (1,)), ((), ()...  138 us
    psum x1, blocking collectives, per_device(): lax.psum((jnp.sum(upstream * normed, axis=0), jnp.sum(upstream, axis=0)),...  73.6 us
    all_gather x1, waiting for transfers between devices, per_device(): act_all = lax.all_gather(act, 'dp', axis=0, tiled=True)  70.3 us
    psum x1, blocking collectives, per_device(): lax.psum((sum_part * jnp.exp(top_part - top_all), label_part), 'dp')  70.2 us
    pmax x1, blocking collectives, per_device(): top_all = lax.pmax(top_part, 'dp')  67 us
    all_gather x1, blocking collectives, merged(): everything = jax.tree.map(lambda part: lax.all_gather(part, axis), x)  45.5 us
  transfers between devices with their start and end apart: 2, of which 2 were waited for; matrix products, arithmetic and copies ran while one was open for 1% of the time, Pallas kernels for 0%

commit v1 on v0

v1 whole, which is shorter than its diff:
```python
import math

import jax
import jax.numpy as jnp
from jax import lax
from jax.sharding import PartitionSpec as P

norm_eps = 1e-06
loss_scale = 16.0


def layer_norm(pooled, norm_gain, norm_shift):
    center = pooled - jnp.mean(pooled, axis=-1, keepdims=True)
    inverse = lax.rsqrt(jnp.mean(center * center, axis=-1, keepdims=True) + norm_eps)
    normed = center * inverse
    return (normed, inverse, (normed * norm_gain + norm_shift).astype(jnp.bfloat16))


def norm_backward(upstream, normed, inverse, norm_gain):
    scaled = upstream * norm_gain
    return inverse * (
        scaled
        - jnp.mean(scaled, axis=-1, keepdims=True)
        - normed * jnp.mean(scaled * normed, axis=-1, keepdims=True)
    )


def per_device(features, labels, norm_gain, norm_bias, head_weight, head_bias):
    dp = lax.axis_size("dp")
    members = lax.axis_size("member")
    chips = dp // 2
    position = lax.axis_index("dp")
    core = lax.rem(position, 2)
    swap = [(i, i ^ 1) for i in range(dp)]
    planes = [[2 * chip + c for chip in range(chips)] for c in range(2)]

    def over_plane(x):
        return lax.all_to_all(x, "dp", 0, 0, axis_index_groups=planes)

    weight = head_weight[0]
    classes_here = weight.shape[1]
    gain_row = norm_gain[0]
    shift_row = norm_bias[0]
    images_here = features.shape[1]
    plane_images = chips * images_here

    weight_other = lax.ppermute(weight, "dp", swap)
    bias_other = lax.ppermute(head_bias[0], "dp", swap)

    pooled = jnp.sum(features[0], axis=1, dtype=jnp.float32) / features.shape[2]
    normed, inverse, act = layer_norm(pooled, gain_row, shift_row)
    act_plane = over_plane(jnp.broadcast_to(act[None], (chips,) + act.shape)).reshape(
        plane_images, -1
    )
    act_other = lax.ppermute(act_plane, "dp", swap)

    plane_labels = lax.dynamic_index_in_dim(
        labels.reshape(chips, 2, images_here), core, axis=1, keepdims=False
    ).reshape(plane_images)
    class_ids = jnp.arange(classes_here, dtype=jnp.int32)[None, :]
    onehot_mine = (plane_labels - position * classes_here)[:, None] == class_ids
    onehot_other = (plane_labels - (position ^ 1) * classes_here)[:, None] == class_ids
    logits_mine = jnp.dot(act_plane, weight, preferred_element_type=jnp.float32) + head_bias[0]
    logits_other = (
        jnp.dot(act_plane, weight_other, preferred_element_type=jnp.float32) + bias_other
    )
    top = jnp.maximum(jnp.max(logits_mine, axis=1), jnp.max(logits_other, axis=1))
    total = jnp.sum(jnp.exp(logits_mine - top[:, None]), axis=1) + jnp.sum(
        jnp.exp(logits_other - top[:, None]), axis=1
    )
    label_part = jnp.sum(jnp.where(onehot_mine, logits_mine, 0.0), axis=1) + jnp.sum(
        jnp.where(onehot_other, logits_other, 0.0), axis=1
    )
    stats = jnp.stack([top + jnp.log(total), label_part])
    stats_all = over_plane(jnp.broadcast_to(stats[None], (chips,) + stats.shape))
    logs = stats_all[:, 0]
    logs_top = jnp.max(logs, axis=0)
    log_total = logs_top + jnp.log(jnp.sum(jnp.exp(logs - logs_top), axis=0))
    label_logp = jnp.sum(stats_all[:, 1], axis=0) - log_total

    logp_all = lax.all_to_all(
        jnp.broadcast_to(label_logp[None], (members, plane_images)), "member", 0, 0
    )

    diff_mine = jnp.exp(logits_mine - log_total[:, None]) - onehot_mine.astype(jnp.float32)
    diff_other = jnp.exp(logits_other - log_total[:, None]) - onehot_other.astype(jnp.float32)
    low_mine = diff_mine.astype(jnp.bfloat16)
    low_other = diff_other.astype(jnp.bfloat16)
    contract = (((1,), (1,)), ((), ()))
    partial = lax.dot_general(
        low_mine, weight, contract, preferred_element_type=jnp.float32
    ) + lax.dot_general(low_other, weight_other, contract, preferred_element_type=jnp.float32)
    pieces = over_plane(partial.astype(jnp.bfloat16).reshape(chips, images_here, -1))
    low_received = lax.ppermute(low_other, "dp", swap)

    joint_top = jnp.max(logp_all, axis=0)
    log_joint = joint_top + jnp.log(jnp.sum(jnp.exp(logp_all - joint_top), axis=0))
    scale = loss_scale * jnp.exp(label_logp - log_joint)

    shift_sum = jnp.sum(scale[:, None] * partial, axis=0)
    act_sum = jnp.sum(scale[:, None] * partial * act_plane.astype(jnp.float32), axis=0)
    sums = jnp.stack([shift_sum, act_sum])
    sums = jnp.sum(
        lax.all_to_all(jnp.broadcast_to(sums[None], (dp,) + sums.shape), "dp", 0, 0), axis=0
    )
    grad_shift = sums[0]
    grad_gain = (sums[1] - shift_row * grad_shift) / gain_row

    grad_other = jnp.sum(scale[:, None] * diff_other, axis=0)
    note = jnp.concatenate([scale, log_joint, grad_other])
    note = lax.ppermute(note, "dp", swap)
    scale_other = note[:plane_images]
    mean_loss = math.log(members) - (
        jnp.sum(log_joint) + jnp.sum(note[plane_images : 2 * plane_images])
    ) / (2 * plane_images)
    grad_mine = scale[:, None] * diff_mine
    grad_head_bias = jnp.sum(grad_mine, axis=0) + note[2 * plane_images :]
    rows = (((0,), (0,)), ((), ()))
    grad_head_weight = (
        lax.dot_general(
            act_plane, grad_mine.astype(jnp.bfloat16), rows, preferred_element_type=jnp.float32
        )
        + lax.dot_general(
            act_other,
            (scale_other[:, None] * low_received.astype(jnp.float32)).astype(jnp.bfloat16),
            rows,
            preferred_element_type=jnp.float32,
        )
    ).astype(jnp.bfloat16)

    scale_own = lax.dynamic_slice_in_dim(scale, (position // 2) * images_here, images_here)
    upstream = scale_own[:, None] * jnp.sum(pieces.astype(jnp.float32), axis=0)
    grad_pooled = norm_backward(upstream, normed, inverse, gain_row)
    return (
        mean_loss,
        grad_pooled[None],
        grad_gain[None],
        grad_shift[None],
        grad_head_weight[None],
        grad_head_bias[None],
    )


def solution(mesh):
    in_specs = (
        P("member", "dp", None, None),
        P(),
        P("member", None),
        P("member", None),
        P("member", None, "dp"),
        P("member", "dp"),
    )
    out_specs = (
        P(),
        P("member", "dp", None),
        P("member", None),
        P("member", None),
        P("member", None, "dp"),
        P("member", "dp"),
    )
    return jax.shard_map(
        per_device, mesh=mesh, in_specs=in_specs, out_specs=out_specs, check_vma=False
    )
```

time: 498 us -> 120 us (0.24)
  blocking collectives: 256 us -> 27.9 us
  waiting for transfers between devices: 208 us -> 22 us
  starting transfers between devices: 0.08 us -> 40.7 us
  between operations: 16 us -> 3.39 us
  matrix products: 8.5 us -> 14.5 us
    psum x2 -> x0, blocking collectives: 144 us -> none  [the longest x1 73.6 us: per_device(): lax.psum((jnp.sum(upstream * normed, axis=0), jnp.sum(upstream, axis=0)),...]
    reduce_scatter x1 -> x0, waiting for transfers between devices: 138 us -> none  [per_device(): lax.psum_scatter(lax.dot_general(grad_low, weight, (((1,), (1,)), ((), ()...]
    all_gather x1 -> x0, waiting for transfers between devices: 70.3 us -> none  [per_device(): act_all = lax.all_gather(act, 'dp', axis=0, tiled=True)]
    pmax x1 -> x0, blocking collectives: 67 us -> none  [per_device(): top_all = lax.pmax(top_part, 'dp')]
    all_gather x1 -> x0, blocking collectives: 45.5 us -> none  [merged(): everything = jax.tree.map(lambda part: lax.all_gather(part, axis), x)]
    all_to_all x0 -> x3, starting transfers between devices: none -> 28.5 us  [the longest x1 15.2 us: per_device(): lax.all_to_all(jnp.broadcast_to(label_logp[None], (members, plane_images)...]
    all_to_all x0 -> x2, blocking collectives: none -> 27.9 us  [the longest x1 17.9 us: per_device(): lax.all_to_all(jnp.broadcast_to(sums[None], (dp,) + sums.shape), 'dp', 0, 0)]
    all_to_all x0 -> x3, waiting for transfers between devices: none -> 21.9 us  [the longest x1 11.6 us: per_device(): lax.all_to_all(jnp.broadcast_to(label_logp[None], (members, plane_images)...]
  transfers between devices with their start and end apart: 2 -> 8, of which waited for: 2 -> 3; matrix products, arithmetic and copies ran while one was open for 1% -> 10% of each run, Pallas kernels for 0% -> 0%
where the time goes in v1:
time: 120 us; the launch traced here: 119 us
  starting transfers between devices  40.7 us (34%)
  blocking collectives  27.9 us (23%)
  waiting for transfers between devices  22 us (18%)
  matrix products  14.5 us (12%)
  other arithmetic  8.32 us (7%)
  between operations  3.39 us (3%)
  local copies, waits for them, and re-layouts  2.49 us (2%)
    all_to_all x1, blocking collectives, per_device(): lax.all_to_all(jnp.broadcast_to(sums[None], (dp,) + sums.shape), 'dp', 0, 0)  17.9 us
    all_to_all x1, starting transfers between devices, per_device(): lax.all_to_all(jnp.broadcast_to(label_logp[None], (members, plane_images)...  15.2 us
    all_to_all x2, starting transfers between devices, over_plane(): return lax.all_to_all(x, 'dp', 0, 0, axis_index_groups=planes)  13.3 us
    all_to_all x1, waiting for transfers between devices, per_device(): lax.all_to_all(jnp.broadcast_to(label_logp[None], (members, plane_images)...  11.6 us
    all_to_all x2, waiting for transfers between devices, over_plane(): return lax.all_to_all(x, 'dp', 0, 0, axis_index_groups=planes)  10.4 us
    all_to_all x1, blocking collectives, over_plane(): return lax.all_to_all(x, 'dp', 0, 0, axis_index_groups=planes)  9.93 us
    ppermute x1, starting transfers between devices, per_device(): weight_other = lax.ppermute(weight, 'dp', swap)  3.96 us
    dot_general x1, matrix products, per_device(): lax.dot_general(low_other, weight_other, contract, preferred_element_type...  3.11 us
  transfers between devices with their start and end apart: 8, of which 3 were waited for; matrix products, arithmetic and copies ran while one was open for 10% of the time, Pallas kernels for 0%

profile of v1, /device:TPU:1, one launch (start us, length us, event | category | flops | bytes accessed | tf_op | source)
XLA Modules:
  0.0 119.2 jit_solution(15000264676579140361)
XLA Ops:
  0.6 0.0 copy-start.3
  0.6 0.0 copy-start.2
  0.7 0.0 copy-start.1
  0.7 0.0 copy-start.4
  0.7 0.0 copy-start.5
  0.7 1.8 %convert_reduce_fusion = f32[16,1024]{1,0:T(8,128)S(1)} fusion(bf16[1,16,49,1024]{3,1,2,0:T(8,128)(2,1)} %param.6), kind=kLoop, calls=%fused_computation | loop fusion | flops 1589248 | bytes 1671168 | tf_op jit(solution)/shard_map/reduce_sum | solution.py:50
  2.5 0.1 multiply_reduce_fusion.6
  2.6 0.2 multiply_reduce_fusion.5
  2.8 0.0 copy-done.3
  2.8 0.0 copy-done.2
  2.8 0.1 add_convert_fusion.1
  2.9 0.9 broadcast_in_dim.17
  3.8 9.1 %all-to-all-start = ((bf16[16,16,1024]{2,1,0:T(8,128)(2,1)}), bf16[16,16,1024]{2,1,0:T(8,128)(2,1)}, u32[]{:S(2)}, u32[]{:S(2)}) async-start(bf16[16,16,1024]{2,1,0:T(8,128)(2,1)} %broadcast_in_dim.17), calls=%async_computation | async-start | bytes 1048576 | tf_op jit(solution)/shard_map/all_to_all | solution.py:38
  12.8 0.0 copy-done.1
  12.8 4.0 %collective-permute-start = (bf16[1024,768]{1,0:T(8,128)(2,1)S(1)}, bf16[1024,768]{1,0:T(8,128)(2,1)}, u32[]{:S(2)}, u32[]{:S(2)}) collective-permute-start(bf16[1024,768]{1,0:T(8,128)(2,1)S(1)} %bitcast.55), channel_id=1, source_target_pairs={{0,1},{1,0},{2,3},{3,2},{4,5},{5,4},{6,7},{7,6},{8,9},{9,8},{10,11... | collective-permute-start | bytes 4718600 | tf_op jit(solution)/shard_map/ppermute | solution.py:47
  16.8 0.0 copy-done.4
  16.8 1.9 %collective-permute-start.1 = (f32[768]{0:T(1024)S(1)}, f32[768]{0:T(1024)S(1)}, u32[]{:S(2)}, u32[]{:S(2)}) collective-permute-start(f32[768]{0:T(1024)S(1)} %reduce.4), channel_id=1, source_target_pairs={{0,1},{1,0},{2,3},{3,2},{4,5},{5,4},{6,7},{7,6},{8,9},{9,8},{10,11... | collective-permute-start | bytes 9224 | tf_op jit(solution)/shard_map/ppermute | solution.py:48
  18.8 0.0 copy-done.5
  18.8 0.1 reshape.386
  18.9 0.1 subtract_reduce_fusion
  18.9 0.1 sub.162
  19.0 0.1 sub.159
  19.1 9.4 %all-to-all-done = bf16[16,16,1024]{2,1,0:T(8,128)(2,1)} async-done(((bf16[16,16,1024]{2,1,0:T(8,128)(2,1)}), bf16[16,16,1024]{2,1,0:T(8,128)(2,1)}, u32[]{:S(2)}, u32[]{:S(2)}) %all-to-all-start) | async-done | bytes 524320 | tf_op jit(solution)/shard_map/all_to_all | solution.py:38
  28.5 1.7 %fusion.28 = (f32[256]{0:T(256)S(1)}, f32[256,768]{1,0:T(8,128)S(1)}) fusion(f32[768]{0:T(1024)S(1)} %reduce.4, bf16[256,1024]{1,0:T(8,128)(2,1)} %bitcast.2, bf16[1,1024,768]{2,1,0:T(8,128)(2,1)S(1)} %copy-done.1), kind=kOutput, calls=%fused_computation.74 | convolution fusion | flops 403046144 | bytes 2887680 | tf_op jit(solution)/shard_map/dot_general | solution.py:63
  30.2 0.0 copy-start
  30.2 0.0 collective-permute-done.1
  30.2 0.0 collective-permute-done
  30.3 2.5 %fusion.29 = (f32[256]{0:T(256)S(1)}, f32[256,768]{1,0:T(8,128)S(1)}) fusion(f32[768]{0:T(1024)S(1)} %collective-permute-done.1, bf16[256,1024]{1,0:T(8,128)(2,1)} %bitcast.2, bf16[1024,768]{1,0:T(8,128)(2,1)} %collective-permute-done), kind=kOutput, calls=%fused_computation.75 | convolution fusion | flops 403046144 | bytes 2887680 | tf_op jit(solution)/shard_map/dot_general | solution.py:65
  32.8 0.6 exponential_reduce_fusion
  33.5 9.9 %all_to_all.29 = f32[16,2,256]{2,1,0:T(2,128)S(1)} all-to-all(f32[16,2,256]{2,1,0:T(2,128)S(1)} %broadcast_in_dim.19), channel_id=1, replica_groups={{0,2,4,6,8,10,12,14,16,18,20,22,24,26,28,30},{1,3,5,7,9,11,13,15,17,19,..., dimensions={0} | all-to-all | bytes 65536 | tf_op jit(solution)/shard_map/all_to_all | solution.py:38
  43.4 0.1 slice_reduce_fusion.2
  43.5 0.6 broadcast_in_dim.20
  44.1 15.2 %all-to-all-start.2 = ((f32[16,1,256]{2,1,0:T(1,128)}), f32[16,1,256]{2,1,0:T(1,128)S(1)}, u32[]{:S(2)}, u32[]{:S(2)}) async-start(f32[16,1,256]{2,1,0:T(1,128)} %broadcast_in_dim.20), calls=%async_computation.2 | async-start | bytes 32768 | tf_op jit(solution)/shard_map/all_to_all | solution.py:81
  59.3 2.1 %fusion.3 = f32[256,1024]{1,0:T(8,128)S(1)} fusion(f32[256,768]{1,0:T(8,128)S(1)} %get-tuple-element.34, f32[256]{0:T(256)S(1)} %get-tuple-element.27, s32[256]{0:T(256)S(1)} %sub.159, bf16[1,1024,768]{2,1,0:T(8,128)(2,1)} %param.10), kind=kOutput, calls=%fused_computation.23 | convolution fusion | flops 403636224 | bytes 3409920 | tf_op jit(solution)/shard_map/dot_general | solution.py:90
  61.4 11.6 %all-to-all-done.2 = f32[16,1,256]{2,1,0:T(1,128)S(1)} async-done(((f32[16,1,256]{2,1,0:T(1,128)}), f32[16,1,256]{2,1,0:T(1,128)S(1)}, u32[]{:S(2)}, u32[]{:S(2)}) %all-to-all-start.2) | async-done | bytes 16416 | tf_op jit(solution)/shard_map/all_to_all | solution.py:81
  73.0 0.0 copy-done
  73.0 1.3 %multiply_reduce_fusion.3 = (f32[768]{0:T(1024)S(1)}, f32[768]{0:T(1024)S(1)}, bf16[256,768]{1,0:T(8,128)(2,1)}) fusion(f32[256,768]{1,0:T(8,128)S(1)} %get-tuple-element.34, f32[256]{0:T(256)S(1)} %get-tuple-element.27, f32[256]{0:T(256)S(1)} %get-tuple-element.24, s32[256]{0:T(256)S(1)} %sub.159, s32[256]{0:T(256)S(1)} %sub.162, ...), kind=kLoop, calls=%fused_computation.19 | loop fusion | flops 2554368 | bytes 1976320 | tf_op jit(solution)/shard_map/reduce_sum | solution.py:117
  74.3 3.1 %multiply_reduce_fusion.1 = (f32[1024]{0:T(1024)S(1)}, f32[1024]{0:T(1024)S(1)}, bf16[256,1024]{1,0:T(8,128)(2,1)}) fusion(f32[256]{0:T(256)S(1)} %get-tuple-element.24, bf16[16,16,1024]{2,1,0:T(8,128)(2,1)} %all-to-all-done, f32[256,1024]{1,0:T(8,128)S(1)} %fusion.3, bf16[256,768]{1,0:T(8,128)(2,1)} %get-tuple-element.29, ...), kind=kOutput, calls=%fused_computation.8 | convolution fusion | flops 404486144 | bytes 4072448 | tf_op jit(solution)/shard_map/dot_general | solution.py:92
  77.4 0.1 broadcast_in_dim.21
  77.5 17.9 %all_to_all.30 = f32[32,2,1024]{2,1,0:T(2,128)S(1)} all-to-all(f32[32,2,1024]{2,1,0:T(2,128)S(1)} %broadcast_in_dim.21), channel_id=1, replica_groups=mesh['member'=16,'dp'=32] {'dp'}, dimensions={0} | all-to-all | bytes 524288 | tf_op jit(solution)/shard_map/all_to_all | solution.py:104
  95.4 4.2 %all-to-all-start.3 = ((bf16[16,16,1024]{2,1,0:T(8,128)(2,1)}), bf16[16,16,1024]{2,1,0:T(8,128)(2,1)}, u32[]{:S(2)}, u32[]{:S(2)}) async-start(bf16[16,16,1024]{2,1,0:T(8,128)(2,1)} %bitcast.6), calls=%async_computation.3 | async-start | bytes 1048576 | tf_op jit(solution)/shard_map/all_to_all | solution.py:38
  99.7 2.0 %collective-permute-start.3 = (bf16[256,1024]{1,0:T(8,128)(2,1)}, bf16[256,1024]{1,0:T(8,128)(2,1)}, u32[]{:S(2)}, u32[]{:S(2)}) collective-permute-start(bf16[256,1024]{1,0:T(8,128)(2,1)} %bitcast.2), channel_id=1, source_target_pairs={{0,1},{1,0},{2,3},{3,2},{4,5},{5,4},{6,7},{7,6},{8,9},{9,8},{10,11... | collective-permute-start | bytes 1572872 | tf_op jit(solution)/shard_map/ppermute | solution.py:55
  101.7 2.4 %collective-permute-start.2 = (f32[1280]{0:T(1024)S(1)}, f32[1280]{0:T(1024)S(1)}, u32[]{:S(2)}, u32[]{:S(2)}) collective-permute-start(f32[1280]{0:T(1024)S(1)} %pad_maximum_fusion), channel_id=1, source_target_pairs={{0,1},{1,0},{2,3},{3,2},{4,5},{5,4},{6,7},{7,6},{8,9},{9,8},{10,11... | collective-permute-start | bytes 15368 | tf_op jit(solution)/shard_map/ppermute | solution.py:111
  104.0 2.1 %fusion.5 = f32[1024,768]{1,0:T(8,128)S(1)} fusion(bf16[256,1024]{1,0:T(8,128)(2,1)} %bitcast.2, f32[256,768]{1,0:T(8,128)} %copy-done, f32[256]{0:T(256)S(1)} %get-tuple-element.27, f32[256]{0:T(256)S(1)} %get-tuple-element.24, s32[256]{0:T(256)S(1)} %sub.159), kind=kOutput, calls=%fused_computation.24 | convolution fusion | flops 403832832 | bytes 4459520 | tf_op jit(solution)/shard_map/dot_general | solution.py:120
  106.2 2.0 %collective-permute-start.4 = (bf16[256,768]{1,0:T(8,128)(2,1)}, bf16[256,768]{1,0:T(8,128)(2,1)}, u32[]{:S(2)}, u32[]{:S(2)}) collective-permute-start(bf16[256,768]{1,0:T(8,128)(2,1)} %get-tuple-element.29), channel_id=1, source_target_pairs={{0,1},{1,0},{2,3},{3,2},{4,5},{5,4},{6,7},{7,6},{8,9},{9,8},{10,11... | collective-permute-start | bytes 1179656 | tf_op jit(solution)/shard_map/ppermute | solution.py:94
  108.1 0.6 reduce_sum.192
  108.7 0.1 dynamic_slice.8
  108.8 0.0 collective-permute-done.2
  108.8 0.6 broadcast_in_dim.23
  109.4 0.6 fusion.27
  111.3 0.0 collective-permute-done.3
  111.3 0.0 collective-permute-done.4
  111.3 3.0 %fusion = bf16[1,1024,768]{2,1,0:T(8,128)(2,1)} fusion(f32[1024,768]{1,0:T(8,128)S(1)} %fusion.5, bf16[256,1024]{1,0:T(8,128)(2,1)} %collective-permute-done.3, bf16[256,768]{1,0:T(8,128)(2,1)} %collective-permute-done.4, f32[256]{0:T(256)S(1)} %get-tuple-element.31), kind=kOutput, calls=%fused_computation.2 | convolution fusion | flops 404815872 | bytes 5637120 | tf_op jit(solution)/shard_map/dot_general | solution.py:123
  114.3 0.1 reduce_sum.201
  114.4 0.6 fusion.23
  115.0 1.0 all-to-all-done.3
  116.0 1.1 convert_reduce_fusion.1
  117.1 0.2 fusion.18
  117.3 0.7 fusion.15
  (17 shorter events, 0.2 us)
Async XLA Ops:
  0.6 2.2 %copy-start.3 = (f32[1,1024]{1,0:T(1,128)S(1)}, f32[1,1024]{1,0:T(1,128)}, u32[]{:S(2)}) copy-start(f32[1,1024]{1,0:T(1,128)} %param.9) | copy-start | bytes 12292
  0.6 2.2 %copy-start.2 = (f32[1,1024]{1,0:T(1,128)S(1)}, f32[1,1024]{1,0:T(1,128)}, u32[]{:S(2)}) copy-start(f32[1,1024]{1,0:T(1,128)} %param.8) | copy-start | bytes 12292
  0.7 12.2 %copy-start.1 = (bf16[1,1024,768]{2,1,0:T(8,128)(2,1)S(1)}, bf16[1,1024,768]{2,1,0:T(8,128)(2,1)}, u32[]{:S(2)}) copy-start(bf16[1,1024,768]{2,1,0:T(8,128)(2,1)} %param.10) | copy-start | bytes 4718596
  0.7 16.1 %copy-start.4 = (f32[1,768]{1,0:T(1,128)S(1)}, f32[1,768]{1,0:T(1,128)}, u32[]{:S(2)}) copy-start(f32[1,768]{1,0:T(1,128)} %param.11) | copy-start | bytes 9220
  0.7 18.1 %copy-start.5 = (s32[512]{0:T(512)S(1)}, s32[512]{0:T(512)}, u32[]{:S(2)}) copy-start(s32[512]{0:T(512)} %param.7) | copy-start | bytes 6148
  3.8 24.8 %all-to-all-start = ((bf16[16,16,1024]{2,1,0:T(8,128)(2,1)}), bf16[16,16,1024]{2,1,0:T(8,128)(2,1)}, u32[]{:S(2)}, u32[]{:S(2)}) async-start(bf16[16,16,1024]{2,1,0:T(8,128)(2,1)} %broadcast_in_dim.17), calls=%async_computation | async-start | bytes 1048576 | tf_op jit(solution)/shard_map/all_to_all | solution.py:38
  12.8 17.4 %collective-permute-start = (bf16[1024,768]{1,0:T(8,128)(2,1)S(1)}, bf16[1024,768]{1,0:T(8,128)(2,1)}, u32[]{:S(2)}, u32[]{:S(2)}) collective-permute-start(bf16[1024,768]{1,0:T(8,128)(2,1)S(1)} %bitcast.55), channel_id=1, source_target_pairs={{0,1},{1,0},{2,3},{3,2},{4,5},{5,4},{6,7},{7,6},{8,9},{9,8},{10,11... | collective-permute-start | bytes 4718600 | tf_op jit(solution)/shard_map/ppermute | solution.py:47
  16.8 13.4 %collective-permute-start.1 = (f32[768]{0:T(1024)S(1)}, f32[768]{0:T(1024)S(1)}, u32[]{:S(2)}, u32[]{:S(2)}) collective-permute-start(f32[768]{0:T(1024)S(1)} %reduce.4), channel_id=1, source_target_pairs={{0,1},{1,0},{2,3},{3,2},{4,5},{5,4},{6,7},{7,6},{8,9},{9,8},{10,11... | collective-permute-start | bytes 9224 | tf_op jit(solution)/shard_map/ppermute | solution.py:48
  30.2 42.8 %copy-start = (f32[256,768]{1,0:T(8,128)}, f32[256,768]{1,0:T(8,128)S(1)}, u32[]{:S(2)}) copy-start(f32[256,768]{1,0:T(8,128)S(1)} %get-tuple-element.34) | copy-start | bytes 2359300
  44.1 28.8 %all-to-all-start.2 = ((f32[16,1,256]{2,1,0:T(1,128)}), f32[16,1,256]{2,1,0:T(1,128)S(1)}, u32[]{:S(2)}, u32[]{:S(2)}) async-start(f32[16,1,256]{2,1,0:T(1,128)} %broadcast_in_dim.20), calls=%async_computation.2 | async-start | bytes 32768 | tf_op jit(solution)/shard_map/all_to_all | solution.py:81
  95.4 20.6 %all-to-all-start.3 = ((bf16[16,16,1024]{2,1,0:T(8,128)(2,1)}), bf16[16,16,1024]{2,1,0:T(8,128)(2,1)}, u32[]{:S(2)}, u32[]{:S(2)}) async-start(bf16[16,16,1024]{2,1,0:T(8,128)(2,1)} %bitcast.6), calls=%async_computation.3 | async-start | bytes 1048576 | tf_op jit(solution)/shard_map/all_to_all | solution.py:38
  99.7 11.6 %collective-permute-start.3 = (bf16[256,1024]{1,0:T(8,128)(2,1)}, bf16[256,1024]{1,0:T(8,128)(2,1)}, u32[]{:S(2)}, u32[]{:S(2)}) collective-permute-start(bf16[256,1024]{1,0:T(8,128)(2,1)} %bitcast.2), channel_id=1, source_target_pairs={{0,1},{1,0},{2,3},{3,2},{4,5},{5,4},{6,7},{7,6},{8,9},{9,8},{10,11... | collective-permute-start | bytes 1572872 | tf_op jit(solution)/shard_map/ppermute | solution.py:55
  101.7 7.1 %collective-permute-start.2 = (f32[1280]{0:T(1024)S(1)}, f32[1280]{0:T(1024)S(1)}, u32[]{:S(2)}, u32[]{:S(2)}) collective-permute-start(f32[1280]{0:T(1024)S(1)} %pad_maximum_fusion), channel_id=1, source_target_pairs={{0,1},{1,0},{2,3},{3,2},{4,5},{5,4},{6,7},{7,6},{8,9},{9,8},{10,11... | collective-permute-start | bytes 15368 | tf_op jit(solution)/shard_map/ppermute | solution.py:111
  106.2 5.2 %collective-permute-start.4 = (bf16[256,768]{1,0:T(8,128)(2,1)}, bf16[256,768]{1,0:T(8,128)(2,1)}, u32[]{:S(2)}, u32[]{:S(2)}) collective-permute-start(bf16[256,768]{1,0:T(8,128)(2,1)} %get-tuple-element.29), channel_id=1, source_target_pairs={{0,1},{1,0},{2,3},{3,2},{4,5},{5,4},{6,7},{7,6},{8,9},{9,8},{10,11... | collective-permute-start | bytes 1179656 | tf_op jit(solution)/shard_map/ppermute | solution.py:94

commit v2 on v1

--- a/solution.py
+++ b/solution.py
@@ -57,20 +57,17 @@
     plane_labels = lax.dynamic_index_in_dim(
         labels.reshape(chips, 2, images_here), core, axis=1, keepdims=False
     ).reshape(plane_images)
-    class_ids = jnp.arange(classes_here, dtype=jnp.int32)[None, :]
-    onehot_mine = (plane_labels - position * classes_here)[:, None] == class_ids
-    onehot_other = (plane_labels - (position ^ 1) * classes_here)[:, None] == class_ids
-    logits_mine = jnp.dot(act_plane, weight, preferred_element_type=jnp.float32) + head_bias[0]
-    logits_other = (
-        jnp.dot(act_plane, weight_other, preferred_element_type=jnp.float32) + bias_other
+    class_ids = jnp.arange(classes_here, dtype=jnp.int32)
+    both_ids = jnp.concatenate(
+        [position * classes_here + class_ids, (position ^ 1) * classes_here + class_ids]
     )
-    top = jnp.maximum(jnp.max(logits_mine, axis=1), jnp.max(logits_other, axis=1))
-    total = jnp.sum(jnp.exp(logits_mine - top[:, None]), axis=1) + jnp.sum(
-        jnp.exp(logits_other - top[:, None]), axis=1
-    )
-    label_part = jnp.sum(jnp.where(onehot_mine, logits_mine, 0.0), axis=1) + jnp.sum(
-        jnp.where(onehot_other, logits_other, 0.0), axis=1
-    )
+    weight_both = jnp.concatenate([weight, weight_other], axis=1)
+    bias_both = jnp.concatenate([head_bias[0], bias_other])
+    onehot = plane_labels[:, None] == both_ids[None, :]
+    logits = jnp.dot(act_plane, weight_both, preferred_element_type=jnp.float32) + bias_both
+    top = jnp.max(logits, axis=1)
+    total = jnp.sum(jnp.exp(logits - top[:, None]), axis=1)
+    label_part = jnp.sum(jnp.where(onehot, logits, 0.0), axis=1)
     stats = jnp.stack([top + jnp.log(total), label_part])
     stats_all = over_plane(jnp.broadcast_to(stats[None], (chips,) + stats.shape))
     logs = stats_all[:, 0]
@@ -82,43 +79,55 @@
         jnp.broadcast_to(label_logp[None], (members, plane_images)), "member", 0, 0
     )
 
-    diff_mine = jnp.exp(logits_mine - log_total[:, None]) - onehot_mine.astype(jnp.float32)
-    diff_other = jnp.exp(logits_other - log_total[:, None]) - onehot_other.astype(jnp.float32)
-    low_mine = diff_mine.astype(jnp.bfloat16)
-    low_other = diff_other.astype(jnp.bfloat16)
-    contract = (((1,), (1,)), ((), ()))
+    diff = jnp.exp(logits - log_total[:, None]) - onehot.astype(jnp.float32)
+    low = diff.astype(jnp.bfloat16)
     partial = lax.dot_general(
-        low_mine, weight, contract, preferred_element_type=jnp.float32
-    ) + lax.dot_general(low_other, weight_other, contract, preferred_element_type=jnp.float32)
-    pieces = over_plane(partial.astype(jnp.bfloat16).reshape(chips, images_here, -1))
-    low_received = lax.ppermute(low_other, "dp", swap)
+        low, weight_both, (((1,), (1,)), ((), ())), preferred_element_type=jnp.float32
+    )
+    low_received = lax.ppermute(low[:, classes_here:], "dp", swap)
 
     joint_top = jnp.max(logp_all, axis=0)
     log_joint = joint_top + jnp.log(jnp.sum(jnp.exp(logp_all - joint_top), axis=0))
     scale = loss_scale * jnp.exp(label_logp - log_joint)
 
     shift_sum = jnp.sum(scale[:, None] * partial, axis=0)
-    act_sum = jnp.sum(scale[:, None] * partial * act_plane.astype(jnp.float32), axis=0)
+    act_sum = jnp.sum(scale[:, None] * (partial * act_plane.astype(jnp.float32)), axis=0)
     sums = jnp.stack([shift_sum, act_sum])
-    sums = jnp.sum(
-        lax.all_to_all(jnp.broadcast_to(sums[None], (dp,) + sums.shape), "dp", 0, 0), axis=0
+    sums_high = sums.astype(jnp.bfloat16)
+    sums_low = (sums - sums_high.astype(jnp.float32)).astype(jnp.bfloat16)
+    tail = jnp.concatenate([sums_high, sums_low]).reshape(images_here, -1)
+    chunks = jnp.concatenate(
+        [
+            partial.astype(jnp.bfloat16).reshape(chips, images_here, -1),
+            jnp.broadcast_to(tail[None], (chips,) + tail.shape),
+        ],
+        axis=2,
     )
+    pieces = over_plane(chunks)
+    channels = act.shape[1]
+    received = jnp.sum(pieces.astype(jnp.float32), axis=0)
+    sums = received[:, channels:].reshape(2, 2, channels)
+    sums = sums[0] + sums[1]
+    sums = sums + lax.ppermute(sums, "dp", swap)
     grad_shift = sums[0]
     grad_gain = (sums[1] - shift_row * grad_shift) / gain_row
 
-    grad_other = jnp.sum(scale[:, None] * diff_other, axis=0)
-    note = jnp.concatenate([scale, log_joint, grad_other])
+    grad_logits = scale[:, None] * diff
+    grad_sum = jnp.sum(grad_logits, axis=0)
+    note = jnp.concatenate([scale, log_joint, grad_sum[classes_here:]])
     note = lax.ppermute(note, "dp", swap)
     scale_other = note[:plane_images]
     mean_loss = math.log(members) - (
         jnp.sum(log_joint) + jnp.sum(note[plane_images : 2 * plane_images])
     ) / (2 * plane_images)
-    grad_mine = scale[:, None] * diff_mine
-    grad_head_bias = jnp.sum(grad_mine, axis=0) + note[2 * plane_images :]
+    grad_head_bias = grad_sum[:classes_here] + note[2 * plane_images :]
     rows = (((0,), (0,)), ((), ()))
     grad_head_weight = (
         lax.dot_general(
-            act_plane, grad_mine.astype(jnp.bfloat16), rows, preferred_element_type=jnp.float32
+            act_plane,
+            grad_logits[:, :classes_here].astype(jnp.bfloat16),
+            rows,
+            preferred_element_type=jnp.float32,
         )
         + lax.dot_general(
             act_other,
@@ -129,7 +138,7 @@
     ).astype(jnp.bfloat16)
 
     scale_own = lax.dynamic_slice_in_dim(scale, (position // 2) * images_here, images_here)
-    upstream = scale_own[:, None] * jnp.sum(pieces.astype(jnp.float32), axis=0)
+    upstream = scale_own[:, None] * received[:, :channels]
     grad_pooled = norm_backward(upstream, normed, inverse, gain_row)
     return (
         mean_loss,

time: 120 us -> 107 us (0.89)
  waiting for transfers between devices: 22 us -> 9.59 us
  blocking collectives: 27.9 us -> 38.6 us
  starting transfers between devices: 40.7 us -> 32.5 us
  matrix products: 14.5 us -> 10.4 us
    all_to_all x1 -> x0, starting transfers between devices: 15.2 us -> none  [per_device(): lax.all_to_all(jnp.broadcast_to(label_logp[None], (members, plane_images)...]
    all_to_all x1 -> x0, waiting for transfers between devices: 11.6 us -> none  [per_device(): lax.all_to_all(jnp.broadcast_to(label_logp[None], (members, plane_images)...]
    all_to_all x1, blocking collectives: 17.9 us -> 28.6 us  [per_device(): lax.all_to_all(jnp.broadcast_to(label_logp[None], (members, plane_images)...]
    dot_general x5 -> x3, matrix products: 11.5 us -> 7.39 us  [the longest x1 2.9 us: per_device(): lax.dot_general(low, weight_both, (((1,), (1,)), ((), ())), preferred_ele...]
    ppermute x1, starting transfers between devices: 1.97 us -> 5.82 us  [per_device(): act_other = lax.ppermute(act_plane, 'dp', swap)]
    ppermute x1 -> x2, starting transfers between devices: 1.97 us -> 5.53 us  [the longest x1 3.13 us: per_device(): sums = sums + lax.ppermute(sums, 'dp', swap)]
    all_to_all x2, waiting for transfers between devices: 10.4 us -> 8.58 us  [over_plane(): return lax.all_to_all(x, 'dp', 0, 0, axis_index_groups=planes)]
    reduce_sum x4 -> x3, other arithmetic: 3.11 us -> 3.18 us  [the longest x1 1.48 us: per_device(): grad_sum = jnp.sum(grad_logits, axis=0)]
  transfers between devices with their start and end apart: 8 -> 8, of which waited for: 3 -> 3; matrix products, arithmetic and copies ran while one was open for 10% -> 8% of each run, Pallas kernels for 0% -> 0%
where the time goes in v2:
time: 107 us; the launch traced here: 106 us
  blocking collectives  38.6 us (36%)
  starting transfers between devices  32.5 us (30%)
  matrix products  10.4 us (10%)
  waiting for transfers between devices  9.59 us (9%)
  other arithmetic  9.29 us (9%)
  between operations  3.45 us (3%)
  local copies, waits for them, and re-layouts  2.57 us (2%)
    all_to_all x1, blocking collectives, per_device(): lax.all_to_all(jnp.broadcast_to(label_logp[None], (members, plane_images)...  28.6 us
    all_to_all x2, starting transfers between devices, over_plane(): return lax.all_to_all(x, 'dp', 0, 0, axis_index_groups=planes)  13.3 us
    all_to_all x1, blocking collectives, over_plane(): return lax.all_to_all(x, 'dp', 0, 0, axis_index_groups=planes)  9.93 us
    all_to_all x2, waiting for transfers between devices, over_plane(): return lax.all_to_all(x, 'dp', 0, 0, axis_index_groups=planes)  8.58 us
    ppermute x1, starting transfers between devices, per_device(): act_other = lax.ppermute(act_plane, 'dp', swap)  5.82 us
    ppermute x1, starting transfers between devices, per_device(): weight_other = lax.ppermute(weight, 'dp', swap)  3.96 us
    ppermute x1, starting transfers between devices, per_device(): sums = sums + lax.ppermute(sums, 'dp', swap)  3.13 us
    dot_general x1, matrix products, per_device(): lax.dot_general(act_other, (scale_other[:, None] * low_received.astype(jn...  3 us
  transfers between devices with their start and end apart: 8, of which 3 were waited for; matrix products, arithmetic and copies ran while one was open for 8% of the time, Pallas kernels for 0%

profile of v2, /device:TPU:1, one launch (start us, length us, event | category | flops | bytes accessed | tf_op | source)
XLA Modules:
  0.0 106.3 jit_solution(7394550999161315291)
XLA Ops:
  0.6 0.0 copy-start.3
  0.6 0.0 copy-start.2
  0.7 0.0 copy-start.6
  0.7 0.0 copy-start.4
  0.7 0.0 copy-start.5
  0.7 1.8 %convert_reduce_fusion = f32[16,1024]{1,0:T(8,128)S(1)} fusion(bf16[1,16,49,1024]{3,1,2,0:T(8,128)(2,1)} %param.6), kind=kLoop, calls=%fused_computation | loop fusion | flops 1589248 | bytes 1671168 | tf_op jit(solution)/shard_map/reduce_sum | solution.py:50
  2.5 0.1 multiply_reduce_fusion.4
  2.6 0.2 multiply_reduce_fusion.3
  2.8 0.0 copy-done.3
  2.8 0.0 copy-done.2
  2.8 0.1 add_convert_fusion.1
  2.9 0.9 broadcast_in_dim.20
  3.8 9.1 %all-to-all-start = ((bf16[16,16,1024]{2,1,0:T(8,128)(2,1)}), bf16[16,16,1024]{2,1,0:T(8,128)(2,1)}, u32[]{:S(2)}, u32[]{:S(2)}) async-start(bf16[16,16,1024]{2,1,0:T(8,128)(2,1)} %broadcast_in_dim.20), calls=%async_computation | async-start | bytes 1048576 | tf_op jit(solution)/shard_map/all_to_all | solution.py:38
  12.8 0.0 copy-done.6
  12.8 4.0 %collective-permute-start = (bf16[1024,768]{1,0:T(8,128)(2,1)S(1)}, bf16[1024,768]{1,0:T(8,128)(2,1)}, u32[]{:S(2)}, u32[]{:S(2)}) collective-permute-start(bf16[1024,768]{1,0:T(8,128)(2,1)S(1)} %bitcast.41), channel_id=1, source_target_pairs={{0,1},{1,0},{2,3},{3,2},{4,5},{5,4},{6,7},{7,6},{8,9},{9,8},{10,11... | collective-permute-start | bytes 4718600 | tf_op jit(solution)/shard_map/ppermute | solution.py:47
  16.8 0.0 copy-done.4
  16.8 1.9 %collective-permute-start.1 = (f32[768]{0:T(1024)S(1)}, f32[768]{0:T(1024)S(1)}, u32[]{:S(2)}, u32[]{:S(2)}) collective-permute-start(f32[768]{0:T(1024)S(1)} %reduce.4), channel_id=1, source_target_pairs={{0,1},{1,0},{2,3},{3,2},{4,5},{5,4},{6,7},{7,6},{8,9},{9,8},{10,11... | collective-permute-start | bytes 9224 | tf_op jit(solution)/shard_map/ppermute | solution.py:48
  18.8 0.0 copy-done.5
  18.8 0.1 reshape.177
  19.0 0.1 eq.15
  19.0 0.9 collective-permute-done.1
  19.9 0.0 collective-permute-done
  20.0 8.6 %all-to-all-done = bf16[16,16,1024]{2,1,0:T(8,128)(2,1)} async-done(((bf16[16,16,1024]{2,1,0:T(8,128)(2,1)}), bf16[16,16,1024]{2,1,0:T(8,128)(2,1)}, u32[]{:S(2)}, u32[]{:S(2)}) %all-to-all-start) | async-done | bytes 524320 | tf_op jit(solution)/shard_map/all_to_all | solution.py:38
  28.5 2.6 %fusion.22 = (f32[256]{0:T(256)S(1)}, f32[256,1536]{1,0:T(8,128)S(1)}) fusion(f32[1536]{0:T(1024)S(1)} %pad_maximum_fusion.4, bf16[256,1024]{1,0:T(8,128)(2,1)} %bitcast.2, bf16[1024,768]{1,0:T(8,128)(2,1)} %collective-permute-done, bf16[1024,768]{1,0:T(8,128)(2,1)S(1)} %bitcast.42), kind=kOutput, calls=%fused_computation.67 | convolution fusion | flops 812384000 | bytes 5250048 | tf_op jit(solution)/shard_map/dot_general | solution.py:67
  31.2 0.5 exponential_reduce_fusion
  31.7 9.9 %all_to_all.24 = f32[16,2,256]{2,1,0:T(2,128)S(1)} all-to-all(f32[16,2,256]{2,1,0:T(2,128)S(1)} %broadcast_in_dim.22), channel_id=1, replica_groups={{0,2,4,6,8,10,12,14,16,18,20,22,24,26,28,30},{1,3,5,7,9,11,13,15,17,19,..., dimensions={0} | all-to-all | bytes 65536 | tf_op jit(solution)/shard_map/all_to_all | solution.py:38
  41.7 0.1 slice_reduce_fusion.2
  41.8 28.6 %all_to_all.25 = f32[16,1,256]{2,1,0:T(1,128)S(1)} all-to-all(f32[16,1,256]{2,1,0:T(1,128)S(1)} %broadcast_in_dim.23), channel_id=1, replica_groups=mesh['member'=16,'dp'=32] {'member'}, dimensions={0} | all-to-all | bytes 32768 | tf_op jit(solution)/shard_map/all_to_all | solution.py:78
  70.5 1.5 %fusion.18 = (f32[1536]{0:T(1024)S(1)}, bf16[256,1536]{1,0:T(8,128)(2,1)}, bf16[256,1536]{1,0:T(8,128)(2,1)S(1)}) fusion(s32[1536]{0:T(1024)S(1)} %pad_add_fusion, s32[256]{0:T(256)S(1)} %eq.15, f32[256,1536]{1,0:T(8,128)S(1)} %get-tuple-element.28, f32[256]{0:T(256)S(1)} %get-tuple-element.21, f32[256]{0:T(256)S(1)} %get-tuple-element.18), kind=kLoop, calls=%fused_computation.64 | loop fusion | flops 3144192 | bytes 3161088 | tf_op jit(solution)/shard_map/reduce_sum | solution.py:116
  72.0 0.0 copy-start
  72.0 2.9 %multiply_reduce_fusion.1 = (f32[1024]{0:T(1024)S(1)}, f32[1024]{0:T(1024)S(1)}, bf16[256,1024]{1,0:T(8,128)(2,1)S(1)}) fusion(f32[256]{0:T(256)S(1)} %get-tuple-element.18, bf16[16,16,1024]{2,1,0:T(8,128)(2,1)} %all-to-all-done, bf16[256,1536]{1,0:T(8,128)(2,1)S(1)} %get-tuple-element.22, bf16[1024,768]{1,0:T(8,128)(2,1)} %collective-permute-done, ...), kind=kOutput, calls=%fused_computation.15 | convolution fusion | flops 813430784 | bytes 4989952 | tf_op jit(solution)/shard_map/dot_general | solution.py:84
  74.9 0.0 copy-done
  75.0 0.9 pad_maximum_fusion.3
  75.9 4.3 %all-to-all-start.3 = ((bf16[16,16,1280]{2,1,0:T(8,128)(2,1)}), bf16[16,16,1280]{2,1,0:T(8,128)(2,1)}, u32[]{:S(2)}, u32[]{:S(2)}) async-start(bf16[16,16,1280]{2,1,0:T(8,128)(2,1)} %pad_maximum_fusion.3), calls=%async_computation.3 | async-start | bytes 1310720 | tf_op jit(solution)/shard_map/all_to_all | solution.py:38
  80.2 5.8 %collective-permute-start.4 = (bf16[256,1024]{1,0:T(8,128)(2,1)}, bf16[256,1024]{1,0:T(8,128)(2,1)}, u32[]{:S(2)}, u32[]{:S(2)}) collective-permute-start(bf16[256,1024]{1,0:T(8,128)(2,1)} %bitcast.2), channel_id=1, source_target_pairs={{0,1},{1,0},{2,3},{3,2},{4,5},{5,4},{6,7},{7,6},{8,9},{9,8},{10,11... | collective-permute-start | bytes 1572872 | tf_op jit(solution)/shard_map/ppermute | solution.py:55
  86.0 1.9 %collective-permute-start.2 = (f32[1280]{0:T(1024)S(1)}, f32[1280]{0:T(1024)S(1)}, u32[]{:S(2)}, u32[]{:S(2)}) collective-permute-start(f32[1280]{0:T(1024)S(1)} %pad_maximum_fusion.5), channel_id=1, source_target_pairs={{0,1},{1,0},{2,3},{3,2},{4,5},{5,4},{6,7},{7,6},{8,9},{9,8},{10,11... | collective-permute-start | bytes 15368 | tf_op jit(solution)/shard_map/ppermute | solution.py:118
  88.0 0.0 copy-start.1
  88.0 1.8 %fusion.6 = f32[1024,768]{1,0:T(8,128)S(1)} fusion(bf16[256,1024]{1,0:T(8,128)(2,1)} %bitcast.2, bf16[256,1536]{1,0:T(8,128)(2,1)} %get-tuple-element.17), kind=kOutput, calls=%fused_computation.19 | convolution fusion | flops 402653184 | bytes 4063232 | tf_op jit(solution)/shard_map/dot_general | solution.py:126
  89.8 0.0 copy-done.1
  89.8 0.8 slice.73
  90.6 0.6 reduce_sum.152
  91.2 0.1 dynamic_slice.8
  91.3 2.4 %collective-permute-start.5 = (bf16[256,768]{1,0:T(8,128)(2,1)}, bf16[256,768]{1,0:T(8,128)(2,1)}, u32[]{:S(2)}, u32[]{:S(2)}) collective-permute-start(bf16[256,768]{1,0:T(8,128)(2,1)} %slice.73), channel_id=1, source_target_pairs={{0,1},{1,0},{2,3},{3,2},{4,5},{5,4},{6,7},{7,6},{8,9},{9,8},{10,11... | collective-permute-start | bytes 1179656 | tf_op jit(solution)/shard_map/ppermute | solution.py:87
  93.7 0.0 collective-permute-done.2
  93.7 0.6 broadcast_in_dim.28
  94.3 0.6 fusion.21
  96.2 0.0 collective-permute-done.4
  96.2 0.0 collective-permute-done.5
  96.2 3.0 %fusion.3 = bf16[1,1024,768]{2,1,0:T(8,128)(2,1)} fusion(f32[1024,768]{1,0:T(8,128)S(1)} %fusion.6, bf16[256,1024]{1,0:T(8,128)(2,1)} %collective-permute-done.4, bf16[256,768]{1,0:T(8,128)(2,1)} %collective-permute-done.5, f32[256]{0:T(256)S(1)} %get-tuple-element.25), kind=kOutput, calls=%fused_computation.10 | convolution fusion | flops 404815872 | bytes 5637120 | tf_op jit(solution)/shard_map/dot_general | solution.py:132
  99.2 0.0 all-to-all-done.3
  99.2 1.2 %convert_reduce_fusion.1 = f32[16,1280]{1,0:T(8,128)S(1)} fusion(bf16[16,16,1280]{2,1,0:T(8,128)(2,1)} %all-to-all-done.3), kind=kLoop, calls=%fused_computation.11 | loop fusion | flops 634880 | bytes 737280 | tf_op jit(solution)/shard_map/reduce_sum | solution.py:108
  100.4 0.2 fusion.9
  100.6 3.1 %collective-permute-start.3 = (f32[2,1024]{1,0:T(2,128)S(1)}, f32[2,1024]{1,0:T(2,128)S(1)}, u32[]{:S(2)}, u32[]{:S(2)}) collective-permute-start(f32[2,1024]{1,0:T(2,128)S(1)} %add.117), channel_id=1, source_target_pairs={{0,1},{1,0},{2,3},{3,2},{4,5},{5,4},{6,7},{7,6},{8,9},{9,8},{10,11... | collective-permute-start | bytes 24584 | tf_op jit(solution)/shard_map/ppermute | solution.py:111
  103.8 0.7 multiply_bitcast_fusion
  104.5 0.1 collective-permute-done.3
  104.6 0.6 fusion.14
  (29 shorter events, 0.3 us)
Async XLA Ops:
  0.6 2.2 %copy-start.3 = (f32[1,1024]{1,0:T(1,128)S(1)}, f32[1,1024]{1,0:T(1,128)}, u32[]{:S(2)}) copy-start(f32[1,1024]{1,0:T(1,128)} %param.9) | copy-start | bytes 12292
  0.6 2.2 %copy-start.2 = (f32[1,1024]{1,0:T(1,128)S(1)}, f32[1,1024]{1,0:T(1,128)}, u32[]{:S(2)}) copy-start(f32[1,1024]{1,0:T(1,128)} %param.8) | copy-start | bytes 12292
  0.7 12.2 %copy-start.6 = (bf16[1,1024,768]{2,1,0:T(8,128)(2,1)S(1)}, bf16[1,1024,768]{2,1,0:T(8,128)(2,1)}, u32[]{:S(2)}) copy-start(bf16[1,1024,768]{2,1,0:T(8,128)(2,1)} %param.10) | copy-start | bytes 4718596
  0.7 16.1 %copy-start.4 = (f32[1,768]{1,0:T(1,128)S(1)}, f32[1,768]{1,0:T(1,128)}, u32[]{:S(2)}) copy-start(f32[1,768]{1,0:T(1,128)} %param.11) | copy-start | bytes 9220
  0.7 18.1 %copy-start.5 = (s32[512]{0:T(512)S(1)}, s32[512]{0:T(512)}, u32[]{:S(2)}) copy-start(s32[512]{0:T(512)} %param.7) | copy-start | bytes 6148
  3.8 24.8 %all-to-all-start = ((bf16[16,16,1024]{2,1,0:T(8,128)(2,1)}), bf16[16,16,1024]{2,1,0:T(8,128)(2,1)}, u32[]{:S(2)}, u32[]{:S(2)}) async-start(bf16[16,16,1024]{2,1,0:T(8,128)(2,1)} %broadcast_in_dim.20), calls=%async_computation | async-start | bytes 1048576 | tf_op jit(solution)/shard_map/all_to_all | solution.py:38
  12.8 7.1 %collective-permute-start = (bf16[1024,768]{1,0:T(8,128)(2,1)S(1)}, bf16[1024,768]{1,0:T(8,128)(2,1)}, u32[]{:S(2)}, u32[]{:S(2)}) collective-permute-start(bf16[1024,768]{1,0:T(8,128)(2,1)S(1)} %bitcast.41), channel_id=1, source_target_pairs={{0,1},{1,0},{2,3},{3,2},{4,5},{5,4},{6,7},{7,6},{8,9},{9,8},{10,11... | collective-permute-start | bytes 4718600 | tf_op jit(solution)/shard_map/ppermute | solution.py:47
  16.8 3.1 %collective-permute-start.1 = (f32[768]{0:T(1024)S(1)}, f32[768]{0:T(1024)S(1)}, u32[]{:S(2)}, u32[]{:S(2)}) collective-permute-start(f32[768]{0:T(1024)S(1)} %reduce.4), channel_id=1, source_target_pairs={{0,1},{1,0},{2,3},{3,2},{4,5},{5,4},{6,7},{7,6},{8,9},{9,8},{10,11... | collective-permute-start | bytes 9224 | tf_op jit(solution)/shard_map/ppermute | solution.py:48
  72.0 2.9 %copy-start = (bf16[256,1536]{1,0:T(8,128)(2,1)}, bf16[256,1536]{1,0:T(8,128)(2,1)S(1)}, u32[]{:S(2)}) copy-start(bf16[256,1536]{1,0:T(8,128)(2,1)S(1)} %get-tuple-element.22) | copy-start | bytes 2359300
  75.9 23.3 %all-to-all-start.3 = ((bf16[16,16,1280]{2,1,0:T(8,128)(2,1)}), bf16[16,16,1280]{2,1,0:T(8,128)(2,1)}, u32[]{:S(2)}, u32[]{:S(2)}) async-start(bf16[16,16,1280]{2,1,0:T(8,128)(2,1)} %pad_maximum_fusion.3), calls=%async_computation.3 | async-start | bytes 1310720 | tf_op jit(solution)/shard_map/all_to_all | solution.py:38
  80.2 16.0 %collective-permute-start.4 = (bf16[256,1024]{1,0:T(8,128)(2,1)}, bf16[256,1024]{1,0:T(8,128)(2,1)}, u32[]{:S(2)}, u32[]{:S(2)}) collective-permute-start(bf16[256,1024]{1,0:T(8,128)(2,1)} %bitcast.2), channel_id=1, source_target_pairs={{0,1},{1,0},{2,3},{3,2},{4,5},{5,4},{6,7},{7,6},{8,9},{9,8},{10,11... | collective-permute-start | bytes 1572872 | tf_op jit(solution)/shard_map/ppermute | solution.py:55
  86.0 7.7 %collective-permute-start.2 = (f32[1280]{0:T(1024)S(1)}, f32[1280]{0:T(1024)S(1)}, u32[]{:S(2)}, u32[]{:S(2)}) collective-permute-start(f32[1280]{0:T(1024)S(1)} %pad_maximum_fusion.5), channel_id=1, source_target_pairs={{0,1},{1,0},{2,3},{3,2},{4,5},{5,4},{6,7},{7,6},{8,9},{9,8},{10,11... | collective-permute-start | bytes 15368 | tf_op jit(solution)/shard_map/ppermute | solution.py:118
  88.0 1.9 %copy-start.1 = (bf16[256,1536]{1,0:T(8,128)(2,1)S(1)}, bf16[256,1536]{1,0:T(8,128)(2,1)}, u32[]{:S(2)}) copy-start(bf16[256,1536]{1,0:T(8,128)(2,1)} %copy-done) | copy-start | bytes 2359300
  91.3 4.9 %collective-permute-start.5 = (bf16[256,768]{1,0:T(8,128)(2,1)}, bf16[256,768]{1,0:T(8,128)(2,1)}, u32[]{:S(2)}, u32[]{:S(2)}) collective-permute-start(bf16[256,768]{1,0:T(8,128)(2,1)} %slice.73), channel_id=1, source_target_pairs={{0,1},{1,0},{2,3},{3,2},{4,5},{5,4},{6,7},{7,6},{8,9},{9,8},{10,11... | collective-permute-start | bytes 1179656 | tf_op jit(solution)/shard_map/ppermute | solution.py:87
  100.6 3.9 %collective-permute-start.3 = (f32[2,1024]{1,0:T(2,128)S(1)}, f32[2,1024]{1,0:T(2,128)S(1)}, u32[]{:S(2)}, u32[]{:S(2)}) collective-permute-start(f32[2,1024]{1,0:T(2,128)S(1)} %add.117), channel_id=1, source_target_pairs={{0,1},{1,0},{2,3},{3,2},{4,5},{5,4},{6,7},{7,6},{8,9},{9,8},{10,11... | collective-permute-start | bytes 24584 | tf_op jit(solution)/shard_map/ppermute | solution.py:111

commit v3 on v2

v3 whole, which is shorter than its diff:
```python
import functools
import math

import jax
import jax.numpy as jnp
from jax import lax
from jax.experimental import pallas as pl
from jax.experimental.pallas import tpu as pltpu
from jax.sharding import PartitionSpec as P

norm_eps = 1e-06
loss_scale = 16.0


def norm_kernel(positions, total_ref, gain_ref, shift_ref, normed_ref, inverse_ref, act_ref):
    pooled = total_ref[...] / positions
    center = pooled - jnp.mean(pooled, axis=-1, keepdims=True)
    inverse = lax.rsqrt(jnp.mean(center * center, axis=-1, keepdims=True) + norm_eps)
    normed = center * inverse
    normed_ref[...] = normed
    inverse_ref[...] = jnp.broadcast_to(inverse, inverse_ref.shape)
    act = (normed * gain_ref[...] + shift_ref[...]).astype(jnp.bfloat16)
    act_ref[...] = jnp.broadcast_to(act[None], act_ref.shape)


def norm_copies(total, positions, gain_row, shift_row, copies):
    images, channels = total.shape
    whole = lambda *shape: pl.BlockSpec(shape, lambda i: (0,) * len(shape))
    return pl.pallas_call(
        functools.partial(norm_kernel, positions),
        grid=(1,),
        in_specs=[whole(images, channels), whole(1, channels), whole(1, channels)],
        out_specs=[
            whole(images, channels),
            whole(images, 128),
            whole(copies, images, channels),
        ],
        out_shape=[
            jax.ShapeDtypeStruct((images, channels), jnp.float32),
            jax.ShapeDtypeStruct((images, 128), jnp.float32),
            jax.ShapeDtypeStruct((copies, images, channels), jnp.bfloat16),
        ],
        compiler_params=pltpu.CompilerParams(vmem_limit_bytes=16 * 2**20),
    )(total, gain_row, shift_row)


def join_kernel(logp_ref, own_ref, partial_ref, act_ref, _, scale_ref, joint_ref, tail_ref):
    logp = logp_ref[...]
    top = jnp.max(logp, axis=0, keepdims=True)
    joint = top + jnp.log(jnp.sum(jnp.exp(logp - top), axis=0, keepdims=True))
    joint_ref[...] = joint
    scale = loss_scale * jnp.exp(own_ref[...] - joint)
    images = scale.shape[1]
    column = jnp.transpose(jnp.broadcast_to(scale, (128, images)))
    scale_ref[...] = column
    scaled = partial_ref[...] * column[:, :1]
    sums = [
        jnp.sum(scaled, axis=0, keepdims=True),
        jnp.sum(scaled * act_ref[...].astype(jnp.float32), axis=0, keepdims=True),
    ]
    high = [x.astype(jnp.bfloat16).astype(jnp.float32) for x in sums]
    low = [x - h for x, h in zip(sums, high)]
    width = tail_ref.shape[2]
    lines = [x[:, k : k + width] for x in high + low for k in range(0, x.shape[1], width)]
    tail = jnp.concatenate(lines, axis=0).astype(jnp.bfloat16)
    tail_ref[...] = jnp.broadcast_to(tail[None], tail_ref.shape)


def join_members(logp_all, label_logp, partial, act, chunks):
    images, channels = act.shape
    width = chunks.shape[2] - channels
    whole = lambda *shape: pl.BlockSpec(shape, lambda i: (0,) * len(shape))
    return pl.pallas_call(
        join_kernel,
        grid=(1,),
        in_specs=[
            whole(*logp_all.shape),
            whole(1, images),
            whole(images, channels),
            whole(images, channels),
            pl.BlockSpec(memory_space=pl.ANY),
        ],
        out_specs=[
            whole(images, 128),
            whole(1, images),
            pl.BlockSpec(chunks.shape[:2] + (width,), lambda i: (0, 0, channels // width)),
        ],
        out_shape=[
            jax.ShapeDtypeStruct((images, 128), jnp.float32),
            jax.ShapeDtypeStruct((1, images), jnp.float32),
            jax.ShapeDtypeStruct(chunks.shape, chunks.dtype),
        ],
        input_output_aliases={4: 2},
        compiler_params=pltpu.CompilerParams(vmem_limit_bytes=24 * 2**20),
    )(logp_all, label_logp, partial, act, chunks)


def close_kernel(_, pieces_ref, scale_ref, normed_ref, inverse_ref, gain_ref, grad_ref):
    received = pieces_ref[0].astype(jnp.float32)
    for k in range(1, pieces_ref.shape[0]):
        received = received + pieces_ref[k].astype(jnp.float32)
    normed = normed_ref[...]
    scaled = scale_ref[:, :1] * received * gain_ref[...]
    grad_ref[...] = inverse_ref[:, :1] * (
        scaled
        - jnp.mean(scaled, axis=-1, keepdims=True)
        - normed * jnp.mean(scaled * normed, axis=-1, keepdims=True)
    )


def close_images(chip, pieces, scale, normed, inverse, gain_row):
    images, channels = normed.shape
    whole = lambda *shape: pl.BlockSpec(shape, lambda i, chip: (0,) * len(shape))
    return pl.pallas_call(
        close_kernel,
        grid_spec=pltpu.PrefetchScalarGridSpec(
            num_scalar_prefetch=1,
            grid=(1,),
            in_specs=[
                whole(pieces.shape[0], images, channels),
                pl.BlockSpec((images, 128), lambda i, chip: (chip[0], 0)),
                whole(images, channels),
                whole(images, 128),
                whole(1, channels),
            ],
            out_specs=whole(images, channels),
        ),
        out_shape=jax.ShapeDtypeStruct((images, channels), jnp.float32),
        cost_estimate=pl.CostEstimate(
            flops=40 * images * channels, bytes_accessed=2**20, transcendentals=0
        ),
        compiler_params=pltpu.CompilerParams(vmem_limit_bytes=16 * 2**20),
    )(jnp.reshape(chip, (1,)), pieces, scale, normed, inverse, gain_row)


def sum_tails_kernel(tails_ref, sums_ref):
    tail = tails_ref[0].astype(jnp.float32)
    for k in range(1, tails_ref.shape[0]):
        tail = tail + tails_ref[k].astype(jnp.float32)
    lines, width = tail.shape
    half, quarter = lines // 2, lines // 4
    tail = tail[:half] + tail[half:]
    for r in range(2):
        for k in range(quarter):
            sums_ref[r : r + 1, k * width : (k + 1) * width] = tail[r * quarter + k][None]


def sum_tails(pieces, channels):
    copies, lines, whole_width = pieces.shape
    width = whole_width - channels
    return pl.pallas_call(
        sum_tails_kernel,
        grid=(1,),
        in_specs=[pl.BlockSpec((copies, lines, width), lambda i: (0, 0, channels // width))],
        out_specs=pl.BlockSpec((2, channels), lambda i: (0, 0)),
        out_shape=jax.ShapeDtypeStruct((2, channels), jnp.float32),
        compiler_params=pltpu.CompilerParams(vmem_limit_bytes=16 * 2**20),
    )(pieces)


def per_device(features, labels, norm_gain, norm_bias, head_weight, head_bias):
    dp = lax.axis_size("dp")
    members = lax.axis_size("member")
    chips = dp // 2
    position = lax.axis_index("dp")
    core = lax.rem(position, 2)
    swap = [(i, i ^ 1) for i in range(dp)]
    planes = [[2 * chip + c for chip in range(chips)] for c in range(2)]

    def over_plane(x):
        return lax.all_to_all(x, "dp", 0, 0, axis_index_groups=planes)

    weight = head_weight[0]
    classes_here = weight.shape[1]
    gain_row = norm_gain[0]
    shift_row = norm_bias[0]
    images_here = features.shape[1]
    plane_images = chips * images_here

    weight_other = lax.ppermute(weight, "dp", swap)
    bias_other = lax.ppermute(head_bias[0], "dp", swap)

    normed, inverse, act_copies = norm_copies(
        jnp.sum(features[0], axis=1, dtype=jnp.float32),
        features.shape[2],
        norm_gain,
        norm_bias,
        chips,
    )
    channels = normed.shape[1]
    act_plane = over_plane(act_copies).reshape(plane_images, channels)

    plane_labels = lax.dynamic_index_in_dim(
        labels.reshape(chips, 2, images_here), core, axis=1, keepdims=False
    ).reshape(plane_images)
    class_ids = jnp.arange(classes_here, dtype=jnp.int32)
    both_ids = jnp.concatenate(
        [position * classes_here + class_ids, (position ^ 1) * classes_here + class_ids]
    )
    weight_both = jnp.concatenate([weight, weight_other], axis=1)
    bias_both = jnp.concatenate([head_bias[0], bias_other])
    onehot = plane_labels[:, None] == both_ids[None, :]
    logits = jnp.dot(act_plane, weight_both, preferred_element_type=jnp.float32) + bias_both
    top = jnp.max(logits, axis=1)
    total = jnp.sum(jnp.exp(logits - top[:, None]), axis=1)
    label_part = jnp.sum(jnp.where(onehot, logits, 0.0), axis=1)
    stats = jnp.stack([top + jnp.log(total), label_part])
    stats_all = over_plane(jnp.broadcast_to(stats[None], (chips,) + stats.shape))
    logs = stats_all[:, 0]
    logs_top = jnp.max(logs, axis=0)
    log_total = logs_top + jnp.log(jnp.sum(jnp.exp(logs - logs_top), axis=0))
    label_logp = jnp.sum(stats_all[:, 1], axis=0) - log_total

    logp_all = lax.all_to_all(
        jnp.broadcast_to(label_logp[None], (members, plane_images)), "member", 0, 0
    )

    diff = jnp.exp(logits - log_total[:, None]) - onehot.astype(jnp.float32)
    low = diff.astype(jnp.bfloat16)
    partial = lax.dot_general(
        low, weight_both, (((1,), (1,)), ((), ())), preferred_element_type=jnp.float32
    )
    tail_columns = 4 * channels // images_here
    chunks = jnp.pad(
        partial.astype(jnp.bfloat16).reshape(chips, images_here, channels),
        ((0, 0), (0, 0), (0, tail_columns)),
    )
    diff, partial, chunks = lax.optimization_barrier((diff, partial, chunks))
    scale, log_joint, chunks = join_members(
        logp_all, label_logp[None], partial, act_plane, chunks
    )
    pieces = over_plane(chunks)

    grad_logits = scale[:, :1] * diff
    grad_sum = jnp.sum(grad_logits, axis=0)
    note = jnp.concatenate([log_joint[0], grad_sum[classes_here:]])
    note = lax.ppermute(note, "dp", swap)
    mean_loss = math.log(members) - (
        jnp.sum(log_joint) + jnp.sum(note[:plane_images])
    ) / (2 * plane_images)
    grad_head_bias = grad_sum[:classes_here] + note[plane_images:]
    rows = (((0,), (0,)), ((), ()))
    grad_low = grad_logits.astype(jnp.bfloat16)
    for_other = lax.dot_general(
        act_plane, grad_low[:, classes_here:], rows, preferred_element_type=jnp.float32
    ).astype(jnp.bfloat16)
    from_other = lax.ppermute(for_other, "dp", swap)
    grad_head_weight = (
        lax.dot_general(
            act_plane, grad_low[:, :classes_here], rows, preferred_element_type=jnp.float32
        )
        + from_other.astype(jnp.float32)
    ).astype(jnp.bfloat16)

    pieces, grad_head_weight, grad_head_bias, mean_loss = lax.optimization_barrier(
        (pieces, grad_head_weight, grad_head_bias, mean_loss)
    )
    sums = sum_tails(pieces, channels)
    grad_pooled = close_images(position // 2, pieces, scale, normed, inverse, norm_gain)
    sums = sums + lax.ppermute(sums, "dp", swap)
    grad_shift = sums[0]
    grad_gain = (sums[1] - shift_row * grad_shift) / gain_row
    return (
        mean_loss,
        grad_pooled[None],
        grad_gain[None],
        grad_shift[None],
        grad_head_weight[None],
        grad_head_bias[None],
    )


def solution(mesh):
    in_specs = (
        P("member", "dp", None, None),
        P(),
        P("member", None),
        P("member", None),
        P("member", None, "dp"),
        P("member", "dp"),
    )
    out_specs = (
        P(),
        P("member", "dp", None),
        P("member", None),
        P("member", None),
        P("member", None, "dp"),
        P("member", "dp"),
    )
    return jax.shard_map(
        per_device, mesh=mesh, in_specs=in_specs, out_specs=out_specs, check_vma=False
    )
```

time: 107 us -> 102 us (0.953)
  blocking collectives: 38.6 us -> 10.1 us
  starting transfers between devices: 32.5 us -> 45.1 us
  waiting for transfers between devices: 9.59 us -> 21.3 us
  other arithmetic: 9.29 us -> 5.79 us
  Pallas kernels: 0 us -> 2.94 us
    all_to_all x1 -> x0, blocking collectives: 28.6 us -> none  [per_device(): lax.all_to_all(jnp.broadcast_to(label_logp[None], (members, plane_images)...]
    all_to_all x0 -> x1, starting transfers between devices: none -> 15 us  [per_device(): lax.all_to_all(jnp.broadcast_to(label_logp[None], (members, plane_images)...]
    all_to_all x0 -> x1, waiting for transfers between devices: none -> 9.86 us  [per_device(): lax.all_to_all(jnp.broadcast_to(label_logp[None], (members, plane_images)...]
    pallas_call x0 -> x4, Pallas kernels: none -> 2.94 us  [the longest x1 1.08 us: join_members(): pl.pallas_call(join_kernel, grid=(1,), in_specs=[whole(*logp_all.shape),...]
    ppermute x2 -> x1, starting transfers between devices: 8.22 us -> 5.82 us  [per_device(): from_other = lax.ppermute(for_other, 'dp', swap)]
    all_to_all x2, waiting for transfers between devices: 8.58 us -> 9.97 us  [over_plane(): return lax.all_to_all(x, 'dp', 0, 0, axis_index_groups=planes)]
    ppermute x1, starting transfers between devices: 3.13 us -> 4.5 us  [per_device(): sums = sums + lax.ppermute(sums, 'dp', swap)]
    reduce_sum x7 -> x3, other arithmetic: 4.11 us -> 2.99 us  [the longest x1 1.79 us: per_device(): jnp.sum(features[0], axis=1, dtype=jnp.float32)]
  transfers between devices with their start and end apart: 8 -> 8, of which waited for: 3 -> 5; matrix products, arithmetic and copies ran while one was open for 8% -> 12% of each run, Pallas kernels for 0% -> 1%
where the time goes in v3:
time: 102 us; the launch traced here: 101 us
  starting transfers between devices  45.1 us (44%)
  waiting for transfers between devices  21.3 us (21%)
  matrix products  10.3 us (10%)
  blocking collectives  10.1 us (10%)
  other arithmetic  5.79 us (6%)
  between operations  3.36 us (3%)
  Pallas kernels  2.94 us (3%)
  local copies, waits for them, and re-layouts  2.42 us (2%)
    all_to_all x1, starting transfers between devices, per_device(): lax.all_to_all(jnp.broadcast_to(label_logp[None], (members, plane_images)...  15 us
    all_to_all x2, starting transfers between devices, over_plane(): return lax.all_to_all(x, 'dp', 0, 0, axis_index_groups=planes)  12.6 us
    all_to_all x1, blocking collectives, over_plane(): return lax.all_to_all(x, 'dp', 0, 0, axis_index_groups=planes)  10.1 us
    all_to_all x2, waiting for transfers between devices, over_plane(): return lax.all_to_all(x, 'dp', 0, 0, axis_index_groups=planes)  9.97 us
    all_to_all x1, waiting for transfers between devices, per_device(): lax.all_to_all(jnp.broadcast_to(label_logp[None], (members, plane_images)...  9.86 us
    ppermute x1, starting transfers between devices, per_device(): from_other = lax.ppermute(for_other, 'dp', swap)  5.82 us
    ppermute x1, starting transfers between devices, per_device(): sums = sums + lax.ppermute(sums, 'dp', swap)  4.5 us
    ppermute x1, starting transfers between devices, per_device(): weight_other = lax.ppermute(weight, 'dp', swap)  3.35 us
  transfers between devices with their start and end apart: 8, of which 5 were waited for; matrix products, arithmetic and copies ran while one was open for 12% of the time, Pallas kernels for 1%

profile of v3, /device:TPU:1, one launch (start us, length us, event | category | flops | bytes accessed | tf_op | source)
XLA Modules:
  0.0 101.3 jit_solution(15240399351758195251)
XLA Ops:
  0.6 0.0 copy-start
  0.6 0.0 copy-start.1
  0.7 0.0 copy-start.4
  0.7 0.0 copy-start.2
  0.7 0.0 copy-start.3
  0.7 1.8 %convert_reduce_fusion.total_ref = f32[16,1024]{1,0:T(8,128)S(1)} fusion(bf16[1,16,49,1024]{3,1,2,0:T(8,128)(2,1)} %param.6), kind=kLoop, calls=%fused_computation | loop fusion | flops 1589248 | bytes 1671168 | tf_op jit(solution)/shard_map/reduce_sum | solution.py:184
  2.5 0.0 copy-done
  2.5 0.0 copy-done.1
  2.5 1.0 shard_map.109
  3.5 9.0 %all-to-all-start = ((bf16[16,16,1024]{2,1,0:T(8,128)(2,1)}), bf16[16,16,1024]{2,1,0:T(8,128)(2,1)S(1)}, u32[]{:S(2)}, u32[]{:S(2)}) async-start(bf16[16,16,1024]{2,1,0:T(8,128)(2,1)} %get-tuple-element.19), calls=%async_computation | async-start | bytes 1048576 | tf_op jit(solution)/shard_map/all_to_all | solution.py:171
  12.5 0.0 copy-done.4
  12.5 3.3 %collective-permute-start = (bf16[1024,768]{1,0:T(8,128)(2,1)S(1)}, bf16[1024,768]{1,0:T(8,128)(2,1)}, u32[]{:S(2)}, u32[]{:S(2)}) collective-permute-start(bf16[1024,768]{1,0:T(8,128)(2,1)S(1)} %bitcast.35), channel_id=1, source_target_pairs={{0,1},{1,0},{2,3},{3,2},{4,5},{5,4},{6,7},{7,6},{8,9},{9,8},{10,11... | collective-permute-start | bytes 4718600 | tf_op jit(solution)/shard_map/ppermute | solution.py:180
  15.9 0.0 copy-done.2
  15.9 1.9 %collective-permute-start.1 = (f32[768]{0:T(1024)S(1)}, f32[768]{0:T(1024)S(1)}, u32[]{:S(2)}, u32[]{:S(2)}) collective-permute-start(f32[768]{0:T(1024)S(1)} %reduce.3), channel_id=1, source_target_pairs={{0,1},{1,0},{2,3},{3,2},{4,5},{5,4},{6,7},{7,6},{8,9},{9,8},{10,11... | collective-permute-start | bytes 9224 | tf_op jit(solution)/shard_map/ppermute | solution.py:181
  17.9 0.0 copy-done.3
  17.9 0.1 reshape.85
  18.0 0.1 eq.15
  18.1 0.9 collective-permute-done.1
  19.0 0.0 collective-permute-done
  19.0 9.2 %all-to-all-done = bf16[16,16,1024]{2,1,0:T(8,128)(2,1)S(1)} async-done(((bf16[16,16,1024]{2,1,0:T(8,128)(2,1)}), bf16[16,16,1024]{2,1,0:T(8,128)(2,1)S(1)}, u32[]{:S(2)}, u32[]{:S(2)}) %all-to-all-start) | async-done | bytes 524320 | tf_op jit(solution)/shard_map/all_to_all | solution.py:171
  28.2 2.5 %fusion.15 = (f32[256]{0:T(256)S(1)}, f32[256,1536]{1,0:T(8,128)S(1)}) fusion(f32[1536]{0:T(1024)S(1)} %pad_maximum_fusion.3, bf16[256,1024]{1,0:T(8,128)(2,1)S(1)} %bitcast.22, bf16[1024,768]{1,0:T(8,128)(2,1)} %collective-permute-done, bf16[1024,768]{1,0:T(8,128)(2,1)S(1)} %bitcast.36), kind=kOutput, calls=%fused_computation.40 | convolution fusion | flops 812384000 | bytes 5250048 | tf_op jit(solution)/shard_map/dot_general | solution.py:203
  30.7 0.5 exponential_reduce_fusion
  31.3 10.1 %all_to_all.23 = f32[16,2,256]{2,1,0:T(2,128)S(1)} all-to-all(f32[16,2,256]{2,1,0:T(2,128)S(1)} %broadcast_in_dim.15), channel_id=1, replica_groups={{0,2,4,6,8,10,12,14,16,18,20,22,24,26,28,30},{1,3,5,7,9,11,13,15,17,19,..., dimensions={0} | all-to-all | bytes 65536 | tf_op jit(solution)/shard_map/all_to_all | solution.py:171
  41.4 0.1 slice_reduce_fusion.3
  41.4 0.4 fusion.2
  41.9 0.6 broadcast_in_dim.16
  42.5 15.0 %all-to-all-start.2 = ((f32[16,1,256]{2,1,0:T(1,128)}), f32[16,1,256]{2,1,0:T(1,128)S(1)}, u32[]{:S(2)}, u32[]{:S(2)}) async-start(f32[16,1,256]{2,1,0:T(1,128)} %broadcast_in_dim.16), calls=%async_computation.2 | async-start | bytes 32768 | tf_op jit(solution)/shard_map/all_to_all | solution.py:214
  57.5 2.9 %fusion.16 = (bf16[256,1024]{1,0:T(8,128)(2,1)S(1)}, f32[256,1024]{1,0:T(8,128)S(1)}) fusion(bf16[1024,768]{1,0:T(8,128)(2,1)} %collective-permute-done, bf16[1024,768]{1,0:T(8,128)(2,1)} %bitcast.34, f32[256,1536]{1,0:T(8,128)S(1)} %fusion.2), kind=kOutput, calls=%fused_computation.41 | convolution fusion | flops 812253184 | bytes 6291456 | tf_op jit(solution)/shard_map/dot_general | solution.py:220
  60.4 0.9 pad.4._
  61.3 9.9 %all-to-all-done.2 = f32[16,1,256]{2,1,0:T(1,128)S(1)} async-done(((f32[16,1,256]{2,1,0:T(1,128)}), f32[16,1,256]{2,1,0:T(1,128)S(1)}, u32[]{:S(2)}, u32[]{:S(2)}) %all-to-all-start.2) | async-done | bytes 16416 | tf_op jit(solution)/shard_map/all_to_all | solution.py:214
  71.1 1.1 %shard_map.110 = (f32[256,128]{1,0:T(8,128)S(1)}, f32[1,256]{1,0:T(1,128)S(1)}, bf16[16,16,1280]{2,1,0:T(8,128)(2,1)}) custom-call(f32[16,256]{1,0:T(8,128)S(1)} %bitcast.26, f32[1,256]{1,0:T(1,128)S(1)} %bitcast.27, f32[256,1024]{1,0:T(8,128)S(1)} %get-tuple-element.20.partial_ref, bf16[256,1024]{1,0:T(8,128)(2,1)S(1)} %bitcast.23, ...), custom_call_target="tpu_custom_call", output_to_operand_aliasing={{2}: (4, {})} | custom-call | tf_op jit(solution)/shard_map/pallas_call | solution.py:73
  72.2 0.1 slice_reduce_fusion
  72.3 3.6 %all-to-all-start.3 = ((bf16[16,16,1280]{2,1,0:T(8,128)(2,1)}), bf16[16,16,1280]{2,1,0:T(8,128)(2,1)S(1)}, u32[]{:S(2)}, u32[]{:S(2)}) async-start(bf16[16,16,1280]{2,1,0:T(8,128)(2,1)} %get-tuple-element.22), calls=%async_computation.3 | async-start | bytes 1310720 | tf_op jit(solution)/shard_map/all_to_all | solution.py:171
  75.9 1.1 %multiply_reduce_fusion = (f32[1536]{0:T(1024)S(1)}, bf16[256,1536]{1,0:T(8,128)(2,1)}) fusion(f32[256,1536]{1,0:T(8,128)S(1)} %fusion.2, f32[256]{0:T(256)S(1)} %slice_reduce_fusion), kind=kLoop, calls=%fused_computation.11 | loop fusion | flops 1178112 | bytes 2366464 | tf_op jit(solution)/shard_map/reduce_sum | solution.py:235
  77.0 1.6 %convolution_convert_fusion = bf16[1024,768]{1,0:T(8,128)(2,1)S(1)} fusion(bf16[256,1024]{1,0:T(8,128)(2,1)S(1)} %bitcast.24, bf16[256,1536]{1,0:T(8,128)(2,1)} %get-tuple-element.41), kind=kOutput, calls=%fused_computation.7 | convolution fusion | flops 403439616 | bytes 2490368 | tf_op jit(solution)/shard_map/dot_general | solution.py:244
  78.6 5.8 %collective-permute-start.2 = (bf16[1024,768]{1,0:T(8,128)(2,1)S(1)}, bf16[1024,768]{1,0:T(8,128)(2,1)}, u32[]{:S(2)}, u32[]{:S(2)}) collective-permute-start(bf16[1024,768]{1,0:T(8,128)(2,1)S(1)} %convolution_convert_fusion), channel_id=1, source_target_pairs={{0,1},{1,0},{2,3},{3,2},{4,5},{5,4},{6,7},{7,6},{8,9},{9,8},{10,11... | collective-permute-start | bytes 4718600 | tf_op jit(solution)/shard_map/ppermute | solution.py:247
  84.5 1.9 %collective-permute-start.3 = (f32[1024]{0:T(1024)S(1)}, f32[1024]{0:T(1024)S(1)}, u32[]{:S(2)}, u32[]{:S(2)}) collective-permute-start(f32[1024]{0:T(1024)S(1)} %pad_maximum_fusion.4), channel_id=1, source_target_pairs={{0,1},{1,0},{2,3},{3,2},{4,5},{5,4},{6,7},{7,6},{8,9},{9,8},{10,11... | collective-permute-start | bytes 12296 | tf_op jit(solution)/shard_map/ppermute | solution.py:237
  86.4 0.6 reduce_sum.78
  87.0 0.5 collective-permute-done.3
  87.6 0.6 slice_reduce_fusion.2
  89.5 0.0 collective-permute-done.2
  89.5 3.3 %add_convert_fusion = bf16[1024,768]{1,0:T(8,128)(2,1)} fusion(bf16[1024,768]{1,0:T(8,128)(2,1)} %collective-permute-done.2, bf16[256,1024]{1,0:T(8,128)(2,1)S(1)} %bitcast.25, bf16[256,1536]{1,0:T(8,128)(2,1)} %get-tuple-element.41), kind=kOutput, calls=%fused_computation.2 | convolution fusion | flops 405012480 | bytes 4063232 | tf_op jit(solution)/shard_map/dot_general | solution.py:249
  92.8 0.8 all-to-all-done.3.pieces_ref.tails_ref
  93.6 4.5 %collective-permute-start.4 = (f32[2,1024]{1,0:T(2,128)S(1)}, f32[2,1024]{1,0:T(2,128)S(1)}, u32[]{:S(2)}, u32[]{:S(2)}) collective-permute-start(f32[2,1024]{1,0:T(2,128)S(1)} %shard_map.112), channel_id=1, source_target_pairs={{0,1},{1,0},{2,3},{3,2},{4,5},{5,4},{6,7},{7,6},{8,9},{9,8},{10,11... | collective-permute-start | bytes 24584 | tf_op jit(solution)/shard_map/ppermute | solution.py:260
  98.1 0.6 broadcast_in_dim.19
  98.7 0.8 shard_map.111
  99.5 0.0 collective-permute-done.4
  99.5 0.6 fusion.11
  (16 shorter events, 0.2 us)
Async XLA Ops:
  0.6 1.8 %copy-start = (f32[1,1024]{1,0:T(1,128)S(1)}, f32[1,1024]{1,0:T(1,128)}, u32[]{:S(2)}) copy-start(f32[1,1024]{1,0:T(1,128)} %gain_ref.3) | copy-start | bytes 12292
  0.6 1.8 %copy-start.1 = (f32[1,1024]{1,0:T(1,128)S(1)}, f32[1,1024]{1,0:T(1,128)}, u32[]{:S(2)}) copy-start(f32[1,1024]{1,0:T(1,128)} %shift_ref.1) | copy-start | bytes 12292
  0.7 11.9 %copy-start.4 = (bf16[1,1024,768]{2,1,0:T(8,128)(2,1)S(1)}, bf16[1,1024,768]{2,1,0:T(8,128)(2,1)}, u32[]{:S(2)}) copy-start(bf16[1,1024,768]{2,1,0:T(8,128)(2,1)} %param.10) | copy-start | bytes 4718596
  0.7 15.2 %copy-start.2 = (f32[1,768]{1,0:T(1,128)S(1)}, f32[1,768]{1,0:T(1,128)}, u32[]{:S(2)}) copy-start(f32[1,768]{1,0:T(1,128)} %param.11) | copy-start | bytes 9220
  0.7 17.2 %copy-start.3 = (s32[512]{0:T(512)S(1)}, s32[512]{0:T(512)}, u32[]{:S(2)}) copy-start(s32[512]{0:T(512)} %param.7) | copy-start | bytes 6148
  3.5 24.7 %all-to-all-start = ((bf16[16,16,1024]{2,1,0:T(8,128)(2,1)}), bf16[16,16,1024]{2,1,0:T(8,128)(2,1)S(1)}, u32[]{:S(2)}, u32[]{:S(2)}) async-start(bf16[16,16,1024]{2,1,0:T(8,128)(2,1)} %get-tuple-element.19), calls=%async_computation | async-start | bytes 1048576 | tf_op jit(solution)/shard_map/all_to_all | solution.py:171
  12.5 6.5 %collective-permute-start = (bf16[1024,768]{1,0:T(8,128)(2,1)S(1)}, bf16[1024,768]{1,0:T(8,128)(2,1)}, u32[]{:S(2)}, u32[]{:S(2)}) collective-permute-start(bf16[1024,768]{1,0:T(8,128)(2,1)S(1)} %bitcast.35), channel_id=1, source_target_pairs={{0,1},{1,0},{2,3},{3,2},{4,5},{5,4},{6,7},{7,6},{8,9},{9,8},{10,11... | collective-permute-start | bytes 4718600 | tf_op jit(solution)/shard_map/ppermute | solution.py:180
  15.9 3.1 %collective-permute-start.1 = (f32[768]{0:T(1024)S(1)}, f32[768]{0:T(1024)S(1)}, u32[]{:S(2)}, u32[]{:S(2)}) collective-permute-start(f32[768]{0:T(1024)S(1)} %reduce.3), channel_id=1, source_target_pairs={{0,1},{1,0},{2,3},{3,2},{4,5},{5,4},{6,7},{7,6},{8,9},{9,8},{10,11... | collective-permute-start | bytes 9224 | tf_op jit(solution)/shard_map/ppermute | solution.py:181
  42.5 28.6 %all-to-all-start.2 = ((f32[16,1,256]{2,1,0:T(1,128)}), f32[16,1,256]{2,1,0:T(1,128)S(1)}, u32[]{:S(2)}, u32[]{:S(2)}) async-start(f32[16,1,256]{2,1,0:T(1,128)} %broadcast_in_dim.16), calls=%async_computation.2 | async-start | bytes 32768 | tf_op jit(solution)/shard_map/all_to_all | solution.py:214
  72.3 21.3 %all-to-all-start.3 = ((bf16[16,16,1280]{2,1,0:T(8,128)(2,1)}), bf16[16,16,1280]{2,1,0:T(8,128)(2,1)S(1)}, u32[]{:S(2)}, u32[]{:S(2)}) async-start(bf16[16,16,1280]{2,1,0:T(8,128)(2,1)} %get-tuple-element.22), calls=%async_computation.3 | async-start | bytes 1310720 | tf_op jit(solution)/shard_map/all_to_all | solution.py:171
  78.6 10.8 %collective-permute-start.2 = (bf16[1024,768]{1,0:T(8,128)(2,1)S(1)}, bf16[1024,768]{1,0:T(8,128)(2,1)}, u32[]{:S(2)}, u32[]{:S(2)}) collective-permute-start(bf16[1024,768]{1,0:T(8,128)(2,1)S(1)} %convolution_convert_fusion), channel_id=1, source_target_pairs={{0,1},{1,0},{2,3},{3,2},{4,5},{5,4},{6,7},{7,6},{8,9},{9,8},{10,11... | collective-permute-start | bytes 4718600 | tf_op jit(solution)/shard_map/ppermute | solution.py:247
  84.5 3.1 %collective-permute-start.3 = (f32[1024]{0:T(1024)S(1)}, f32[1024]{0:T(1024)S(1)}, u32[]{:S(2)}, u32[]{:S(2)}) collective-permute-start(f32[1024]{0:T(1024)S(1)} %pad_maximum_fusion.4), channel_id=1, source_target_pairs={{0,1},{1,0},{2,3},{3,2},{4,5},{5,4},{6,7},{7,6},{8,9},{9,8},{10,11... | collective-permute-start | bytes 12296 | tf_op jit(solution)/shard_map/ppermute | solution.py:237
  93.6 5.9 %collective-permute-start.4 = (f32[2,1024]{1,0:T(2,128)S(1)}, f32[2,1024]{1,0:T(2,128)S(1)}, u32[]{:S(2)}, u32[]{:S(2)}) collective-permute-start(f32[2,1024]{1,0:T(2,128)S(1)} %shard_map.112), channel_id=1, source_target_pairs={{0,1},{1,0},{2,3},{3,2},{4,5},{5,4},{6,7},{7,6},{8,9},{9,8},{10,11... | collective-permute-start | bytes 24584 | tf_op jit(solution)/shard_map/ppermute | solution.py:260

commit v4 on v3

--- a/solution.py
+++ b/solution.py
@@ -95,22 +95,36 @@
     )(logp_all, label_logp, partial, act, chunks)
 
 
-def close_kernel(_, pieces_ref, scale_ref, normed_ref, inverse_ref, gain_ref, grad_ref):
+def close_kernel(
+    place, pieces_ref, scale_ref, normed_ref, inverse_ref, gain_ref, shift_ref, sums_ref, bias_ref, *outs
+):
+    grad_ref, grad_gain_ref, grad_shift_ref, grad_bias_ref, joint_ref = outs
     received = pieces_ref[0].astype(jnp.float32)
     for k in range(1, pieces_ref.shape[0]):
         received = received + pieces_ref[k].astype(jnp.float32)
     normed = normed_ref[...]
-    scaled = scale_ref[:, :1] * received * gain_ref[...]
+    gain = gain_ref[...]
+    scaled = scale_ref[:, :1] * received * gain
     grad_ref[...] = inverse_ref[:, :1] * (
         scaled
         - jnp.mean(scaled, axis=-1, keepdims=True)
         - normed * jnp.mean(scaled * normed, axis=-1, keepdims=True)
     )
-
-
-def close_images(chip, pieces, scale, normed, inverse, gain_row):
+    sums = sums_ref[0] + sums_ref[1]
+    grad_shift_ref[...] = sums[:1]
+    grad_gain_ref[...] = (sums[1:2] - shift_ref[...] * sums[:1]) / gain
+    plane_images = sums.shape[1] - bias_ref.shape[1]
+    other_note = jnp.where(place[1] == 0, sums_ref[1, 2:3], sums_ref[0, 2:3])
+    grad_bias_ref[...] = bias_ref[...] + other_note[:, plane_images:]
+    joint_ref[...] = jnp.mean(sums[2:3, :plane_images], axis=1, keepdims=True) / 2
+
+
+def close_images(
+    position, pieces, scale, normed, inverse, gain_row, shift_row, sums, bias_part
+):
     images, channels = normed.shape
-    whole = lambda *shape: pl.BlockSpec(shape, lambda i, chip: (0,) * len(shape))
+    whole = lambda *shape: pl.BlockSpec(shape, lambda i, place: (0,) * len(shape))
+    small = [(1, channels), (1, channels), bias_part.shape, (1, 1)]
     return pl.pallas_call(
         close_kernel,
         grid_spec=pltpu.PrefetchScalarGridSpec(
@@ -118,22 +132,33 @@
             grid=(1,),
             in_specs=[
                 whole(pieces.shape[0], images, channels),
-                pl.BlockSpec((images, 128), lambda i, chip: (chip[0], 0)),
+                pl.BlockSpec((images, 128), lambda i, place: (place[0], 0)),
                 whole(images, channels),
                 whole(images, 128),
                 whole(1, channels),
+                whole(1, channels),
+                whole(*sums.shape),
+                whole(*bias_part.shape),
             ],
-            out_specs=whole(images, channels),
+            out_specs=[whole(images, channels)] + [whole(*shape) for shape in small],
         ),
-        out_shape=jax.ShapeDtypeStruct((images, channels), jnp.float32),
-        cost_estimate=pl.CostEstimate(
-            flops=40 * images * channels, bytes_accessed=2**20, transcendentals=0
-        ),
+        out_shape=[jax.ShapeDtypeStruct((images, channels), jnp.float32)]
+        + [jax.ShapeDtypeStruct(shape, jnp.float32) for shape in small],
         compiler_params=pltpu.CompilerParams(vmem_limit_bytes=16 * 2**20),
-    )(jnp.reshape(chip, (1,)), pieces, scale, normed, inverse, gain_row)
-
-
-def sum_tails_kernel(tails_ref, sums_ref):
+    )(
+        jnp.stack([position // 2, lax.rem(position, 2)]),
+        pieces,
+        scale,
+        normed,
+        inverse,
+        gain_row,
+        shift_row,
+        sums,
+        bias_part,
+    )
+
+
+def sum_tails_kernel(tails_ref, note_ref, sums_ref):
     tail = tails_ref[0].astype(jnp.float32)
     for k in range(1, tails_ref.shape[0]):
         tail = tail + tails_ref[k].astype(jnp.float32)
@@ -143,19 +168,24 @@
     for r in range(2):
         for k in range(quarter):
             sums_ref[r : r + 1, k * width : (k + 1) * width] = tail[r * quarter + k][None]
-
-
-def sum_tails(pieces, channels):
+    sums_ref[2:3] = note_ref[...]
+
+
+def sum_tails(pieces, note):
     copies, lines, whole_width = pieces.shape
+    channels = note.shape[1]
     width = whole_width - channels
     return pl.pallas_call(
         sum_tails_kernel,
         grid=(1,),
-        in_specs=[pl.BlockSpec((copies, lines, width), lambda i: (0, 0, channels // width))],
-        out_specs=pl.BlockSpec((2, channels), lambda i: (0, 0)),
-        out_shape=jax.ShapeDtypeStruct((2, channels), jnp.float32),
+        in_specs=[
+            pl.BlockSpec((copies, lines, width), lambda i: (0, 0, channels // width)),
+            pl.BlockSpec((1, channels), lambda i: (0, 0)),
+        ],
+        out_specs=pl.BlockSpec((3, channels), lambda i: (0, 0)),
+        out_shape=jax.ShapeDtypeStruct((3, channels), jnp.float32),
         compiler_params=pltpu.CompilerParams(vmem_limit_bytes=16 * 2**20),
-    )(pieces)
+    )(pieces, note)
 
 
 def per_device(features, labels, norm_gain, norm_bias, head_weight, head_bias):
@@ -231,42 +261,39 @@
     )
     pieces = over_plane(chunks)
 
-    grad_logits = scale[:, :1] * diff
-    grad_sum = jnp.sum(grad_logits, axis=0)
-    note = jnp.concatenate([log_joint[0], grad_sum[classes_here:]])
-    note = lax.ppermute(note, "dp", swap)
-    mean_loss = math.log(members) - (
-        jnp.sum(log_joint) + jnp.sum(note[:plane_images])
-    ) / (2 * plane_images)
-    grad_head_bias = grad_sum[:classes_here] + note[plane_images:]
     rows = (((0,), (0,)), ((), ()))
-    grad_low = grad_logits.astype(jnp.bfloat16)
+    grad_other = scale[:, :1] * diff[:, classes_here:]
+    bias_other_part = jnp.sum(grad_other, axis=0)
     for_other = lax.dot_general(
-        act_plane, grad_low[:, classes_here:], rows, preferred_element_type=jnp.float32
+        act_plane, grad_other.astype(jnp.bfloat16), rows, preferred_element_type=jnp.float32
     ).astype(jnp.bfloat16)
     from_other = lax.ppermute(for_other, "dp", swap)
+    grad_mine = scale[:, :1] * diff[:, :classes_here]
+    bias_part = jnp.sum(grad_mine, axis=0)
     grad_head_weight = (
         lax.dot_general(
-            act_plane, grad_low[:, :classes_here], rows, preferred_element_type=jnp.float32
+            act_plane, grad_mine.astype(jnp.bfloat16), rows, preferred_element_type=jnp.float32
         )
         + from_other.astype(jnp.float32)
-    ).astype(jnp.bfloat16)
-
-    pieces, grad_head_weight, grad_head_bias, mean_loss = lax.optimization_barrier(
-        (pieces, grad_head_weight, grad_head_bias, mean_loss)
-    )
-    sums = sum_tails(pieces, channels)
-    grad_pooled = close_images(position // 2, pieces, scale, normed, inverse, norm_gain)
-    sums = sums + lax.ppermute(sums, "dp", swap)
-    grad_shift = sums[0]
-    grad_gain = (sums[1] - shift_row * grad_shift) / gain_row
+    ).astype(jnp.bfloat16)[None]
+
+    note = jnp.concatenate([log_joint, bias_other_part[None]], axis=1)
+    pieces, grad_head_weight, note, bias_part = lax.optimization_barrier(
+        (pieces, grad_head_weight, note, bias_part[None])
+    )
+    pairs = [[2 * chip, 2 * chip + 1] for chip in range(chips)]
+    sums = lax.all_gather(sum_tails(pieces, note), "dp", axis_index_groups=pairs)
+    grad_pooled, grad_gain, grad_shift, grad_head_bias, joint_mean = close_images(
+        position, pieces, scale, normed, inverse, norm_gain, norm_bias, sums, bias_part
+    )
+    mean_loss = math.log(members) - joint_mean[0, 0]
     return (
         mean_loss,
         grad_pooled[None],
-        grad_gain[None],
-        grad_shift[None],
-        grad_head_weight[None],
-        grad_head_bias[None],
+        grad_gain,
+        grad_shift,
+        grad_head_weight,
+        grad_head_bias,
     )
 
 

time: 102 us -> 101 us (level)
  starting transfers between devices: 45.1 us -> 38.7 us
  blocking collectives: 10.1 us -> 14.2 us
  waiting for transfers between devices: 21.3 us -> 24.7 us
  other arithmetic: 5.79 us -> 4.64 us
    ppermute x2 -> x0, starting transfers between devices: 6.42 us -> none  [the longest x1 4.5 us: per_device(): sums = sums + lax.ppermute(sums, 'dp', swap)]
    all_gather x0 -> x1, blocking collectives: none -> 4.08 us  [per_device(): lax.all_gather(sum_tails(pieces, note), 'dp', axis_index_groups=pairs)]
    ppermute x1, waiting for transfers between devices: 0.01 us -> 3.04 us  [per_device(): from_other = lax.ppermute(for_other, 'dp', swap)]
    all_to_all x2, waiting for transfers between devices: 9.97 us -> 12.5 us  [over_plane(): return lax.all_to_all(x, 'dp', 0, 0, axis_index_groups=planes)]
    reduce_sum x3 -> x1, other arithmetic: 2.29 us -> 0.18 us  [per_device(): bias_part = jnp.sum(grad_mine, axis=0)]
    all_to_all x1, waiting for transfers between devices: 9.86 us -> 8.34 us  [per_device(): lax.all_to_all(jnp.broadcast_to(label_logp[None], (members, plane_images)...]
    sub x1, other arithmetic: 0.44 us -> 1.95 us  [per_device(): diff = jnp.exp(logits - log_total[:, None]) - onehot.astype(jnp.float32)]
  transfers between devices with their start and end apart: 8 -> 6, of which waited for: 5 -> 5; matrix products, arithmetic and copies ran while one was open for 12% -> 11% of each run, Pallas kernels for 1% -> 0%
where the time goes in v4:
time: 101 us; the launch traced here: 100 us
  starting transfers between devices  38.7 us (38%)
  waiting for transfers between devices  24.7 us (24%)
  blocking collectives  14.2 us (14%)
  matrix products  10 us (10%)
  other arithmetic  4.64 us (5%)
  Pallas kernels  3.45 us (3%)
  between operations  2.71 us (3%)
  local copies, waits for them, and re-layouts  1.88 us (2%)
    all_to_all x1, starting transfers between devices, per_device(): lax.all_to_all(jnp.broadcast_to(label_logp[None], (members, plane_images)...  15 us
    all_to_all x2, starting transfers between devices, over_plane(): return lax.all_to_all(x, 'dp', 0, 0, axis_index_groups=planes)  12.6 us
    all_to_all x2, waiting for transfers between devices, over_plane(): return lax.all_to_all(x, 'dp', 0, 0, axis_index_groups=planes)  12.5 us
    all_to_all x1, blocking collectives, over_plane(): return lax.all_to_all(x, 'dp', 0, 0, axis_index_groups=planes)  10.1 us
    all_to_all x1, waiting for transfers between devices, per_device(): lax.all_to_all(jnp.broadcast_to(label_logp[None], (members, plane_images)...  8.34 us
    ppermute x1, starting transfers between devices, per_device(): from_other = lax.ppermute(for_other, 'dp', swap)  5.82 us
    all_gather x1, blocking collectives, per_device(): lax.all_gather(sum_tails(pieces, note), 'dp', axis_index_groups=pairs)  4.08 us
    ppermute x1, starting transfers between devices, per_device(): weight_other = lax.ppermute(weight, 'dp', swap)  3.35 us
  transfers between devices with their start and end apart: 6, of which 5 were waited for; matrix products, arithmetic and copies ran while one was open for 11% of the time, Pallas kernels for 0%

profile of v4, /device:TPU:1, one launch (start us, length us, event | category | flops | bytes accessed | tf_op | source)
XLA Modules:
  0.0 100.2 jit_solution(11358914381641380106)
XLA Ops:
  0.6 0.0 copy-start
  0.6 0.0 copy-start.1
  0.7 0.0 copy-start.5
  0.7 0.0 copy-start.3
  0.7 0.0 copy-start.4
  0.7 1.8 %convert_reduce_fusion.total_ref = f32[16,1024]{1,0:T(8,128)S(1)} fusion(bf16[1,16,49,1024]{3,1,2,0:T(8,128)(2,1)} %param.6), kind=kLoop, calls=%fused_computation | loop fusion | flops 1589248 | bytes 1671168 | tf_op jit(solution)/shard_map/reduce_sum | solution.py:214
  2.5 0.0 copy-done
  2.5 0.0 copy-done.1
  2.5 1.0 %shard_map.109 = (f32[16,1024]{1,0:T(8,128)S(1)}, f32[16,128]{1,0:T(8,128)S(1)}, bf16[16,16,1024]{2,1,0:T(8,128)(2,1)}) custom-call(f32[16,1024]{1,0:T(8,128)S(1)} %convert_reduce_fusion.total_ref, f32[1,1024]{1,0:T(1,128)S(1)} %copy-done, f32[1,1024]{1,0:T(1,128)S(1)} %copy-done.1), custom_call_target="tpu_custom_call" | custom-call | tf_op jit(solution)/shard_map/pallas_call | solution.py:29
  3.5 9.0 %all-to-all-start = ((bf16[16,16,1024]{2,1,0:T(8,128)(2,1)}), bf16[16,16,1024]{2,1,0:T(8,128)(2,1)S(1)}, u32[]{:S(2)}, u32[]{:S(2)}) async-start(bf16[16,16,1024]{2,1,0:T(8,128)(2,1)} %get-tuple-element.24), calls=%async_computation | async-start | bytes 1048576 | tf_op jit(solution)/shard_map/all_to_all | solution.py:201
  12.5 0.0 copy-done.5
  12.5 3.3 %collective-permute-start = (bf16[1024,768]{1,0:T(8,128)(2,1)S(1)}, bf16[1024,768]{1,0:T(8,128)(2,1)}, u32[]{:S(2)}, u32[]{:S(2)}) collective-permute-start(bf16[1024,768]{1,0:T(8,128)(2,1)S(1)} %bitcast.35), channel_id=1, source_target_pairs={{0,1},{1,0},{2,3},{3,2},{4,5},{5,4},{6,7},{7,6},{8,9},{9,8},{10,11... | collective-permute-start | bytes 4718600 | tf_op jit(solution)/shard_map/ppermute | solution.py:210
  15.9 0.0 copy-done.3
  15.9 1.9 %collective-permute-start.1 = (f32[768]{0:T(1024)S(1)}, f32[768]{0:T(1024)S(1)}, u32[]{:S(2)}, u32[]{:S(2)}) collective-permute-start(f32[768]{0:T(1024)S(1)} %reduce.3), channel_id=1, source_target_pairs={{0,1},{1,0},{2,3},{3,2},{4,5},{5,4},{6,7},{7,6},{8,9},{9,8},{10,11... | collective-permute-start | bytes 9224 | tf_op jit(solution)/shard_map/ppermute | solution.py:211
  17.9 0.0 copy-done.4
  17.9 0.1 reshape.84
  18.0 0.1 eq.15
  18.1 0.9 collective-permute-done.1
  19.0 0.0 collective-permute-done
  19.0 9.2 %all-to-all-done = bf16[16,16,1024]{2,1,0:T(8,128)(2,1)S(1)} async-done(((bf16[16,16,1024]{2,1,0:T(8,128)(2,1)}), bf16[16,16,1024]{2,1,0:T(8,128)(2,1)S(1)}, u32[]{:S(2)}, u32[]{:S(2)}) %all-to-all-start) | async-done | bytes 524320 | tf_op jit(solution)/shard_map/all_to_all | solution.py:201
  28.2 2.5 %fusion.21 = (f32[256]{0:T(256)S(1)}, f32[256,1536]{1,0:T(8,128)S(1)}) fusion(f32[1536]{0:T(1024)S(1)} %pad_maximum_fusion.3, bf16[256,1024]{1,0:T(8,128)(2,1)S(1)} %bitcast.25, bf16[1024,768]{1,0:T(8,128)(2,1)} %collective-permute-done, bf16[1024,768]{1,0:T(8,128)(2,1)S(1)} %bitcast.36), kind=kOutput, calls=%fused_computation.42 | convolution fusion | flops 812384000 | bytes 5250048 | tf_op jit(solution)/shard_map/dot_general | solution.py:233
  30.7 0.0 copy-start.2
  30.7 0.5 exponential_reduce_fusion
  31.3 10.1 %all_to_all.23 = f32[16,2,256]{2,1,0:T(2,128)S(1)} all-to-all(f32[16,2,256]{2,1,0:T(2,128)S(1)} %broadcast_in_dim.17), channel_id=1, replica_groups={{0,2,4,6,8,10,12,14,16,18,20,22,24,26,28,30},{1,3,5,7,9,11,13,15,17,19,..., dimensions={0} | all-to-all | bytes 65536 | tf_op jit(solution)/shard_map/all_to_all | solution.py:201
  41.4 0.1 slice_reduce_fusion.2
  41.4 0.0 copy-done.2
  41.5 0.6 broadcast_in_dim.18
  42.1 15.0 %all-to-all-start.2 = ((f32[16,1,256]{2,1,0:T(1,128)}), f32[16,1,256]{2,1,0:T(1,128)S(1)}, u32[]{:S(2)}, u32[]{:S(2)}) async-start(f32[16,1,256]{2,1,0:T(1,128)} %broadcast_in_dim.18), calls=%async_computation.2 | async-start | bytes 32768 | tf_op jit(solution)/shard_map/all_to_all | solution.py:244
  57.1 0.0 copy-start.6
  57.1 2.0 %fusion.2 = f32[256,1536]{1,0:T(8,128)S(1)} fusion(f32[256,1536]{1,0:T(8,128)} %copy-done.2, f32[256]{0:T(256)S(1)} %get-tuple-element.49, s32[1536]{0:T(1024)S(1)} %pad_add_fusion, s32[256]{0:T(256)S(1)} %eq.15), kind=kLoop, calls=%fused_computation.9 | loop fusion | flops 1572864 | bytes 3153920 | tf_op jit(solution)/shard_map/sub | solution.py:248
  59.0 0.0 copy-done.6
  59.0 2.4 %fusion.22 = (bf16[256,1024]{1,0:T(8,128)(2,1)S(1)}, f32[256,1024]{1,0:T(8,128)S(1)}) fusion(bf16[1024,768]{1,0:T(8,128)(2,1)} %collective-permute-done, bf16[1024,768]{1,0:T(8,128)(2,1)S(1)} %bitcast.37, f32[256,1536]{1,0:T(8,128)S(1)} %fusion.2), kind=kOutput, calls=%fused_computation.43 | convolution fusion | flops 812253184 | bytes 6291456 | tf_op jit(solution)/shard_map/dot_general | solution.py:250
  61.5 0.9 pad.4._
  62.4 8.3 %all-to-all-done.2 = f32[16,1,256]{2,1,0:T(1,128)S(1)} async-done(((f32[16,1,256]{2,1,0:T(1,128)}), f32[16,1,256]{2,1,0:T(1,128)S(1)}, u32[]{:S(2)}, u32[]{:S(2)}) %all-to-all-start.2) | async-done | bytes 16416 | tf_op jit(solution)/shard_map/all_to_all | solution.py:244
  70.7 1.0 %shard_map.110 = (f32[256,128]{1,0:T(8,128)S(1)}, f32[1,256]{1,0:T(1,128)S(1)}, bf16[16,16,1280]{2,1,0:T(8,128)(2,1)}) custom-call(f32[16,256]{1,0:T(8,128)S(1)} %bitcast.29, f32[1,256]{1,0:T(1,128)S(1)} %bitcast.31, f32[256,1024]{1,0:T(8,128)S(1)} %get-tuple-element.25.partial_ref, bf16[256,1024]{1,0:T(8,128)(2,1)S(1)} %bitcast.26, ...), custom_call_target="tpu_custom_call", output_to_operand_aliasing={{2}: (4, {})} | custom-call | tf_op jit(solution)/shard_map/pallas_call | solution.py:73
  71.7 3.6 %all-to-all-start.3 = ((bf16[16,16,1280]{2,1,0:T(8,128)(2,1)}), bf16[16,16,1280]{2,1,0:T(8,128)(2,1)S(1)}, u32[]{:S(2)}, u32[]{:S(2)}) async-start(bf16[16,16,1280]{2,1,0:T(8,128)(2,1)} %get-tuple-element.27), calls=%async_computation.3 | async-start | bytes 1310720 | tf_op jit(solution)/shard_map/all_to_all | solution.py:201
  75.3 0.1 slice_reduce_fusion
  75.5 1.8 %convolution_convert_fusion = bf16[1024,768]{1,0:T(8,128)(2,1)} fusion(bf16[256,1024]{1,0:T(8,128)(2,1)S(1)} %bitcast.27, f32[256,1536]{1,0:T(8,128)S(1)} %fusion.2, f32[256]{0:T(256)S(1)} %slice_reduce_fusion), kind=kOutput, calls=%fused_computation.7 | convolution fusion | flops 403832832 | bytes 2884608 | tf_op jit(solution)/shard_map/dot_general | solution.py:267
  77.3 5.8 %collective-permute-start.2 = (bf16[1024,768]{1,0:T(8,128)(2,1)}, bf16[1024,768]{1,0:T(8,128)(2,1)}, u32[]{:S(2)}, u32[]{:S(2)}) collective-permute-start(bf16[1024,768]{1,0:T(8,128)(2,1)} %convolution_convert_fusion), channel_id=1, source_target_pairs={{0,1},{1,0},{2,3},{3,2},{4,5},{5,4},{6,7},{7,6},{8,9},{9,8},{10,11... | collective-permute-start | bytes 4718600 | tf_op jit(solution)/shard_map/ppermute | solution.py:270
  83.1 0.1 pad_add_fusion.1.place
  83.2 0.2 fusion.5
  83.4 3.0 %collective-permute-done.2 = bf16[1024,768]{1,0:T(8,128)(2,1)} collective-permute-done((bf16[1024,768]{1,0:T(8,128)(2,1)}, bf16[1024,768]{1,0:T(8,128)(2,1)}, u32[]{:S(2)}, u32[]{:S(2)}) %collective-permute-start.2) | collective-permute-done | bytes 1572896 | tf_op jit(solution)/shard_map/ppermute | solution.py:270
  86.5 3.2 %fusion.3 = bf16[1,1024,768]{2,1,0:T(8,128)(2,1)} fusion(bf16[1024,768]{1,0:T(8,128)(2,1)} %collective-permute-done.2, bf16[256,1024]{1,0:T(8,128)(2,1)S(1)} %bitcast.28, f32[256,1536]{1,0:T(8,128)S(1)} %fusion.2, f32[256]{0:T(256)S(1)} %slice_reduce_fusion), kind=kOutput, calls=%fused_computation.10 | convolution fusion | flops 405405696 | bytes 4457472 | tf_op jit(solution)/shard_map/dot_general | solution.py:274
  89.7 3.3 %all-to-all-done.3.tails_ref.pieces_ref = bf16[16,16,1280]{2,1,0:T(8,128)(2,1)S(1)} async-done(((bf16[16,16,1280]{2,1,0:T(8,128)(2,1)}), bf16[16,16,1280]{2,1,0:T(8,128)(2,1)S(1)}, u32[]{:S(2)}, u32[]{:S(2)}) %all-to-all-start.3) | async-done | bytes 655392 | tf_op jit(solution)/shard_map/all_to_all | solution.py:201
  93.0 4.1 %all-gather.1.sums_ref = f32[2,3,1024]{2,1,0:T(4,128)S(1)} all-gather(f32[1,3,1024]{2,1,0:T(4,128)S(1)} %bitcast.30), channel_id=2, replica_groups={{0,1},{2,3},{4,5},{6,7},{8,9},{10,11},{12,13},{14,15},{16,17},{18,19},{..., dimensions={0}, use_global_device_ids=true | all-gather | bytes 36864 | tf_op jit(solution)/shard_map/all_gather | solution.py:285
  97.1 1.4 %shard_map.112 = (f32[16,1024]{1,0:T(8,128)}, f32[1,1024]{1,0:T(1,128)}, f32[1,1024]{1,0:T(1,128)}, f32[1,768]{1,0:T(1,128)}, f32[1,1]{1,0:T(1,128)}) custom-call(s32[2]{0:T(128)S(1)} %pad_add_fusion.1.place, bf16[16,16,1280]{2,1,0:T(8,128)(2,1)S(1)} %all-to-all-done.3.tails_ref.pieces_ref, f32[256,128]{1,0:T(8,128)S(1)} %get-tuple-element.28.scale_ref, ...), custom_call_target="tpu_custom_call" | custom-call | tf_op jit(solution)/shard_map/pallas_call | solution.py:128
  (15 shorter events, 0.2 us)
Async XLA Ops:
  0.6 1.8 %copy-start = (f32[1,1024]{1,0:T(1,128)S(1)}, f32[1,1024]{1,0:T(1,128)}, u32[]{:S(2)}) copy-start(f32[1,1024]{1,0:T(1,128)} %gain_ref.3) | copy-start | bytes 12292
  0.6 1.8 %copy-start.1 = (f32[1,1024]{1,0:T(1,128)S(1)}, f32[1,1024]{1,0:T(1,128)}, u32[]{:S(2)}) copy-start(f32[1,1024]{1,0:T(1,128)} %shift_ref.3) | copy-start | bytes 12292
  0.7 11.9 %copy-start.5 = (bf16[1,1024,768]{2,1,0:T(8,128)(2,1)S(1)}, bf16[1,1024,768]{2,1,0:T(8,128)(2,1)}, u32[]{:S(2)}) copy-start(bf16[1,1024,768]{2,1,0:T(8,128)(2,1)} %param.10) | copy-start | bytes 4718596
  0.7 15.2 %copy-start.3 = (f32[1,768]{1,0:T(1,128)S(1)}, f32[1,768]{1,0:T(1,128)}, u32[]{:S(2)}) copy-start(f32[1,768]{1,0:T(1,128)} %param.11) | copy-start | bytes 9220
  0.7 17.2 %copy-start.4 = (s32[512]{0:T(512)S(1)}, s32[512]{0:T(512)}, u32[]{:S(2)}) copy-start(s32[512]{0:T(512)} %param.7) | copy-start | bytes 6148
  3.5 24.7 %all-to-all-start = ((bf16[16,16,1024]{2,1,0:T(8,128)(2,1)}), bf16[16,16,1024]{2,1,0:T(8,128)(2,1)S(1)}, u32[]{:S(2)}, u32[]{:S(2)}) async-start(bf16[16,16,1024]{2,1,0:T(8,128)(2,1)} %get-tuple-element.24), calls=%async_computation | async-start | bytes 1048576 | tf_op jit(solution)/shard_map/all_to_all | solution.py:201
  12.5 6.5 %collective-permute-start = (bf16[1024,768]{1,0:T(8,128)(2,1)S(1)}, bf16[1024,768]{1,0:T(8,128)(2,1)}, u32[]{:S(2)}, u32[]{:S(2)}) collective-permute-start(bf16[1024,768]{1,0:T(8,128)(2,1)S(1)} %bitcast.35), channel_id=1, source_target_pairs={{0,1},{1,0},{2,3},{3,2},{4,5},{5,4},{6,7},{7,6},{8,9},{9,8},{10,11... | collective-permute-start | bytes 4718600 | tf_op jit(solution)/shard_map/ppermute | solution.py:210
  15.9 3.1 %collective-permute-start.1 = (f32[768]{0:T(1024)S(1)}, f32[768]{0:T(1024)S(1)}, u32[]{:S(2)}, u32[]{:S(2)}) collective-permute-start(f32[768]{0:T(1024)S(1)} %reduce.3), channel_id=1, source_target_pairs={{0,1},{1,0},{2,3},{3,2},{4,5},{5,4},{6,7},{7,6},{8,9},{9,8},{10,11... | collective-permute-start | bytes 9224 | tf_op jit(solution)/shard_map/ppermute | solution.py:211
  30.7 10.7 %copy-start.2 = (f32[256,1536]{1,0:T(8,128)}, f32[256,1536]{1,0:T(8,128)S(1)}, u32[]{:S(2)}) copy-start(f32[256,1536]{1,0:T(8,128)S(1)} %get-tuple-element.52) | copy-start | bytes 4718596
  42.1 28.6 %all-to-all-start.2 = ((f32[16,1,256]{2,1,0:T(1,128)}), f32[16,1,256]{2,1,0:T(1,128)S(1)}, u32[]{:S(2)}, u32[]{:S(2)}) async-start(f32[16,1,256]{2,1,0:T(1,128)} %broadcast_in_dim.18), calls=%async_computation.2 | async-start | bytes 32768 | tf_op jit(solution)/shard_map/all_to_all | solution.py:244
  57.1 2.0 %copy-start.6 = (bf16[1,1024,768]{2,1,0:T(8,128)(2,1)S(1)}, bf16[1,1024,768]{2,1,0:T(8,128)(2,1)}, u32[]{:S(2)}) copy-start(bf16[1,1024,768]{2,1,0:T(8,128)(2,1)} %param.10) | copy-start | bytes 4718596
  71.7 21.2 %all-to-all-start.3 = ((bf16[16,16,1280]{2,1,0:T(8,128)(2,1)}), bf16[16,16,1280]{2,1,0:T(8,128)(2,1)S(1)}, u32[]{:S(2)}, u32[]{:S(2)}) async-start(bf16[16,16,1280]{2,1,0:T(8,128)(2,1)} %get-tuple-element.27), calls=%async_computation.3 | async-start | bytes 1310720 | tf_op jit(solution)/shard_map/all_to_all | solution.py:201
  77.3 9.2 %collective-permute-start.2 = (bf16[1024,768]{1,0:T(8,128)(2,1)}, bf16[1024,768]{1,0:T(8,128)(2,1)}, u32[]{:S(2)}, u32[]{:S(2)}) collective-permute-start(bf16[1024,768]{1,0:T(8,128)(2,1)} %convolution_convert_fusion), channel_id=1, source_target_pairs={{0,1},{1,0},{2,3},{3,2},{4,5},{5,4},{6,7},{7,6},{8,9},{9,8},{10,11... | collective-permute-start | bytes 4718600 | tf_op jit(solution)/shard_map/ppermute | solution.py:270

commit v5 on v3

--- a/solution.py
+++ b/solution.py
@@ -95,20 +95,27 @@
     )(logp_all, label_logp, partial, act, chunks)
 
 
-def close_kernel(_, pieces_ref, scale_ref, normed_ref, inverse_ref, gain_ref, grad_ref):
+def close_kernel(
+    _, pieces_ref, scale_ref, normed_ref, inverse_ref, gain_ref, shift_ref, sums_ref, *outs
+):
+    grad_ref, grad_gain_ref, grad_shift_ref = outs
     received = pieces_ref[0].astype(jnp.float32)
     for k in range(1, pieces_ref.shape[0]):
         received = received + pieces_ref[k].astype(jnp.float32)
     normed = normed_ref[...]
-    scaled = scale_ref[:, :1] * received * gain_ref[...]
+    gain = gain_ref[...]
+    scaled = scale_ref[:, :1] * received * gain
     grad_ref[...] = inverse_ref[:, :1] * (
         scaled
         - jnp.mean(scaled, axis=-1, keepdims=True)
         - normed * jnp.mean(scaled * normed, axis=-1, keepdims=True)
     )
-
-
-def close_images(chip, pieces, scale, normed, inverse, gain_row):
+    sums = sums_ref[0] + sums_ref[1]
+    grad_shift_ref[...] = sums[:1]
+    grad_gain_ref[...] = (sums[1:] - shift_ref[...] * sums[:1]) / gain
+
+
+def close_images(chip, pieces, scale, normed, inverse, gain_row, shift_row, sums):
     images, channels = normed.shape
     whole = lambda *shape: pl.BlockSpec(shape, lambda i, chip: (0,) * len(shape))
     return pl.pallas_call(
@@ -122,15 +129,18 @@
                 whole(images, channels),
                 whole(images, 128),
                 whole(1, channels),
+                whole(1, channels),
+                whole(*sums.shape),
             ],
-            out_specs=whole(images, channels),
+            out_specs=[whole(images, channels), whole(1, channels), whole(1, channels)],
         ),
-        out_shape=jax.ShapeDtypeStruct((images, channels), jnp.float32),
-        cost_estimate=pl.CostEstimate(
-            flops=40 * images * channels, bytes_accessed=2**20, transcendentals=0
-        ),
+        out_shape=[
+            jax.ShapeDtypeStruct((images, channels), jnp.float32),
+            jax.ShapeDtypeStruct((1, channels), jnp.float32),
+            jax.ShapeDtypeStruct((1, channels), jnp.float32),
+        ],
         compiler_params=pltpu.CompilerParams(vmem_limit_bytes=16 * 2**20),
-    )(jnp.reshape(chip, (1,)), pieces, scale, normed, inverse, gain_row)
+    )(jnp.reshape(chip, (1,)), pieces, scale, normed, inverse, gain_row, shift_row, sums)
 
 
 def sum_tails_kernel(tails_ref, sums_ref):
@@ -231,42 +241,43 @@
     )
     pieces = over_plane(chunks)
 
-    grad_logits = scale[:, :1] * diff
-    grad_sum = jnp.sum(grad_logits, axis=0)
-    note = jnp.concatenate([log_joint[0], grad_sum[classes_here:]])
-    note = lax.ppermute(note, "dp", swap)
-    mean_loss = math.log(members) - (
-        jnp.sum(log_joint) + jnp.sum(note[:plane_images])
-    ) / (2 * plane_images)
-    grad_head_bias = grad_sum[:classes_here] + note[plane_images:]
     rows = (((0,), (0,)), ((), ()))
-    grad_low = grad_logits.astype(jnp.bfloat16)
+    grad_other = scale[:, :1] * diff[:, classes_here:]
+    bias_other_part = jnp.sum(grad_other, axis=0)
     for_other = lax.dot_general(
-        act_plane, grad_low[:, classes_here:], rows, preferred_element_type=jnp.float32
+        act_plane, grad_other.astype(jnp.bfloat16), rows, preferred_element_type=jnp.float32
     ).astype(jnp.bfloat16)
     from_other = lax.ppermute(for_other, "dp", swap)
+    grad_mine = scale[:, :1] * diff[:, :classes_here]
+    bias_part = jnp.sum(grad_mine, axis=0)
     grad_head_weight = (
         lax.dot_general(
-            act_plane, grad_low[:, :classes_here], rows, preferred_element_type=jnp.float32
+            act_plane, grad_mine.astype(jnp.bfloat16), rows, preferred_element_type=jnp.float32
         )
         + from_other.astype(jnp.float32)
-    ).astype(jnp.bfloat16)
-
+    ).astype(jnp.bfloat16)[None]
+
+    note = jnp.concatenate([log_joint[0], bias_other_part])
+    note = lax.ppermute(note, "dp", swap)
+    mean_loss = math.log(members) - jnp.sum(log_joint[0] + note[:plane_images]) / (
+        2 * plane_images
+    )
+    grad_head_bias = (bias_part + note[plane_images:])[None]
     pieces, grad_head_weight, grad_head_bias, mean_loss = lax.optimization_barrier(
         (pieces, grad_head_weight, grad_head_bias, mean_loss)
     )
-    sums = sum_tails(pieces, channels)
-    grad_pooled = close_images(position // 2, pieces, scale, normed, inverse, norm_gain)
-    sums = sums + lax.ppermute(sums, "dp", swap)
-    grad_shift = sums[0]
-    grad_gain = (sums[1] - shift_row * grad_shift) / gain_row
+    pairs = [[2 * chip, 2 * chip + 1] for chip in range(chips)]
+    sums = lax.all_gather(sum_tails(pieces, channels), "dp", axis_index_groups=pairs)
+    grad_pooled, grad_gain, grad_shift = close_images(
+        position // 2, pieces, scale, normed, inverse, norm_gain, norm_bias, sums
+    )
     return (
         mean_loss,
         grad_pooled[None],
-        grad_gain[None],
-        grad_shift[None],
-        grad_head_weight[None],
-        grad_head_bias[None],
+        grad_gain,
+        grad_shift,
+        grad_head_weight,
+        grad_head_bias,
     )
 
 

time: 102 us -> 99.7 us (0.977)
  starting transfers between devices: 45.1 us -> 40.6 us
  blocking collectives: 10.1 us -> 14.2 us
    ppermute x1 -> x0, starting transfers between devices: 4.5 us -> none  [per_device(): sums = sums + lax.ppermute(sums, 'dp', swap)]
    all_gather x0 -> x1, blocking collectives: none -> 4.08 us  [per_device(): lax.all_gather(sum_tails(pieces, channels), 'dp', axis_index_groups=pairs)]
    all_to_all x1, waiting for transfers between devices: 9.86 us -> 8.34 us  [per_device(): lax.all_to_all(jnp.broadcast_to(label_logp[None], (members, plane_images)...]
    sub x1, other arithmetic: 0.44 us -> 1.95 us  [per_device(): diff = jnp.exp(logits - log_total[:, None]) - onehot.astype(jnp.float32)]
    reduce_sum x3 -> x2, other arithmetic: 2.29 us -> 0.78 us  [the longest x1 0.6 us: per_device(): jnp.sum(log_joint[0] + note[:plane_images]) / (2 * plane_images)]
  transfers between devices with their start and end apart: 8 -> 7, of which waited for: 5 -> 5; matrix products, arithmetic and copies ran while one was open for 12% -> 12% of each run, Pallas kernels for 1% -> 0%
where the time goes in v5:
time: 99.7 us; the launch traced here: 99 us
  starting transfers between devices  40.6 us (41%)
  waiting for transfers between devices  21.1 us (21%)
  blocking collectives  14.2 us (14%)
  matrix products  10 us (10%)
  other arithmetic  5.17 us (5%)
  Pallas kernels  2.9 us (3%)
  between operations  2.72 us (3%)
  local copies, waits for them, and re-layouts  2.45 us (2%)
    all_to_all x1, starting transfers between devices, per_device(): lax.all_to_all(jnp.broadcast_to(label_logp[None], (members, plane_images)...  15 us
    all_to_all x2, starting transfers between devices, over_plane(): return lax.all_to_all(x, 'dp', 0, 0, axis_index_groups=planes)  12.6 us
    all_to_all x2, waiting for transfers between devices, over_plane(): return lax.all_to_all(x, 'dp', 0, 0, axis_index_groups=planes)  10.7 us
    all_to_all x1, blocking collectives, over_plane(): return lax.all_to_all(x, 'dp', 0, 0, axis_index_groups=planes)  10.1 us
    all_to_all x1, waiting for transfers between devices, per_device(): lax.all_to_all(jnp.broadcast_to(label_logp[None], (members, plane_images)...  8.34 us
    ppermute x1, starting transfers between devices, per_device(): from_other = lax.ppermute(for_other, 'dp', swap)  5.81 us
    all_gather x1, blocking collectives, per_device(): lax.all_gather(sum_tails(pieces, channels), 'dp', axis_index_groups=pairs)  4.08 us
    ppermute x1, starting transfers between devices, per_device(): weight_other = lax.ppermute(weight, 'dp', swap)  3.35 us
  transfers between devices with their start and end apart: 7, of which 5 were waited for; matrix products, arithmetic and copies ran while one was open for 12% of the time, Pallas kernels for 0%

profile of v5, /device:TPU:1, one launch (start us, length us, event | category | flops | bytes accessed | tf_op | source)
XLA Modules:
  0.0 99.0 jit_solution(280881388656093749)
XLA Ops:
  0.6 0.0 copy-start
  0.6 0.0 copy-start.1
  0.7 0.0 copy-start.5
  0.7 0.0 copy-start.3
  0.7 0.0 copy-start.4
  0.7 1.8 %convert_reduce_fusion.total_ref = f32[16,1024]{1,0:T(8,128)S(1)} fusion(bf16[1,16,49,1024]{3,1,2,0:T(8,128)(2,1)} %param.6), kind=kLoop, calls=%fused_computation | loop fusion | flops 1589248 | bytes 1671168 | tf_op jit(solution)/shard_map/reduce_sum | solution.py:194
  2.5 0.0 copy-done
  2.5 0.0 copy-done.1
  2.5 1.0 %shard_map.109 = (f32[16,1024]{1,0:T(8,128)S(1)}, f32[16,128]{1,0:T(8,128)S(1)}, bf16[16,16,1024]{2,1,0:T(8,128)(2,1)}) custom-call(f32[16,1024]{1,0:T(8,128)S(1)} %convert_reduce_fusion.total_ref, f32[1,1024]{1,0:T(1,128)S(1)} %copy-done, f32[1,1024]{1,0:T(1,128)S(1)} %copy-done.1), custom_call_target="tpu_custom_call" | custom-call | tf_op jit(solution)/shard_map/pallas_call | solution.py:29
  3.5 9.0 %all-to-all-start = ((bf16[16,16,1024]{2,1,0:T(8,128)(2,1)}), bf16[16,16,1024]{2,1,0:T(8,128)(2,1)S(1)}, u32[]{:S(2)}, u32[]{:S(2)}) async-start(bf16[16,16,1024]{2,1,0:T(8,128)(2,1)} %get-tuple-element.22), calls=%async_computation | async-start | bytes 1048576 | tf_op jit(solution)/shard_map/all_to_all | solution.py:181
  12.5 0.0 copy-done.5
  12.5 3.3 %collective-permute-start = (bf16[1024,768]{1,0:T(8,128)(2,1)S(1)}, bf16[1024,768]{1,0:T(8,128)(2,1)}, u32[]{:S(2)}, u32[]{:S(2)}) collective-permute-start(bf16[1024,768]{1,0:T(8,128)(2,1)S(1)} %bitcast.36), channel_id=1, source_target_pairs={{0,1},{1,0},{2,3},{3,2},{4,5},{5,4},{6,7},{7,6},{8,9},{9,8},{10,11... | collective-permute-start | bytes 4718600 | tf_op jit(solution)/shard_map/ppermute | solution.py:190
  15.9 0.0 copy-done.3
  15.9 1.9 %collective-permute-start.1 = (f32[768]{0:T(1024)S(1)}, f32[768]{0:T(1024)S(1)}, u32[]{:S(2)}, u32[]{:S(2)}) collective-permute-start(f32[768]{0:T(1024)S(1)} %reduce.3), channel_id=1, source_target_pairs={{0,1},{1,0},{2,3},{3,2},{4,5},{5,4},{6,7},{7,6},{8,9},{9,8},{10,11... | collective-permute-start | bytes 9224 | tf_op jit(solution)/shard_map/ppermute | solution.py:191
  17.9 0.0 copy-done.4
  17.9 0.1 reshape.85
  18.0 0.1 eq.15
  18.1 0.9 collective-permute-done.1
  19.0 0.0 collective-permute-done
  19.0 9.2 %all-to-all-done = bf16[16,16,1024]{2,1,0:T(8,128)(2,1)S(1)} async-done(((bf16[16,16,1024]{2,1,0:T(8,128)(2,1)}), bf16[16,16,1024]{2,1,0:T(8,128)(2,1)S(1)}, u32[]{:S(2)}, u32[]{:S(2)}) %all-to-all-start) | async-done | bytes 524320 | tf_op jit(solution)/shard_map/all_to_all | solution.py:181
  28.2 2.5 %fusion.21 = (f32[256]{0:T(256)S(1)}, f32[256,1536]{1,0:T(8,128)S(1)}) fusion(f32[1536]{0:T(1024)S(1)} %pad_maximum_fusion.3, bf16[256,1024]{1,0:T(8,128)(2,1)S(1)} %bitcast.24, bf16[1024,768]{1,0:T(8,128)(2,1)} %collective-permute-done, bf16[1024,768]{1,0:T(8,128)(2,1)S(1)} %bitcast.37), kind=kOutput, calls=%fused_computation.43 | convolution fusion | flops 812384000 | bytes 5250048 | tf_op jit(solution)/shard_map/dot_general | solution.py:213
  30.7 0.0 copy-start.2
  30.7 0.5 exponential_reduce_fusion
  31.3 10.1 %all_to_all.23 = f32[16,2,256]{2,1,0:T(2,128)S(1)} all-to-all(f32[16,2,256]{2,1,0:T(2,128)S(1)} %broadcast_in_dim.15), channel_id=1, replica_groups={{0,2,4,6,8,10,12,14,16,18,20,22,24,26,28,30},{1,3,5,7,9,11,13,15,17,19,..., dimensions={0} | all-to-all | bytes 65536 | tf_op jit(solution)/shard_map/all_to_all | solution.py:181
  41.4 0.1 slice_reduce_fusion.2
  41.4 0.0 copy-done.2
  41.5 0.6 broadcast_in_dim.16
  42.1 15.0 %all-to-all-start.2 = ((f32[16,1,256]{2,1,0:T(1,128)}), f32[16,1,256]{2,1,0:T(1,128)S(1)}, u32[]{:S(2)}, u32[]{:S(2)}) async-start(f32[16,1,256]{2,1,0:T(1,128)} %broadcast_in_dim.16), calls=%async_computation.2 | async-start | bytes 32768 | tf_op jit(solution)/shard_map/all_to_all | solution.py:224
  57.1 0.0 copy-start.6
  57.1 2.0 %fusion.2 = f32[256,1536]{1,0:T(8,128)S(1)} fusion(f32[256,1536]{1,0:T(8,128)} %copy-done.2, f32[256]{0:T(256)S(1)} %get-tuple-element.45, s32[1536]{0:T(1024)S(1)} %pad_add_fusion, s32[256]{0:T(256)S(1)} %eq.15), kind=kLoop, calls=%fused_computation.9 | loop fusion | flops 1572864 | bytes 3153920 | tf_op jit(solution)/shard_map/sub | solution.py:228
  59.0 0.0 copy-done.6
  59.0 2.4 %fusion.22 = (bf16[256,1024]{1,0:T(8,128)(2,1)S(1)}, f32[256,1024]{1,0:T(8,128)S(1)}) fusion(bf16[1024,768]{1,0:T(8,128)(2,1)} %collective-permute-done, bf16[1024,768]{1,0:T(8,128)(2,1)S(1)} %bitcast.38, f32[256,1536]{1,0:T(8,128)S(1)} %fusion.2), kind=kOutput, calls=%fused_computation.44 | convolution fusion | flops 812253184 | bytes 6291456 | tf_op jit(solution)/shard_map/dot_general | solution.py:230
  61.5 0.9 pad.4._
  62.4 8.3 %all-to-all-done.2 = f32[16,1,256]{2,1,0:T(1,128)S(1)} async-done(((f32[16,1,256]{2,1,0:T(1,128)}), f32[16,1,256]{2,1,0:T(1,128)S(1)}, u32[]{:S(2)}, u32[]{:S(2)}) %all-to-all-start.2) | async-done | bytes 16416 | tf_op jit(solution)/shard_map/all_to_all | solution.py:224
  70.7 1.0 %shard_map.110 = (f32[256,128]{1,0:T(8,128)S(1)}, f32[1,256]{1,0:T(1,128)S(1)}, bf16[16,16,1280]{2,1,0:T(8,128)(2,1)}) custom-call(f32[16,256]{1,0:T(8,128)S(1)} %bitcast.28, f32[1,256]{1,0:T(1,128)S(1)} %bitcast.30, f32[256,1024]{1,0:T(8,128)S(1)} %get-tuple-element.23.partial_ref, bf16[256,1024]{1,0:T(8,128)(2,1)S(1)} %bitcast.25, ...), custom_call_target="tpu_custom_call", output_to_operand_aliasing={{2}: (4, {})} | custom-call | tf_op jit(solution)/shard_map/pallas_call | solution.py:73
  71.7 3.6 %all-to-all-start.3 = ((bf16[16,16,1280]{2,1,0:T(8,128)(2,1)}), bf16[16,16,1280]{2,1,0:T(8,128)(2,1)S(1)}, u32[]{:S(2)}, u32[]{:S(2)}) async-start(bf16[16,16,1280]{2,1,0:T(8,128)(2,1)} %get-tuple-element.25), calls=%async_computation.3 | async-start | bytes 1310720 | tf_op jit(solution)/shard_map/all_to_all | solution.py:181
  75.3 0.1 slice_reduce_fusion
  75.5 1.8 %convolution_convert_fusion = bf16[1024,768]{1,0:T(8,128)(2,1)} fusion(bf16[256,1024]{1,0:T(8,128)(2,1)S(1)} %bitcast.26, f32[256,1536]{1,0:T(8,128)S(1)} %fusion.2, f32[256]{0:T(256)S(1)} %slice_reduce_fusion), kind=kOutput, calls=%fused_computation.7 | convolution fusion | flops 403832832 | bytes 2884608 | tf_op jit(solution)/shard_map/dot_general | solution.py:247
  77.3 5.8 %collective-permute-start.2 = (bf16[1024,768]{1,0:T(8,128)(2,1)}, bf16[1024,768]{1,0:T(8,128)(2,1)}, u32[]{:S(2)}, u32[]{:S(2)}) collective-permute-start(bf16[1024,768]{1,0:T(8,128)(2,1)} %convolution_convert_fusion), channel_id=1, source_target_pairs={{0,1},{1,0},{2,3},{3,2},{4,5},{5,4},{6,7},{7,6},{8,9},{9,8},{10,11... | collective-permute-start | bytes 4718600 | tf_op jit(solution)/shard_map/ppermute | solution.py:250
  83.1 0.2 fusion.7
  83.3 1.9 %collective-permute-start.3 = (f32[1024]{0:T(1024)S(1)}, f32[1024]{0:T(1024)S(1)}, u32[]{:S(2)}, u32[]{:S(2)}) collective-permute-start(f32[1024]{0:T(1024)S(1)} %pad_maximum_fusion.4), channel_id=1, source_target_pairs={{0,1},{1,0},{2,3},{3,2},{4,5},{5,4},{6,7},{7,6},{8,9},{9,8},{10,11... | collective-permute-start | bytes 12296 | tf_op jit(solution)/shard_map/ppermute | solution.py:261
  85.3 1.1 %collective-permute-done.3 = f32[1024]{0:T(1024)S(1)} collective-permute-done((f32[1024]{0:T(1024)S(1)}, f32[1024]{0:T(1024)S(1)}, u32[]{:S(2)}, u32[]{:S(2)}) %collective-permute-start.3) | collective-permute-done | bytes 4128 | tf_op jit(solution)/shard_map/ppermute | solution.py:261
  86.4 0.6 broadcast_in_dim.18
  87.0 0.6 add_reduce_fusion
  88.2 0.0 collective-permute-done.2
  88.2 3.2 %fusion.3 = bf16[1,1024,768]{2,1,0:T(8,128)(2,1)} fusion(bf16[1024,768]{1,0:T(8,128)(2,1)} %collective-permute-done.2, bf16[256,1024]{1,0:T(8,128)(2,1)S(1)} %bitcast.27, f32[256,1536]{1,0:T(8,128)S(1)} %fusion.2, f32[256]{0:T(256)S(1)} %slice_reduce_fusion), kind=kOutput, calls=%fused_computation.10 | convolution fusion | flops 405405696 | bytes 4457472 | tf_op jit(solution)/shard_map/dot_general | solution.py:254
  91.5 1.5 %all-to-all-done.3.tails_ref.pieces_ref = bf16[16,16,1280]{2,1,0:T(8,128)(2,1)S(1)} async-done(((bf16[16,16,1280]{2,1,0:T(8,128)(2,1)}), bf16[16,16,1280]{2,1,0:T(8,128)(2,1)S(1)}, u32[]{:S(2)}, u32[]{:S(2)}) %all-to-all-start.3) | async-done | bytes 655392 | tf_op jit(solution)/shard_map/all_to_all | solution.py:181
  93.0 4.1 %all-gather.1.sums_ref = f32[2,2,1024]{2,1,0:T(2,128)S(1)} all-gather(f32[1,2,1024]{2,1,0:T(2,128)S(1)} %bitcast.29), channel_id=2, replica_groups={{0,1},{2,3},{4,5},{6,7},{8,9},{10,11},{12,13},{14,15},{16,17},{18,19},{..., dimensions={0}, use_global_device_ids=true | all-gather | bytes 24576 | tf_op jit(solution)/shard_map/all_gather | solution.py:270
  97.1 0.8 shard_map.112
  (14 shorter events, 0.2 us)
Async XLA Ops:
  0.6 1.8 %copy-start = (f32[1,1024]{1,0:T(1,128)S(1)}, f32[1,1024]{1,0:T(1,128)}, u32[]{:S(2)}) copy-start(f32[1,1024]{1,0:T(1,128)} %gain_ref.3) | copy-start | bytes 12292
  0.6 1.8 %copy-start.1 = (f32[1,1024]{1,0:T(1,128)S(1)}, f32[1,1024]{1,0:T(1,128)}, u32[]{:S(2)}) copy-start(f32[1,1024]{1,0:T(1,128)} %shift_ref.3) | copy-start | bytes 12292
  0.7 11.9 %copy-start.5 = (bf16[1,1024,768]{2,1,0:T(8,128)(2,1)S(1)}, bf16[1,1024,768]{2,1,0:T(8,128)(2,1)}, u32[]{:S(2)}) copy-start(bf16[1,1024,768]{2,1,0:T(8,128)(2,1)} %param.10) | copy-start | bytes 4718596
  0.7 15.2 %copy-start.3 = (f32[1,768]{1,0:T(1,128)S(1)}, f32[1,768]{1,0:T(1,128)}, u32[]{:S(2)}) copy-start(f32[1,768]{1,0:T(1,128)} %param.11) | copy-start | bytes 9220
  0.7 17.2 %copy-start.4 = (s32[512]{0:T(512)S(1)}, s32[512]{0:T(512)}, u32[]{:S(2)}) copy-start(s32[512]{0:T(512)} %param.7) | copy-start | bytes 6148
  3.5 24.7 %all-to-all-start = ((bf16[16,16,1024]{2,1,0:T(8,128)(2,1)}), bf16[16,16,1024]{2,1,0:T(8,128)(2,1)S(1)}, u32[]{:S(2)}, u32[]{:S(2)}) async-start(bf16[16,16,1024]{2,1,0:T(8,128)(2,1)} %get-tuple-element.22), calls=%async_computation | async-start | bytes 1048576 | tf_op jit(solution)/shard_map/all_to_all | solution.py:181
  12.5 6.5 %collective-permute-start = (bf16[1024,768]{1,0:T(8,128)(2,1)S(1)}, bf16[1024,768]{1,0:T(8,128)(2,1)}, u32[]{:S(2)}, u32[]{:S(2)}) collective-permute-start(bf16[1024,768]{1,0:T(8,128)(2,1)S(1)} %bitcast.36), channel_id=1, source_target_pairs={{0,1},{1,0},{2,3},{3,2},{4,5},{5,4},{6,7},{7,6},{8,9},{9,8},{10,11... | collective-permute-start | bytes 4718600 | tf_op jit(solution)/shard_map/ppermute | solution.py:190
  15.9 3.1 %collective-permute-start.1 = (f32[768]{0:T(1024)S(1)}, f32[768]{0:T(1024)S(1)}, u32[]{:S(2)}, u32[]{:S(2)}) collective-permute-start(f32[768]{0:T(1024)S(1)} %reduce.3), channel_id=1, source_target_pairs={{0,1},{1,0},{2,3},{3,2},{4,5},{5,4},{6,7},{7,6},{8,9},{9,8},{10,11... | collective-permute-start | bytes 9224 | tf_op jit(solution)/shard_map/ppermute | solution.py:191
  30.7 10.7 %copy-start.2 = (f32[256,1536]{1,0:T(8,128)}, f32[256,1536]{1,0:T(8,128)S(1)}, u32[]{:S(2)}) copy-start(f32[256,1536]{1,0:T(8,128)S(1)} %get-tuple-element.48) | copy-start | bytes 4718596
  42.1 28.6 %all-to-all-start.2 = ((f32[16,1,256]{2,1,0:T(1,128)}), f32[16,1,256]{2,1,0:T(1,128)S(1)}, u32[]{:S(2)}, u32[]{:S(2)}) async-start(f32[16,1,256]{2,1,0:T(1,128)} %broadcast_in_dim.16), calls=%async_computation.2 | async-start | bytes 32768 | tf_op jit(solution)/shard_map/all_to_all | solution.py:224
  57.1 2.0 %copy-start.6 = (bf16[1,1024,768]{2,1,0:T(8,128)(2,1)S(1)}, bf16[1,1024,768]{2,1,0:T(8,128)(2,1)}, u32[]{:S(2)}) copy-start(bf16[1,1024,768]{2,1,0:T(8,128)(2,1)} %param.10) | copy-start | bytes 4718596
  71.7 21.2 %all-to-all-start.3 = ((bf16[16,16,1280]{2,1,0:T(8,128)(2,1)}), bf16[16,16,1280]{2,1,0:T(8,128)(2,1)S(1)}, u32[]{:S(2)}, u32[]{:S(2)}) async-start(bf16[16,16,1280]{2,1,0:T(8,128)(2,1)} %get-tuple-element.25), calls=%async_computation.3 | async-start | bytes 1310720 | tf_op jit(solution)/shard_map/all_to_all | solution.py:181
  77.3 10.9 %collective-permute-start.2 = (bf16[1024,768]{1,0:T(8,128)(2,1)}, bf16[1024,768]{1,0:T(8,128)(2,1)}, u32[]{:S(2)}, u32[]{:S(2)}) collective-permute-start(bf16[1024,768]{1,0:T(8,128)(2,1)} %convolution_convert_fusion), channel_id=1, source_target_pairs={{0,1},{1,0},{2,3},{3,2},{4,5},{5,4},{6,7},{7,6},{8,9},{9,8},{10,11... | collective-permute-start | bytes 4718600 | tf_op jit(solution)/shard_map/ppermute | solution.py:250
  83.3 3.1 %collective-permute-start.3 = (f32[1024]{0:T(1024)S(1)}, f32[1024]{0:T(1024)S(1)}, u32[]{:S(2)}, u32[]{:S(2)}) collective-permute-start(f32[1024]{0:T(1024)S(1)} %pad_maximum_fusion.4), channel_id=1, source_target_pairs={{0,1},{1,0},{2,3},{3,2},{4,5},{5,4},{6,7},{7,6},{8,9},{9,8},{10,11... | collective-permute-start | bytes 12296 | tf_op jit(solution)/shard_map/ppermute | solution.py:261

commit v6 on v5

--- a/solution.py
+++ b/solution.py
@@ -58,10 +58,8 @@
         jnp.sum(scaled, axis=0, keepdims=True),
         jnp.sum(scaled * act_ref[...].astype(jnp.float32), axis=0, keepdims=True),
     ]
-    high = [x.astype(jnp.bfloat16).astype(jnp.float32) for x in sums]
-    low = [x - h for x, h in zip(sums, high)]
     width = tail_ref.shape[2]
-    lines = [x[:, k : k + width] for x in high + low for k in range(0, x.shape[1], width)]
+    lines = [x[:, k : k + width] for x in sums for k in range(0, x.shape[1], width)]
     tail = jnp.concatenate(lines, axis=0).astype(jnp.bfloat16)
     tail_ref[...] = jnp.broadcast_to(tail[None], tail_ref.shape)
 
@@ -148,8 +146,7 @@
     for k in range(1, tails_ref.shape[0]):
         tail = tail + tails_ref[k].astype(jnp.float32)
     lines, width = tail.shape
-    half, quarter = lines // 2, lines // 4
-    tail = tail[:half] + tail[half:]
+    quarter = lines // 2
     for r in range(2):
         for k in range(quarter):
             sums_ref[r : r + 1, k * width : (k + 1) * width] = tail[r * quarter + k][None]
@@ -230,7 +227,7 @@
     partial = lax.dot_general(
         low, weight_both, (((1,), (1,)), ((), ())), preferred_element_type=jnp.float32
     )
-    tail_columns = 4 * channels // images_here
+    tail_columns = 2 * channels // images_here
     chunks = jnp.pad(
         partial.astype(jnp.bfloat16).reshape(chips, images_here, channels),
         ((0, 0), (0, 0), (0, tail_columns)),

time: 99.7 us -> 98.2 us (0.985)
  waiting for transfers between devices: 21.1 us -> 19.6 us
    all_to_all x2, waiting for transfers between devices: 10.7 us -> 9.19 us  [over_plane(): return lax.all_to_all(x, 'dp', 0, 0, axis_index_groups=planes)]
  transfers between devices with their start and end apart: 7 -> 7, of which waited for: 5 -> 4; matrix products, arithmetic and copies ran while one was open for 12% -> 12% of each run, Pallas kernels for 0% -> 0%
where the time goes in v6:
time: 98.2 us; the launch traced here: 97.6 us
  starting transfers between devices  40.6 us (41%)
  waiting for transfers between devices  19.6 us (20%)
  blocking collectives  14.3 us (15%)
  matrix products  10 us (10%)
  other arithmetic  5.17 us (5%)
  Pallas kernels  2.89 us (3%)
  between operations  2.71 us (3%)
  local copies, waits for them, and re-layouts  2.41 us (2%)
    all_to_all x1, starting transfers between devices, per_device(): lax.all_to_all(jnp.broadcast_to(label_logp[None], (members, plane_images)...  15 us
    all_to_all x2, starting transfers between devices, over_plane(): return lax.all_to_all(x, 'dp', 0, 0, axis_index_groups=planes)  12.6 us
    all_to_all x1, blocking collectives, over_plane(): return lax.all_to_all(x, 'dp', 0, 0, axis_index_groups=planes)  10.1 us
    all_to_all x2, waiting for transfers between devices, over_plane(): return lax.all_to_all(x, 'dp', 0, 0, axis_index_groups=planes)  9.19 us
    all_to_all x1, waiting for transfers between devices, per_device(): lax.all_to_all(jnp.broadcast_to(label_logp[None], (members, plane_images)...  8.38 us
    ppermute x1, starting transfers between devices, per_device(): from_other = lax.ppermute(for_other, 'dp', swap)  5.81 us
    all_gather x1, blocking collectives, per_device(): lax.all_gather(sum_tails(pieces, channels), 'dp', axis_index_groups=pairs)  4.18 us
    ppermute x1, starting transfers between devices, per_device(): weight_other = lax.ppermute(weight, 'dp', swap)  3.35 us
  transfers between devices with their start and end apart: 7, of which 4 were waited for; matrix products, arithmetic and copies ran while one was open for 12% of the time, Pallas kernels for 0%

profile of v6, /device:TPU:1, one launch (start us, length us, event | category | flops | bytes accessed | tf_op | source)
XLA Modules:
  0.0 97.6 jit_solution(1961772236574358824)
XLA Ops:
  0.6 0.0 copy-start
  0.6 0.0 copy-start.1
  0.7 0.0 copy-start.5
  0.7 0.0 copy-start.3
  0.7 0.0 copy-start.4
  0.7 1.8 %convert_reduce_fusion.total_ref = f32[16,1024]{1,0:T(8,128)S(1)} fusion(bf16[1,16,49,1024]{3,1,2,0:T(8,128)(2,1)} %param.6), kind=kLoop, calls=%fused_computation | loop fusion | flops 1589248 | bytes 1671168 | tf_op jit(solution)/shard_map/reduce_sum | solution.py:191
  2.5 0.0 copy-done
  2.5 0.0 copy-done.1
  2.5 1.0 %shard_map.109 = (f32[16,1024]{1,0:T(8,128)S(1)}, f32[16,128]{1,0:T(8,128)S(1)}, bf16[16,16,1024]{2,1,0:T(8,128)(2,1)}) custom-call(f32[16,1024]{1,0:T(8,128)S(1)} %convert_reduce_fusion.total_ref, f32[1,1024]{1,0:T(1,128)S(1)} %copy-done, f32[1,1024]{1,0:T(1,128)S(1)} %copy-done.1), custom_call_target="tpu_custom_call" | custom-call | tf_op jit(solution)/shard_map/pallas_call | solution.py:29
  3.5 9.0 %all-to-all-start = ((bf16[16,16,1024]{2,1,0:T(8,128)(2,1)}), bf16[16,16,1024]{2,1,0:T(8,128)(2,1)S(1)}, u32[]{:S(2)}, u32[]{:S(2)}) async-start(bf16[16,16,1024]{2,1,0:T(8,128)(2,1)} %get-tuple-element.22), calls=%async_computation | async-start | bytes 1048576 | tf_op jit(solution)/shard_map/all_to_all | solution.py:178
  12.5 0.0 copy-done.5
  12.5 3.3 %collective-permute-start = (bf16[1024,768]{1,0:T(8,128)(2,1)S(1)}, bf16[1024,768]{1,0:T(8,128)(2,1)}, u32[]{:S(2)}, u32[]{:S(2)}) collective-permute-start(bf16[1024,768]{1,0:T(8,128)(2,1)S(1)} %bitcast.36), channel_id=1, source_target_pairs={{0,1},{1,0},{2,3},{3,2},{4,5},{5,4},{6,7},{7,6},{8,9},{9,8},{10,11... | collective-permute-start | bytes 4718600 | tf_op jit(solution)/shard_map/ppermute | solution.py:187
  15.9 0.0 copy-done.3
  15.9 1.9 %collective-permute-start.1 = (f32[768]{0:T(1024)S(1)}, f32[768]{0:T(1024)S(1)}, u32[]{:S(2)}, u32[]{:S(2)}) collective-permute-start(f32[768]{0:T(1024)S(1)} %reduce.3), channel_id=1, source_target_pairs={{0,1},{1,0},{2,3},{3,2},{4,5},{5,4},{6,7},{7,6},{8,9},{9,8},{10,11... | collective-permute-start | bytes 9224 | tf_op jit(solution)/shard_map/ppermute | solution.py:188
  17.9 0.0 copy-done.4
  17.9 0.1 reshape.85
  18.0 0.1 eq.15
  18.1 0.9 collective-permute-done.1
  19.0 0.0 collective-permute-done
  19.0 9.2 %all-to-all-done = bf16[16,16,1024]{2,1,0:T(8,128)(2,1)S(1)} async-done(((bf16[16,16,1024]{2,1,0:T(8,128)(2,1)}), bf16[16,16,1024]{2,1,0:T(8,128)(2,1)S(1)}, u32[]{:S(2)}, u32[]{:S(2)}) %all-to-all-start) | async-done | bytes 524320 | tf_op jit(solution)/shard_map/all_to_all | solution.py:178
  28.2 2.5 %fusion.21 = (f32[256]{0:T(256)S(1)}, f32[256,1536]{1,0:T(8,128)S(1)}) fusion(f32[1536]{0:T(1024)S(1)} %pad_maximum_fusion.3, bf16[256,1024]{1,0:T(8,128)(2,1)S(1)} %bitcast.24, bf16[1024,768]{1,0:T(8,128)(2,1)} %collective-permute-done, bf16[1024,768]{1,0:T(8,128)(2,1)S(1)} %bitcast.37), kind=kOutput, calls=%fused_computation.43 | convolution fusion | flops 812384000 | bytes 5250048 | tf_op jit(solution)/shard_map/dot_general | solution.py:210
  30.7 0.0 copy-start.2
  30.7 0.5 exponential_reduce_fusion
  31.3 10.1 %all_to_all.23 = f32[16,2,256]{2,1,0:T(2,128)S(1)} all-to-all(f32[16,2,256]{2,1,0:T(2,128)S(1)} %broadcast_in_dim.15), channel_id=1, replica_groups={{0,2,4,6,8,10,12,14,16,18,20,22,24,26,28,30},{1,3,5,7,9,11,13,15,17,19,..., dimensions={0} | all-to-all | bytes 65536 | tf_op jit(solution)/shard_map/all_to_all | solution.py:178
  41.4 0.1 slice_reduce_fusion.2
  41.4 0.0 copy-done.2
  41.5 0.6 broadcast_in_dim.16
  42.1 15.0 %all-to-all-start.2 = ((f32[16,1,256]{2,1,0:T(1,128)}), f32[16,1,256]{2,1,0:T(1,128)S(1)}, u32[]{:S(2)}, u32[]{:S(2)}) async-start(f32[16,1,256]{2,1,0:T(1,128)} %broadcast_in_dim.16), calls=%async_computation.2 | async-start | bytes 32768 | tf_op jit(solution)/shard_map/all_to_all | solution.py:221
  57.1 0.0 copy-start.6
  57.1 2.0 %fusion.2 = f32[256,1536]{1,0:T(8,128)S(1)} fusion(f32[256,1536]{1,0:T(8,128)} %copy-done.2, f32[256]{0:T(256)S(1)} %get-tuple-element.45, s32[1536]{0:T(1024)S(1)} %pad_add_fusion, s32[256]{0:T(256)S(1)} %eq.15), kind=kLoop, calls=%fused_computation.9 | loop fusion | flops 1572864 | bytes 3153920 | tf_op jit(solution)/shard_map/sub | solution.py:225
  59.0 0.0 copy-done.6
  59.0 2.4 %fusion.22 = (bf16[256,1024]{1,0:T(8,128)(2,1)S(1)}, f32[256,1024]{1,0:T(8,128)S(1)}) fusion(bf16[1024,768]{1,0:T(8,128)(2,1)} %collective-permute-done, bf16[1024,768]{1,0:T(8,128)(2,1)S(1)} %bitcast.38, f32[256,1536]{1,0:T(8,128)S(1)} %fusion.2), kind=kOutput, calls=%fused_computation.44 | convolution fusion | flops 812253184 | bytes 6291456 | tf_op jit(solution)/shard_map/dot_general | solution.py:227
  61.5 0.9 pad.4._
  62.3 8.4 %all-to-all-done.2 = f32[16,1,256]{2,1,0:T(1,128)S(1)} async-done(((f32[16,1,256]{2,1,0:T(1,128)}), f32[16,1,256]{2,1,0:T(1,128)S(1)}, u32[]{:S(2)}, u32[]{:S(2)}) %all-to-all-start.2) | async-done | bytes 16416 | tf_op jit(solution)/shard_map/all_to_all | solution.py:221
  70.7 1.0 %shard_map.110 = (f32[256,128]{1,0:T(8,128)S(1)}, f32[1,256]{1,0:T(1,128)S(1)}, bf16[16,16,1152]{2,1,0:T(8,128)(2,1)}) custom-call(f32[16,256]{1,0:T(8,128)S(1)} %bitcast.28, f32[1,256]{1,0:T(1,128)S(1)} %bitcast.30, f32[256,1024]{1,0:T(8,128)S(1)} %get-tuple-element.23.partial_ref, bf16[256,1024]{1,0:T(8,128)(2,1)S(1)} %bitcast.25, ...), custom_call_target="tpu_custom_call", output_to_operand_aliasing={{2}: (4, {})} | custom-call | tf_op jit(solution)/shard_map/pallas_call | solution.py:71
  71.7 3.6 %all-to-all-start.3 = ((bf16[16,16,1152]{2,1,0:T(8,128)(2,1)}), bf16[16,16,1152]{2,1,0:T(8,128)(2,1)S(1)}, u32[]{:S(2)}, u32[]{:S(2)}) async-start(bf16[16,16,1152]{2,1,0:T(8,128)(2,1)} %get-tuple-element.25), calls=%async_computation.3 | async-start | bytes 1179648 | tf_op jit(solution)/shard_map/all_to_all | solution.py:178
  75.3 0.1 slice_reduce_fusion
  75.4 1.8 %convolution_convert_fusion = bf16[1024,768]{1,0:T(8,128)(2,1)} fusion(bf16[256,1024]{1,0:T(8,128)(2,1)S(1)} %bitcast.26, f32[256,1536]{1,0:T(8,128)S(1)} %fusion.2, f32[256]{0:T(256)S(1)} %slice_reduce_fusion), kind=kOutput, calls=%fused_computation.7 | convolution fusion | flops 403832832 | bytes 2884608 | tf_op jit(solution)/shard_map/dot_general | solution.py:244
  77.3 5.8 %collective-permute-start.2 = (bf16[1024,768]{1,0:T(8,128)(2,1)}, bf16[1024,768]{1,0:T(8,128)(2,1)}, u32[]{:S(2)}, u32[]{:S(2)}) collective-permute-start(bf16[1024,768]{1,0:T(8,128)(2,1)} %convolution_convert_fusion), channel_id=1, source_target_pairs={{0,1},{1,0},{2,3},{3,2},{4,5},{5,4},{6,7},{7,6},{8,9},{9,8},{10,11... | collective-permute-start | bytes 4718600 | tf_op jit(solution)/shard_map/ppermute | solution.py:247
  83.1 0.2 fusion.7
  83.3 1.9 %collective-permute-start.3 = (f32[1024]{0:T(1024)S(1)}, f32[1024]{0:T(1024)S(1)}, u32[]{:S(2)}, u32[]{:S(2)}) collective-permute-start(f32[1024]{0:T(1024)S(1)} %pad_maximum_fusion.4), channel_id=1, source_target_pairs={{0,1},{1,0},{2,3},{3,2},{4,5},{5,4},{6,7},{7,6},{8,9},{9,8},{10,11... | collective-permute-start | bytes 12296 | tf_op jit(solution)/shard_map/ppermute | solution.py:258
  85.2 1.1 %collective-permute-done.3 = f32[1024]{0:T(1024)S(1)} collective-permute-done((f32[1024]{0:T(1024)S(1)}, f32[1024]{0:T(1024)S(1)}, u32[]{:S(2)}, u32[]{:S(2)}) %collective-permute-start.3) | collective-permute-done | bytes 4128 | tf_op jit(solution)/shard_map/ppermute | solution.py:258
  86.4 0.6 broadcast_in_dim.18
  86.9 0.6 add_reduce_fusion
  88.2 0.0 collective-permute-done.2
  88.2 3.2 %fusion.3 = bf16[1,1024,768]{2,1,0:T(8,128)(2,1)} fusion(bf16[1024,768]{1,0:T(8,128)(2,1)} %collective-permute-done.2, bf16[256,1024]{1,0:T(8,128)(2,1)S(1)} %bitcast.27, f32[256,1536]{1,0:T(8,128)S(1)} %fusion.2, f32[256]{0:T(256)S(1)} %slice_reduce_fusion), kind=kOutput, calls=%fused_computation.10 | convolution fusion | flops 405405696 | bytes 4457472 | tf_op jit(solution)/shard_map/dot_general | solution.py:251
  91.4 0.0 all-to-all-done.3.tails_ref.pieces_ref
  91.5 4.2 %all-gather.1.sums_ref = f32[2,2,1024]{2,1,0:T(2,128)S(1)} all-gather(f32[1,2,1024]{2,1,0:T(2,128)S(1)} %bitcast.29), channel_id=2, replica_groups={{0,1},{2,3},{4,5},{6,7},{8,9},{10,11},{12,13},{14,15},{16,17},{18,19},{..., dimensions={0}, use_global_device_ids=true | all-gather | bytes 24576 | tf_op jit(solution)/shard_map/all_gather | solution.py:267
  95.7 0.8 shard_map.112
  (14 shorter events, 0.2 us)
Async XLA Ops:
  0.6 1.8 %copy-start = (f32[1,1024]{1,0:T(1,128)S(1)}, f32[1,1024]{1,0:T(1,128)}, u32[]{:S(2)}) copy-start(f32[1,1024]{1,0:T(1,128)} %gain_ref.3) | copy-start | bytes 12292
  0.6 1.8 %copy-start.1 = (f32[1,1024]{1,0:T(1,128)S(1)}, f32[1,1024]{1,0:T(1,128)}, u32[]{:S(2)}) copy-start(f32[1,1024]{1,0:T(1,128)} %shift_ref.3) | copy-start | bytes 12292
  0.7 11.9 %copy-start.5 = (bf16[1,1024,768]{2,1,0:T(8,128)(2,1)S(1)}, bf16[1,1024,768]{2,1,0:T(8,128)(2,1)}, u32[]{:S(2)}) copy-start(bf16[1,1024,768]{2,1,0:T(8,128)(2,1)} %param.10) | copy-start | bytes 4718596
  0.7 15.2 %copy-start.3 = (f32[1,768]{1,0:T(1,128)S(1)}, f32[1,768]{1,0:T(1,128)}, u32[]{:S(2)}) copy-start(f32[1,768]{1,0:T(1,128)} %param.11) | copy-start | bytes 9220
  0.7 17.2 %copy-start.4 = (s32[512]{0:T(512)S(1)}, s32[512]{0:T(512)}, u32[]{:S(2)}) copy-start(s32[512]{0:T(512)} %param.7) | copy-start | bytes 6148
  3.5 24.7 %all-to-all-start = ((bf16[16,16,1024]{2,1,0:T(8,128)(2,1)}), bf16[16,16,1024]{2,1,0:T(8,128)(2,1)S(1)}, u32[]{:S(2)}, u32[]{:S(2)}) async-start(bf16[16,16,1024]{2,1,0:T(8,128)(2,1)} %get-tuple-element.22), calls=%async_computation | async-start | bytes 1048576 | tf_op jit(solution)/shard_map/all_to_all | solution.py:178
  12.5 6.5 %collective-permute-start = (bf16[1024,768]{1,0:T(8,128)(2,1)S(1)}, bf16[1024,768]{1,0:T(8,128)(2,1)}, u32[]{:S(2)}, u32[]{:S(2)}) collective-permute-start(bf16[1024,768]{1,0:T(8,128)(2,1)S(1)} %bitcast.36), channel_id=1, source_target_pairs={{0,1},{1,0},{2,3},{3,2},{4,5},{5,4},{6,7},{7,6},{8,9},{9,8},{10,11... | collective-permute-start | bytes 4718600 | tf_op jit(solution)/shard_map/ppermute | solution.py:187
  15.9 3.1 %collective-permute-start.1 = (f32[768]{0:T(1024)S(1)}, f32[768]{0:T(1024)S(1)}, u32[]{:S(2)}, u32[]{:S(2)}) collective-permute-start(f32[768]{0:T(1024)S(1)} %reduce.3), channel_id=1, source_target_pairs={{0,1},{1,0},{2,3},{3,2},{4,5},{5,4},{6,7},{7,6},{8,9},{9,8},{10,11... | collective-permute-start | bytes 9224 | tf_op jit(solution)/shard_map/ppermute | solution.py:188
  30.7 10.7 %copy-start.2 = (f32[256,1536]{1,0:T(8,128)}, f32[256,1536]{1,0:T(8,128)S(1)}, u32[]{:S(2)}) copy-start(f32[256,1536]{1,0:T(8,128)S(1)} %get-tuple-element.48) | copy-start | bytes 4718596
  42.1 28.6 %all-to-all-start.2 = ((f32[16,1,256]{2,1,0:T(1,128)}), f32[16,1,256]{2,1,0:T(1,128)S(1)}, u32[]{:S(2)}, u32[]{:S(2)}) async-start(f32[16,1,256]{2,1,0:T(1,128)} %broadcast_in_dim.16), calls=%async_computation.2 | async-start | bytes 32768 | tf_op jit(solution)/shard_map/all_to_all | solution.py:221
  57.1 2.0 %copy-start.6 = (bf16[1,1024,768]{2,1,0:T(8,128)(2,1)S(1)}, bf16[1,1024,768]{2,1,0:T(8,128)(2,1)}, u32[]{:S(2)}) copy-start(bf16[1,1024,768]{2,1,0:T(8,128)(2,1)} %param.10) | copy-start | bytes 4718596
  71.7 19.7 %all-to-all-start.3 = ((bf16[16,16,1152]{2,1,0:T(8,128)(2,1)}), bf16[16,16,1152]{2,1,0:T(8,128)(2,1)S(1)}, u32[]{:S(2)}, u32[]{:S(2)}) async-start(bf16[16,16,1152]{2,1,0:T(8,128)(2,1)} %get-tuple-element.25), calls=%async_computation.3 | async-start | bytes 1179648 | tf_op jit(solution)/shard_map/all_to_all | solution.py:178
  77.3 10.9 %collective-permute-start.2 = (bf16[1024,768]{1,0:T(8,128)(2,1)}, bf16[1024,768]{1,0:T(8,128)(2,1)}, u32[]{:S(2)}, u32[]{:S(2)}) collective-permute-start(bf16[1024,768]{1,0:T(8,128)(2,1)} %convolution_convert_fusion), channel_id=1, source_target_pairs={{0,1},{1,0},{2,3},{3,2},{4,5},{5,4},{6,7},{7,6},{8,9},{9,8},{10,11... | collective-permute-start | bytes 4718600 | tf_op jit(solution)/shard_map/ppermute | solution.py:247
  83.3 3.1 %collective-permute-start.3 = (f32[1024]{0:T(1024)S(1)}, f32[1024]{0:T(1024)S(1)}, u32[]{:S(2)}, u32[]{:S(2)}) collective-permute-start(f32[1024]{0:T(1024)S(1)} %pad_maximum_fusion.4), channel_id=1, source_target_pairs={{0,1},{1,0},{2,3},{3,2},{4,5},{5,4},{6,7},{7,6},{8,9},{9,8},{10,11... | collective-permute-start | bytes 12296 | tf_op jit(solution)/shard_map/ppermute | solution.py:258

commit v7 on v6

--- a/solution.py
+++ b/solution.py
@@ -172,7 +172,11 @@
     position = lax.axis_index("dp")
     core = lax.rem(position, 2)
     swap = [(i, i ^ 1) for i in range(dp)]
-    planes = [[2 * chip + c for chip in range(chips)] for c in range(2)]
+    planes = [
+        [2 * chip for chip in range(chips)],
+        [2 * chip + 1 for chip in reversed(range(chips))],
+    ]
+    slot = jnp.where(core == 0, position // 2, chips - 1 - position // 2)
 
     def over_plane(x):
         return lax.all_to_all(x, "dp", 0, 0, axis_index_groups=planes)
@@ -197,9 +201,8 @@
     channels = normed.shape[1]
     act_plane = over_plane(act_copies).reshape(plane_images, channels)
 
-    plane_labels = lax.dynamic_index_in_dim(
-        labels.reshape(chips, 2, images_here), core, axis=1, keepdims=False
-    ).reshape(plane_images)
+    by_chip = labels.reshape(chips, 2, images_here)
+    plane_labels = jnp.where(core == 0, by_chip[:, 0], by_chip[::-1, 1]).reshape(plane_images)
     class_ids = jnp.arange(classes_here, dtype=jnp.int32)
     both_ids = jnp.concatenate(
         [position * classes_here + class_ids, (position ^ 1) * classes_here + class_ids]
@@ -266,7 +269,7 @@
     pairs = [[2 * chip, 2 * chip + 1] for chip in range(chips)]
     sums = lax.all_gather(sum_tails(pieces, channels), "dp", axis_index_groups=pairs)
     grad_pooled, grad_gain, grad_shift = close_images(
-        position // 2, pieces, scale, normed, inverse, norm_gain, norm_bias, sums
+        slot, pieces, scale, normed, inverse, norm_gain, norm_bias, sums
     )
     return (
         mean_loss,

time: 98.2 us -> 96.5 us (0.983)
  starting transfers between devices: 40.6 us -> 43.6 us
  waiting for transfers between devices: 19.6 us -> 17.2 us
  blocking collectives: 14.3 us -> 11.9 us
    all_to_all x2, starting transfers between devices: 12.6 us -> 18.9 us  [over_plane(): return lax.all_to_all(x, 'dp', 0, 0, axis_index_groups=planes)]
    ppermute x1, starting transfers between devices: 5.81 us -> 2.89 us  [per_device(): from_other = lax.ppermute(for_other, 'dp', swap)]
    all_to_all x2, waiting for transfers between devices: 9.19 us -> 6.91 us  [over_plane(): return lax.all_to_all(x, 'dp', 0, 0, axis_index_groups=planes)]
    ppermute x1, starting transfers between devices: 3.35 us -> 1.92 us  [per_device(): weight_other = lax.ppermute(weight, 'dp', swap)]
    all_gather x1, blocking collectives: 4.18 us -> 2.87 us  [per_device(): lax.all_gather(sum_tails(pieces, channels), 'dp', axis_index_groups=pairs)]
    all_to_all x1, blocking collectives: 10.1 us -> 9.01 us  [over_plane(): return lax.all_to_all(x, 'dp', 0, 0, axis_index_groups=planes)]
  transfers between devices with their start and end apart: 7 -> 7, of which waited for: 4 -> 5; matrix products, arithmetic and copies ran while one was open for 12% -> 13% of each run, Pallas kernels for 0% -> 0%
where the time goes in v7:
time: 96.5 us; the launch traced here: 95.8 us
  starting transfers between devices  43.6 us (45%)
  waiting for transfers between devices  17.2 us (18%)
  blocking collectives  11.9 us (12%)
  matrix products  10 us (10%)
  other arithmetic  5.2 us (5%)
  Pallas kernels  2.89 us (3%)
  between operations  2.7 us (3%)
  local copies, waits for them, and re-layouts  2.39 us (2%)
    all_to_all x2, starting transfers between devices, over_plane(): return lax.all_to_all(x, 'dp', 0, 0, axis_index_groups=planes)  18.9 us
    all_to_all x1, starting transfers between devices, per_device(): lax.all_to_all(jnp.broadcast_to(label_logp[None], (members, plane_images)...  15.5 us
    all_to_all x1, blocking collectives, over_plane(): return lax.all_to_all(x, 'dp', 0, 0, axis_index_groups=planes)  9.01 us
    all_to_all x1, waiting for transfers between devices, per_device(): lax.all_to_all(jnp.broadcast_to(label_logp[None], (members, plane_images)...  8.41 us
    all_to_all x2, waiting for transfers between devices, over_plane(): return lax.all_to_all(x, 'dp', 0, 0, axis_index_groups=planes)  6.91 us
    dot_general x1, matrix products, per_device(): lax.dot_general(act_plane, grad_mine.astype(jnp.bfloat16), rows, preferre...  3.24 us
    ppermute x1, starting transfers between devices, per_device(): from_other = lax.ppermute(for_other, 'dp', swap)  2.89 us
    all_gather x1, blocking collectives, per_device(): lax.all_gather(sum_tails(pieces, channels), 'dp', axis_index_groups=pairs)  2.87 us
  transfers between devices with their start and end apart: 7, of which 5 were waited for; matrix products, arithmetic and copies ran while one was open for 13% of the time, Pallas kernels for 0%

profile of v7, /device:TPU:1, one launch (start us, length us, event | category | flops | bytes accessed | tf_op | source)
XLA Modules:
  0.0 95.8 jit_solution(16020703091200504597)
XLA Ops:
  0.6 0.0 copy-start
  0.6 0.0 copy-start.1
  0.7 0.0 copy-start.5
  0.7 0.0 copy-start.3
  0.7 0.0 copy-start.4
  0.7 1.8 %convert_reduce_fusion.total_ref = f32[16,1024]{1,0:T(8,128)S(1)} fusion(bf16[1,16,49,1024]{3,1,2,0:T(8,128)(2,1)} %param.6), kind=kLoop, calls=%fused_computation | loop fusion | flops 1589248 | bytes 1671168 | tf_op jit(solution)/shard_map/reduce_sum | solution.py:195
  2.5 0.0 copy-done
  2.5 0.0 copy-done.1
  2.5 1.0 %shard_map.109 = (f32[16,1024]{1,0:T(8,128)S(1)}, f32[16,128]{1,0:T(8,128)S(1)}, bf16[16,16,1024]{2,1,0:T(8,128)(2,1)}) custom-call(f32[16,1024]{1,0:T(8,128)S(1)} %convert_reduce_fusion.total_ref, f32[1,1024]{1,0:T(1,128)S(1)} %copy-done, f32[1,1024]{1,0:T(1,128)S(1)} %copy-done.1), custom_call_target="tpu_custom_call" | custom-call | tf_op jit(solution)/shard_map/pallas_call | solution.py:29
  3.5 10.8 %all-to-all-start = ((bf16[16,16,1024]{2,1,0:T(8,128)(2,1)}), bf16[16,16,1024]{2,1,0:T(8,128)(2,1)S(1)}, u32[]{:S(2)}, u32[]{:S(2)}) async-start(bf16[16,16,1024]{2,1,0:T(8,128)(2,1)} %get-tuple-element.22), calls=%async_computation | async-start | bytes 1048576 | tf_op jit(solution)/shard_map/all_to_all | solution.py:182
  14.3 0.0 copy-done.5
  14.3 1.9 %collective-permute-start = (bf16[1024,768]{1,0:T(8,128)(2,1)S(1)}, bf16[1024,768]{1,0:T(8,128)(2,1)}, u32[]{:S(2)}, u32[]{:S(2)}) collective-permute-start(bf16[1024,768]{1,0:T(8,128)(2,1)S(1)} %bitcast.36), channel_id=1, source_target_pairs={{0,1},{1,0},{2,3},{3,2},{4,5},{5,4},{6,7},{7,6},{8,9},{9,8},{10,11... | collective-permute-start | bytes 4718600 | tf_op jit(solution)/shard_map/ppermute | solution.py:191
  16.3 0.0 copy-done.3
  16.3 2.4 %collective-permute-start.1 = (f32[768]{0:T(1024)S(1)}, f32[768]{0:T(1024)S(1)}, u32[]{:S(2)}, u32[]{:S(2)}) collective-permute-start(f32[768]{0:T(1024)S(1)} %reduce.3), channel_id=1, source_target_pairs={{0,1},{1,0},{2,3},{3,2},{4,5},{5,4},{6,7},{7,6},{8,9},{9,8},{10,11... | collective-permute-start | bytes 9224 | tf_op jit(solution)/shard_map/ppermute | solution.py:192
  18.7 0.0 copy-done.4
  18.7 0.1 reshape.94
  18.9 0.1 select_n.30
  19.0 0.7 collective-permute-done.1
  19.6 0.1 collective-permute-done
  19.8 6.9 %all-to-all-done = bf16[16,16,1024]{2,1,0:T(8,128)(2,1)S(1)} async-done(((bf16[16,16,1024]{2,1,0:T(8,128)(2,1)}), bf16[16,16,1024]{2,1,0:T(8,128)(2,1)S(1)}, u32[]{:S(2)}, u32[]{:S(2)}) %all-to-all-start) | async-done | bytes 524320 | tf_op jit(solution)/shard_map/all_to_all | solution.py:182
  26.7 2.5 %fusion.22 = (f32[256]{0:T(256)S(1)}, f32[256,1536]{1,0:T(8,128)S(1)}) fusion(f32[1536]{0:T(1024)S(1)} %pad_maximum_fusion.3, bf16[256,1024]{1,0:T(8,128)(2,1)S(1)} %bitcast.24, bf16[1024,768]{1,0:T(8,128)(2,1)} %collective-permute-done, bf16[1024,768]{1,0:T(8,128)(2,1)S(1)} %bitcast.37), kind=kOutput, calls=%fused_computation.44 | convolution fusion | flops 812384000 | bytes 5250048 | tf_op jit(solution)/shard_map/dot_general | solution.py:213
  29.2 0.0 copy-start.2
  29.2 0.5 exponential_reduce_fusion
  29.7 9.0 %all_to_all.23 = f32[16,2,256]{2,1,0:T(2,128)S(1)} all-to-all(f32[16,2,256]{2,1,0:T(2,128)S(1)} %broadcast_in_dim.15), channel_id=1, replica_groups={{0,2,4,6,8,10,12,14,16,18,20,22,24,26,28,30},{31,29,27,25,23,21,19,17,1..., dimensions={0} | all-to-all | bytes 65536 | tf_op jit(solution)/shard_map/all_to_all | solution.py:182
  38.7 0.1 slice_reduce_fusion.2
  38.8 0.0 copy-done.2
  38.8 0.6 broadcast_in_dim.16
  39.5 15.5 %all-to-all-start.2 = ((f32[16,1,256]{2,1,0:T(1,128)}), f32[16,1,256]{2,1,0:T(1,128)S(1)}, u32[]{:S(2)}, u32[]{:S(2)}) async-start(f32[16,1,256]{2,1,0:T(1,128)} %broadcast_in_dim.16), calls=%async_computation.2 | async-start | bytes 32768 | tf_op jit(solution)/shard_map/all_to_all | solution.py:224
  55.0 0.0 copy-start.6
  55.0 2.0 %fusion.2 = f32[256,1536]{1,0:T(8,128)S(1)} fusion(f32[256,1536]{1,0:T(8,128)} %copy-done.2, f32[256]{0:T(256)S(1)} %get-tuple-element.45, s32[1536]{0:T(1024)S(1)} %pad_add_fusion, s32[256]{0:T(256)S(1)} %select_n.30), kind=kLoop, calls=%fused_computation.9 | loop fusion | flops 1572864 | bytes 3153920 | tf_op jit(solution)/shard_map/sub | solution.py:228
  57.0 0.0 copy-done.6
  57.0 2.4 %fusion.23 = (bf16[256,1024]{1,0:T(8,128)(2,1)S(1)}, f32[256,1024]{1,0:T(8,128)S(1)}) fusion(bf16[1024,768]{1,0:T(8,128)(2,1)} %collective-permute-done, bf16[1024,768]{1,0:T(8,128)(2,1)S(1)} %bitcast.38, f32[256,1536]{1,0:T(8,128)S(1)} %fusion.2), kind=kOutput, calls=%fused_computation.45 | convolution fusion | flops 812253184 | bytes 6291456 | tf_op jit(solution)/shard_map/dot_general | solution.py:230
  59.4 0.9 pad.4._
  60.3 8.4 %all-to-all-done.2 = f32[16,1,256]{2,1,0:T(1,128)S(1)} async-done(((f32[16,1,256]{2,1,0:T(1,128)}), f32[16,1,256]{2,1,0:T(1,128)S(1)}, u32[]{:S(2)}, u32[]{:S(2)}) %all-to-all-start.2) | async-done | bytes 16416 | tf_op jit(solution)/shard_map/all_to_all | solution.py:224
  68.7 1.0 %shard_map.110 = (f32[256,128]{1,0:T(8,128)S(1)}, f32[1,256]{1,0:T(1,128)S(1)}, bf16[16,16,1152]{2,1,0:T(8,128)(2,1)}) custom-call(f32[16,256]{1,0:T(8,128)S(1)} %bitcast.28, f32[1,256]{1,0:T(1,128)S(1)} %bitcast.30, f32[256,1024]{1,0:T(8,128)S(1)} %get-tuple-element.23.partial_ref, bf16[256,1024]{1,0:T(8,128)(2,1)S(1)} %bitcast.25, ...), custom_call_target="tpu_custom_call", output_to_operand_aliasing={{2}: (4, {})} | custom-call | tf_op jit(solution)/shard_map/pallas_call | solution.py:71
  69.7 8.1 %all-to-all-start.3 = ((bf16[16,16,1152]{2,1,0:T(8,128)(2,1)}), bf16[16,16,1152]{2,1,0:T(8,128)(2,1)S(1)}, u32[]{:S(2)}, u32[]{:S(2)}) async-start(bf16[16,16,1152]{2,1,0:T(8,128)(2,1)} %get-tuple-element.25), calls=%async_computation.3 | async-start | bytes 1179648 | tf_op jit(solution)/shard_map/all_to_all | solution.py:182
  77.8 0.1 slice_reduce_fusion
  77.9 1.8 %convolution_convert_fusion = bf16[1024,768]{1,0:T(8,128)(2,1)} fusion(bf16[256,1024]{1,0:T(8,128)(2,1)S(1)} %bitcast.26, f32[256,1536]{1,0:T(8,128)S(1)} %fusion.2, f32[256]{0:T(256)S(1)} %slice_reduce_fusion), kind=kOutput, calls=%fused_computation.7 | convolution fusion | flops 403832832 | bytes 2884608 | tf_op jit(solution)/shard_map/dot_general | solution.py:247
  79.7 2.9 %collective-permute-start.2 = (bf16[1024,768]{1,0:T(8,128)(2,1)}, bf16[1024,768]{1,0:T(8,128)(2,1)}, u32[]{:S(2)}, u32[]{:S(2)}) collective-permute-start(bf16[1024,768]{1,0:T(8,128)(2,1)} %convolution_convert_fusion), channel_id=1, source_target_pairs={{0,1},{1,0},{2,3},{3,2},{4,5},{5,4},{6,7},{7,6},{8,9},{9,8},{10,11... | collective-permute-start | bytes 4718600 | tf_op jit(solution)/shard_map/ppermute | solution.py:250
  82.6 0.2 fusion.7
  82.8 1.9 %collective-permute-start.3 = (f32[1024]{0:T(1024)S(1)}, f32[1024]{0:T(1024)S(1)}, u32[]{:S(2)}, u32[]{:S(2)}) collective-permute-start(f32[1024]{0:T(1024)S(1)} %pad_maximum_fusion.4), channel_id=1, source_target_pairs={{0,1},{1,0},{2,3},{3,2},{4,5},{5,4},{6,7},{7,6},{8,9},{9,8},{10,11... | collective-permute-start | bytes 12296 | tf_op jit(solution)/shard_map/ppermute | solution.py:261
  84.8 1.1 %collective-permute-done.3 = f32[1024]{0:T(1024)S(1)} collective-permute-done((f32[1024]{0:T(1024)S(1)}, f32[1024]{0:T(1024)S(1)}, u32[]{:S(2)}, u32[]{:S(2)}) %collective-permute-start.3) | collective-permute-done | bytes 4128 | tf_op jit(solution)/shard_map/ppermute | solution.py:261
  85.9 0.6 broadcast_in_dim.18
  86.5 0.6 add_reduce_fusion
  87.7 0.0 collective-permute-done.2
  87.7 3.2 %fusion.3 = bf16[1,1024,768]{2,1,0:T(8,128)(2,1)} fusion(bf16[1024,768]{1,0:T(8,128)(2,1)} %collective-permute-done.2, bf16[256,1024]{1,0:T(8,128)(2,1)S(1)} %bitcast.27, f32[256,1536]{1,0:T(8,128)S(1)} %fusion.2, f32[256]{0:T(256)S(1)} %slice_reduce_fusion), kind=kOutput, calls=%fused_computation.10 | convolution fusion | flops 405405696 | bytes 4457472 | tf_op jit(solution)/shard_map/dot_general | solution.py:254
  91.0 0.0 all-to-all-done.3.tails_ref.pieces_ref
  91.0 2.9 %all-gather.1.sums_ref = f32[2,2,1024]{2,1,0:T(2,128)S(1)} all-gather(f32[1,2,1024]{2,1,0:T(2,128)S(1)} %bitcast.29), channel_id=2, replica_groups={{0,1},{2,3},{4,5},{6,7},{8,9},{10,11},{12,13},{14,15},{16,17},{18,19},{..., dimensions={0}, use_global_device_ids=true | all-gather | bytes 24576 | tf_op jit(solution)/shard_map/all_gather | solution.py:270
  93.9 0.8 shard_map.112
  (15 shorter events, 0.2 us)
Async XLA Ops:
  0.6 1.8 %copy-start = (f32[1,1024]{1,0:T(1,128)S(1)}, f32[1,1024]{1,0:T(1,128)}, u32[]{:S(2)}) copy-start(f32[1,1024]{1,0:T(1,128)} %gain_ref.3) | copy-start | bytes 12292
  0.6 1.8 %copy-start.1 = (f32[1,1024]{1,0:T(1,128)S(1)}, f32[1,1024]{1,0:T(1,128)}, u32[]{:S(2)}) copy-start(f32[1,1024]{1,0:T(1,128)} %shift_ref.3) | copy-start | bytes 12292
  0.7 13.7 %copy-start.5 = (bf16[1,1024,768]{2,1,0:T(8,128)(2,1)S(1)}, bf16[1,1024,768]{2,1,0:T(8,128)(2,1)}, u32[]{:S(2)}) copy-start(bf16[1,1024,768]{2,1,0:T(8,128)(2,1)} %param.10) | copy-start | bytes 4718596
  0.7 15.6 %copy-start.3 = (f32[1,768]{1,0:T(1,128)S(1)}, f32[1,768]{1,0:T(1,128)}, u32[]{:S(2)}) copy-start(f32[1,768]{1,0:T(1,128)} %param.11) | copy-start | bytes 9220
  0.7 18.0 %copy-start.4 = (s32[512]{0:T(512)S(1)}, s32[512]{0:T(512)}, u32[]{:S(2)}) copy-start(s32[512]{0:T(512)} %param.7) | copy-start | bytes 6148
  3.5 23.2 %all-to-all-start = ((bf16[16,16,1024]{2,1,0:T(8,128)(2,1)}), bf16[16,16,1024]{2,1,0:T(8,128)(2,1)S(1)}, u32[]{:S(2)}, u32[]{:S(2)}) async-start(bf16[16,16,1024]{2,1,0:T(8,128)(2,1)} %get-tuple-element.22), calls=%async_computation | async-start | bytes 1048576 | tf_op jit(solution)/shard_map/all_to_all | solution.py:182
  14.3 5.4 %collective-permute-start = (bf16[1024,768]{1,0:T(8,128)(2,1)S(1)}, bf16[1024,768]{1,0:T(8,128)(2,1)}, u32[]{:S(2)}, u32[]{:S(2)}) collective-permute-start(bf16[1024,768]{1,0:T(8,128)(2,1)S(1)} %bitcast.36), channel_id=1, source_target_pairs={{0,1},{1,0},{2,3},{3,2},{4,5},{5,4},{6,7},{7,6},{8,9},{9,8},{10,11... | collective-permute-start | bytes 4718600 | tf_op jit(solution)/shard_map/ppermute | solution.py:191
  16.3 3.3 %collective-permute-start.1 = (f32[768]{0:T(1024)S(1)}, f32[768]{0:T(1024)S(1)}, u32[]{:S(2)}, u32[]{:S(2)}) collective-permute-start(f32[768]{0:T(1024)S(1)} %reduce.3), channel_id=1, source_target_pairs={{0,1},{1,0},{2,3},{3,2},{4,5},{5,4},{6,7},{7,6},{8,9},{9,8},{10,11... | collective-permute-start | bytes 9224 | tf_op jit(solution)/shard_map/ppermute | solution.py:192
  29.2 9.7 %copy-start.2 = (f32[256,1536]{1,0:T(8,128)}, f32[256,1536]{1,0:T(8,128)S(1)}, u32[]{:S(2)}) copy-start(f32[256,1536]{1,0:T(8,128)S(1)} %get-tuple-element.48) | copy-start | bytes 4718596
  39.5 29.2 %all-to-all-start.2 = ((f32[16,1,256]{2,1,0:T(1,128)}), f32[16,1,256]{2,1,0:T(1,128)S(1)}, u32[]{:S(2)}, u32[]{:S(2)}) async-start(f32[16,1,256]{2,1,0:T(1,128)} %broadcast_in_dim.16), calls=%async_computation.2 | async-start | bytes 32768 | tf_op jit(solution)/shard_map/all_to_all | solution.py:224
  55.0 2.0 %copy-start.6 = (bf16[1,1024,768]{2,1,0:T(8,128)(2,1)S(1)}, bf16[1,1024,768]{2,1,0:T(8,128)(2,1)}, u32[]{:S(2)}) copy-start(bf16[1,1024,768]{2,1,0:T(8,128)(2,1)} %param.10) | copy-start | bytes 4718596
  69.7 21.3 %all-to-all-start.3 = ((bf16[16,16,1152]{2,1,0:T(8,128)(2,1)}), bf16[16,16,1152]{2,1,0:T(8,128)(2,1)S(1)}, u32[]{:S(2)}, u32[]{:S(2)}) async-start(bf16[16,16,1152]{2,1,0:T(8,128)(2,1)} %get-tuple-element.25), calls=%async_computation.3 | async-start | bytes 1179648 | tf_op jit(solution)/shard_map/all_to_all | solution.py:182
  79.7 8.0 %collective-permute-start.2 = (bf16[1024,768]{1,0:T(8,128)(2,1)}, bf16[1024,768]{1,0:T(8,128)(2,1)}, u32[]{:S(2)}, u32[]{:S(2)}) collective-permute-start(bf16[1024,768]{1,0:T(8,128)(2,1)} %convolution_convert_fusion), channel_id=1, source_target_pairs={{0,1},{1,0},{2,3},{3,2},{4,5},{5,4},{6,7},{7,6},{8,9},{9,8},{10,11... | collective-permute-start | bytes 4718600 | tf_op jit(solution)/shard_map/ppermute | solution.py:250
  82.8 3.1 %collective-permute-start.3 = (f32[1024]{0:T(1024)S(1)}, f32[1024]{0:T(1024)S(1)}, u32[]{:S(2)}, u32[]{:S(2)}) collective-permute-start(f32[1024]{0:T(1024)S(1)} %pad_maximum_fusion.4), channel_id=1, source_target_pairs={{0,1},{1,0},{2,3},{3,2},{4,5},{5,4},{6,7},{7,6},{8,9},{9,8},{10,11... | collective-permute-start | bytes 12296 | tf_op jit(solution)/shard_map/ppermute | solution.py:261

commit v8 on v7

--- a/solution.py
+++ b/solution.py
@@ -172,11 +172,10 @@
     position = lax.axis_index("dp")
     core = lax.rem(position, 2)
     swap = [(i, i ^ 1) for i in range(dp)]
-    planes = [
-        [2 * chip for chip in range(chips)],
-        [2 * chip + 1 for chip in reversed(range(chips))],
-    ]
-    slot = jnp.where(core == 0, position // 2, chips - 1 - position // 2)
+    order = [(7 * k) % chips for k in range(chips)]
+    planes = [[2 * chip for chip in order], [2 * chip + 1 for chip in reversed(order)]]
+    forth = jnp.sum(jnp.where(jnp.array(order) == position // 2, jnp.arange(chips), 0))
+    slot = jnp.where(core == 0, forth, chips - 1 - forth).astype(jnp.int32)
 
     def over_plane(x):
         return lax.all_to_all(x, "dp", 0, 0, axis_index_groups=planes)
@@ -202,7 +201,11 @@
     act_plane = over_plane(act_copies).reshape(plane_images, channels)
 
     by_chip = labels.reshape(chips, 2, images_here)
-    plane_labels = jnp.where(core == 0, by_chip[:, 0], by_chip[::-1, 1]).reshape(plane_images)
+    plane_labels = jnp.where(
+        core == 0,
+        jnp.concatenate([by_chip[chip, 0] for chip in order]),
+        jnp.concatenate([by_chip[chip, 1] for chip in reversed(order)]),
+    )
     class_ids = jnp.arange(classes_here, dtype=jnp.int32)
     both_ids = jnp.concatenate(
         [position * classes_here + class_ids, (position ^ 1) * classes_here + class_ids]

time: 96.5 us -> 96.6 us (level)
  waiting for transfers between devices: 17.2 us -> 14.6 us
  between operations: 2.7 us -> 4.03 us
    ppermute x1, starting transfers between devices: 2.89 us -> 6.67 us  [per_device(): from_other = lax.ppermute(for_other, 'dp', swap)]
    all_to_all x2, starting transfers between devices: 18.9 us -> 15.8 us  [over_plane(): return lax.all_to_all(x, 'dp', 0, 0, axis_index_groups=planes)]
    all_to_all x2, waiting for transfers between devices: 6.91 us -> 5.41 us  [over_plane(): return lax.all_to_all(x, 'dp', 0, 0, axis_index_groups=planes)]
    ppermute x1, waiting for transfers between devices: 1.11 us -> 0.01 us  [per_device(): note = lax.ppermute(note, 'dp', swap)]
  transfers between devices with their start and end apart: 7 -> 7, of which waited for: 5 -> 3; matrix products, arithmetic and copies ran while one was open for 13% -> 13% of each run, Pallas kernels for 0% -> 0%
where the time goes in v8:
time: 96.6 us; the launch traced here: 96 us
  starting transfers between devices  44.4 us (46%)
  waiting for transfers between devices  14.6 us (15%)
  blocking collectives  11.8 us (12%)
  matrix products  9.98 us (10%)
  other arithmetic  5.81 us (6%)
  between operations  4.03 us (4%)
  Pallas kernels  2.89 us (3%)
  local copies, waits for them, and re-layouts  2.5 us (3%)
    all_to_all x2, starting transfers between devices, over_plane(): return lax.all_to_all(x, 'dp', 0, 0, axis_index_groups=planes)  15.8 us
    all_to_all x1, starting transfers between devices, per_device(): lax.all_to_all(jnp.broadcast_to(label_logp[None], (members, plane_images)...  15.5 us
    all_to_all x1, blocking collectives, over_plane(): return lax.all_to_all(x, 'dp', 0, 0, axis_index_groups=planes)  9.8 us
    all_to_all x1, waiting for transfers between devices, per_device(): lax.all_to_all(jnp.broadcast_to(label_logp[None], (members, plane_images)...  8.38 us
    ppermute x1, starting transfers between devices, per_device(): from_other = lax.ppermute(for_other, 'dp', swap)  6.67 us
    all_to_all x2, waiting for transfers between devices, over_plane(): return lax.all_to_all(x, 'dp', 0, 0, axis_index_groups=planes)  5.41 us
    dot_general x1, matrix products, per_device(): lax.dot_general(act_plane, grad_mine.astype(jnp.bfloat16), rows, preferre...  3.24 us
    ppermute x1, starting transfers between devices, per_device(): weight_other = lax.ppermute(weight, 'dp', swap)  2.53 us
  transfers between devices with their start and end apart: 7, of which 3 were waited for; matrix products, arithmetic and copies ran while one was open for 13% of the time, Pallas kernels for 0%

profile of v8, /device:TPU:1, one launch (start us, length us, event | category | flops | bytes accessed | tf_op | source)
XLA Modules:
  0.0 96.0 jit_solution(12892275068583518418)
XLA Ops:
  0.6 0.0 copy-start
  0.6 0.0 copy-start.1
  0.7 0.0 copy-start.5
  0.7 0.0 copy-start.3
  0.7 0.0 copy-start.4
  0.7 1.8 %convert_reduce_fusion.total_ref = f32[16,1024]{1,0:T(8,128)S(1)} fusion(bf16[1,16,49,1024]{3,1,2,0:T(8,128)(2,1)} %param.7), kind=kLoop, calls=%fused_computation | loop fusion | flops 1589248 | bytes 1671168 | tf_op jit(solution)/shard_map/reduce_sum | solution.py:194
  2.5 0.0 copy-done
  2.5 0.0 copy-done.1
  2.5 1.0 %shard_map.118 = (f32[16,1024]{1,0:T(8,128)S(1)}, f32[16,128]{1,0:T(8,128)S(1)}, bf16[16,16,1024]{2,1,0:T(8,128)(2,1)}) custom-call(f32[16,1024]{1,0:T(8,128)S(1)} %convert_reduce_fusion.total_ref, f32[1,1024]{1,0:T(1,128)S(1)} %copy-done, f32[1,1024]{1,0:T(1,128)S(1)} %copy-done.1), custom_call_target="tpu_custom_call" | custom-call | tf_op jit(solution)/shard_map/pallas_call | solution.py:29
  3.5 9.8 %all-to-all-start = ((bf16[16,16,1024]{2,1,0:T(8,128)(2,1)}), bf16[16,16,1024]{2,1,0:T(8,128)(2,1)S(1)}, u32[]{:S(2)}, u32[]{:S(2)}) async-start(bf16[16,16,1024]{2,1,0:T(8,128)(2,1)} %get-tuple-element.22), calls=%async_computation | async-start | bytes 1048576 | tf_op jit(solution)/shard_map/all_to_all | solution.py:181
  13.3 0.0 copy-done.5
  13.4 2.5 %collective-permute-start = (bf16[1024,768]{1,0:T(8,128)(2,1)S(1)}, bf16[1024,768]{1,0:T(8,128)(2,1)}, u32[]{:S(2)}, u32[]{:S(2)}) collective-permute-start(bf16[1024,768]{1,0:T(8,128)(2,1)S(1)} %bitcast.100), channel_id=1, source_target_pairs={{0,1},{1,0},{2,3},{3,2},{4,5},{5,4},{6,7},{7,6},{8,9},{9,8},{10,11... | collective-permute-start | bytes 4718600 | tf_op jit(solution)/shard_map/ppermute | solution.py:190
  15.9 0.0 copy-done.3
  15.9 1.9 %collective-permute-start.1 = (f32[768]{0:T(1024)S(1)}, f32[768]{0:T(1024)S(1)}, u32[]{:S(2)}, u32[]{:S(2)}) collective-permute-start(f32[768]{0:T(1024)S(1)} %reduce.3), channel_id=1, source_target_pairs={{0,1},{1,0},{2,3},{3,2},{4,5},{5,4},{6,7},{7,6},{8,9},{9,8},{10,11... | collective-permute-start | bytes 9224 | tf_op jit(solution)/shard_map/ppermute | solution.py:191
  17.9 0.0 copy-done.4
  17.9 0.1 reshape.340
  18.0 0.1 concatenate.108
  18.1 0.1 concatenate.125
  18.2 0.8 collective-permute-done.1
  19.0 0.0 collective-permute-done
  19.0 5.4 %all-to-all-done = bf16[16,16,1024]{2,1,0:T(8,128)(2,1)S(1)} async-done(((bf16[16,16,1024]{2,1,0:T(8,128)(2,1)}), bf16[16,16,1024]{2,1,0:T(8,128)(2,1)S(1)}, u32[]{:S(2)}, u32[]{:S(2)}) %all-to-all-start) | async-done | bytes 524320 | tf_op jit(solution)/shard_map/all_to_all | solution.py:181
  24.4 2.5 %fusion.22 = (f32[256]{0:T(256)S(1)}, f32[256,1536]{1,0:T(8,128)S(1)}) fusion(f32[1536]{0:T(1024)S(1)} %pad_maximum_fusion.3, bf16[256,1024]{1,0:T(8,128)(2,1)S(1)} %bitcast.88, bf16[1024,768]{1,0:T(8,128)(2,1)} %collective-permute-done, bf16[1024,768]{1,0:T(8,128)(2,1)S(1)} %bitcast.101), kind=kOutput, calls=%fused_computation.77 | convolution fusion | flops 812384000 | bytes 5250048 | tf_op jit(solution)/shard_map/dot_general | solution.py:216
  26.9 0.0 copy-start.2
  26.9 0.5 exponential_reduce_fusion
  27.5 9.8 %all_to_all.23 = f32[16,2,256]{2,1,0:T(2,128)S(1)} all-to-all(f32[16,2,256]{2,1,0:T(2,128)S(1)} %broadcast_in_dim.19), channel_id=1, replica_groups={{0,14,28,10,24,6,20,2,16,30,12,26,8,22,4,18},{19,5,23,9,27,13,31,17,3,2..., dimensions={0} | all-to-all | bytes 65536 | tf_op jit(solution)/shard_map/all_to_all | solution.py:181
  37.3 0.1 slice_reduce_fusion.2
  37.4 0.0 copy-done.2
  37.4 0.6 broadcast_in_dim.20
  38.0 15.5 %all-to-all-start.2 = ((f32[16,1,256]{2,1,0:T(1,128)}), f32[16,1,256]{2,1,0:T(1,128)S(1)}, u32[]{:S(2)}, u32[]{:S(2)}) async-start(f32[16,1,256]{2,1,0:T(1,128)} %broadcast_in_dim.20), calls=%async_computation.2 | async-start | bytes 32768 | tf_op jit(solution)/shard_map/all_to_all | solution.py:227
  53.5 0.0 copy-start.6
  53.5 2.0 %fusion.2 = f32[256,1536]{1,0:T(8,128)S(1)} fusion(f32[256,1536]{1,0:T(8,128)} %copy-done.2, f32[256]{0:T(256)S(1)} %get-tuple-element.45, s32[1536]{0:T(1024)S(1)} %pad_add_fusion, s32[256]{0:T(256)S(1)} %broadcast_select_fusion), kind=kLoop, calls=%fused_computation.9 | loop fusion | flops 1572864 | bytes 3153920 | tf_op jit(solution)/shard_map/sub | solution.py:231
  55.5 0.0 copy-done.6
  55.5 2.4 %fusion.23 = (bf16[256,1024]{1,0:T(8,128)(2,1)S(1)}, f32[256,1024]{1,0:T(8,128)S(1)}) fusion(bf16[1024,768]{1,0:T(8,128)(2,1)} %collective-permute-done, bf16[1024,768]{1,0:T(8,128)(2,1)S(1)} %bitcast.102, f32[256,1536]{1,0:T(8,128)S(1)} %fusion.2), kind=kOutput, calls=%fused_computation.78 | convolution fusion | flops 812253184 | bytes 6291456 | tf_op jit(solution)/shard_map/dot_general | solution.py:233
  57.9 0.9 pad.4._
  58.8 8.4 %all-to-all-done.2 = f32[16,1,256]{2,1,0:T(1,128)S(1)} async-done(((f32[16,1,256]{2,1,0:T(1,128)}), f32[16,1,256]{2,1,0:T(1,128)S(1)}, u32[]{:S(2)}, u32[]{:S(2)}) %all-to-all-start.2) | async-done | bytes 16416 | tf_op jit(solution)/shard_map/all_to_all | solution.py:227
  67.2 1.0 %shard_map.119 = (f32[256,128]{1,0:T(8,128)S(1)}, f32[1,256]{1,0:T(1,128)S(1)}, bf16[16,16,1152]{2,1,0:T(8,128)(2,1)}) custom-call(f32[16,256]{1,0:T(8,128)S(1)} %bitcast.92, f32[1,256]{1,0:T(1,128)S(1)} %bitcast.94, f32[256,1024]{1,0:T(8,128)S(1)} %get-tuple-element.23.partial_ref, bf16[256,1024]{1,0:T(8,128)(2,1)S(1)} %bitcast.89, ...), custom_call_target="tpu_custom_call", output_to_operand_aliasing={{2}: (4, {})} | custom-call | tf_op jit(solution)/shard_map/pallas_call | solution.py:71
  68.2 6.0 %all-to-all-start.3 = ((bf16[16,16,1152]{2,1,0:T(8,128)(2,1)}), bf16[16,16,1152]{2,1,0:T(8,128)(2,1)S(1)}, u32[]{:S(2)}, u32[]{:S(2)}) async-start(bf16[16,16,1152]{2,1,0:T(8,128)(2,1)} %get-tuple-element.25), calls=%async_computation.3 | async-start | bytes 1179648 | tf_op jit(solution)/shard_map/all_to_all | solution.py:181
  74.2 0.1 slice_reduce_fusion
  74.3 0.0 copy-start.7
  74.3 1.8 %convolution_convert_fusion = bf16[1024,768]{1,0:T(8,128)(2,1)} fusion(bf16[256,1024]{1,0:T(8,128)(2,1)S(1)} %bitcast.90, f32[256,1536]{1,0:T(8,128)S(1)} %fusion.2, f32[256]{0:T(256)S(1)} %slice_reduce_fusion), kind=kOutput, calls=%fused_computation.7 | convolution fusion | flops 403832832 | bytes 2884608 | tf_op jit(solution)/shard_map/dot_general | solution.py:250
  76.1 6.7 %collective-permute-start.2 = (bf16[1024,768]{1,0:T(8,128)(2,1)}, bf16[1024,768]{1,0:T(8,128)(2,1)}, u32[]{:S(2)}, u32[]{:S(2)}) collective-permute-start(bf16[1024,768]{1,0:T(8,128)(2,1)} %convolution_convert_fusion), channel_id=1, source_target_pairs={{0,1},{1,0},{2,3},{3,2},{4,5},{5,4},{6,7},{7,6},{8,9},{9,8},{10,11... | collective-permute-start | bytes 4718600 | tf_op jit(solution)/shard_map/ppermute | solution.py:253
  82.8 0.2 fusion.7
  83.0 1.9 %collective-permute-start.3 = (f32[1024]{0:T(1024)S(1)}, f32[1024]{0:T(1024)S(1)}, u32[]{:S(2)}, u32[]{:S(2)}) collective-permute-start(f32[1024]{0:T(1024)S(1)} %pad_maximum_fusion.4), channel_id=1, source_target_pairs={{0,1},{1,0},{2,3},{3,2},{4,5},{5,4},{6,7},{7,6},{8,9},{9,8},{10,11... | collective-permute-start | bytes 12296 | tf_op jit(solution)/shard_map/ppermute | solution.py:264
  84.9 0.0 copy-done.7
  85.0 0.6 fusion.18
  86.9 0.0 collective-permute-done.3
  86.9 0.6 broadcast_in_dim.40
  87.5 0.6 add_reduce_fusion
  88.7 0.0 collective-permute-done.2
  88.8 3.2 %fusion.3 = bf16[1,1024,768]{2,1,0:T(8,128)(2,1)} fusion(bf16[1024,768]{1,0:T(8,128)(2,1)} %collective-permute-done.2, bf16[256,1024]{1,0:T(8,128)(2,1)S(1)} %bitcast.91, f32[256,1536]{1,0:T(8,128)S(1)} %fusion.2, f32[256]{0:T(256)S(1)} %slice_reduce_fusion), kind=kOutput, calls=%fused_computation.10 | convolution fusion | flops 405405696 | bytes 4457472 | tf_op jit(solution)/shard_map/dot_general | solution.py:257
  92.0 0.0 all-to-all-done.3.tails_ref.pieces_ref
  92.0 2.0 %all-gather.1.sums_ref = f32[2,2,1024]{2,1,0:T(2,128)S(1)} all-gather(f32[1,2,1024]{2,1,0:T(2,128)S(1)} %bitcast.93), channel_id=2, replica_groups={{0,1},{2,3},{4,5},{6,7},{8,9},{10,11},{12,13},{14,15},{16,17},{18,19},{..., dimensions={0}, use_global_device_ids=true | all-gather | bytes 24576 | tf_op jit(solution)/shard_map/all_gather | solution.py:273
  94.0 0.8 shard_map.121
  (16 shorter events, 0.2 us)
Async XLA Ops:
  0.6 1.8 %copy-start = (f32[1,1024]{1,0:T(1,128)S(1)}, f32[1,1024]{1,0:T(1,128)}, u32[]{:S(2)}) copy-start(f32[1,1024]{1,0:T(1,128)} %gain_ref.3) | copy-start | bytes 12292
  0.6 1.8 %copy-start.1 = (f32[1,1024]{1,0:T(1,128)S(1)}, f32[1,1024]{1,0:T(1,128)}, u32[]{:S(2)}) copy-start(f32[1,1024]{1,0:T(1,128)} %shift_ref.3) | copy-start | bytes 12292
  0.7 12.7 %copy-start.5 = (bf16[1,1024,768]{2,1,0:T(8,128)(2,1)S(1)}, bf16[1,1024,768]{2,1,0:T(8,128)(2,1)}, u32[]{:S(2)}) copy-start(bf16[1,1024,768]{2,1,0:T(8,128)(2,1)} %param.11) | copy-start | bytes 4718596
  0.7 15.2 %copy-start.3 = (f32[1,768]{1,0:T(1,128)S(1)}, f32[1,768]{1,0:T(1,128)}, u32[]{:S(2)}) copy-start(f32[1,768]{1,0:T(1,128)} %param.12) | copy-start | bytes 9220
  0.7 17.2 %copy-start.4 = (s32[512]{0:T(512)S(1)}, s32[512]{0:T(512)}, u32[]{:S(2)}) copy-start(s32[512]{0:T(512)} %param.8) | copy-start | bytes 6148
  3.5 20.9 %all-to-all-start = ((bf16[16,16,1024]{2,1,0:T(8,128)(2,1)}), bf16[16,16,1024]{2,1,0:T(8,128)(2,1)S(1)}, u32[]{:S(2)}, u32[]{:S(2)}) async-start(bf16[16,16,1024]{2,1,0:T(8,128)(2,1)} %get-tuple-element.22), calls=%async_computation | async-start | bytes 1048576 | tf_op jit(solution)/shard_map/all_to_all | solution.py:181
  13.4 5.7 %collective-permute-start = (bf16[1024,768]{1,0:T(8,128)(2,1)S(1)}, bf16[1024,768]{1,0:T(8,128)(2,1)}, u32[]{:S(2)}, u32[]{:S(2)}) collective-permute-start(bf16[1024,768]{1,0:T(8,128)(2,1)S(1)} %bitcast.100), channel_id=1, source_target_pairs={{0,1},{1,0},{2,3},{3,2},{4,5},{5,4},{6,7},{7,6},{8,9},{9,8},{10,11... | collective-permute-start | bytes 4718600 | tf_op jit(solution)/shard_map/ppermute | solution.py:190
  15.9 3.1 %collective-permute-start.1 = (f32[768]{0:T(1024)S(1)}, f32[768]{0:T(1024)S(1)}, u32[]{:S(2)}, u32[]{:S(2)}) collective-permute-start(f32[768]{0:T(1024)S(1)} %reduce.3), channel_id=1, source_target_pairs={{0,1},{1,0},{2,3},{3,2},{4,5},{5,4},{6,7},{7,6},{8,9},{9,8},{10,11... | collective-permute-start | bytes 9224 | tf_op jit(solution)/shard_map/ppermute | solution.py:191
  26.9 10.4 %copy-start.2 = (f32[256,1536]{1,0:T(8,128)}, f32[256,1536]{1,0:T(8,128)S(1)}, u32[]{:S(2)}) copy-start(f32[256,1536]{1,0:T(8,128)S(1)} %get-tuple-element.80) | copy-start | bytes 4718596
  38.0 29.2 %all-to-all-start.2 = ((f32[16,1,256]{2,1,0:T(1,128)}), f32[16,1,256]{2,1,0:T(1,128)S(1)}, u32[]{:S(2)}, u32[]{:S(2)}) async-start(f32[16,1,256]{2,1,0:T(1,128)} %broadcast_in_dim.20), calls=%async_computation.2 | async-start | bytes 32768 | tf_op jit(solution)/shard_map/all_to_all | solution.py:227
  53.5 2.0 %copy-start.6 = (bf16[1,1024,768]{2,1,0:T(8,128)(2,1)S(1)}, bf16[1,1024,768]{2,1,0:T(8,128)(2,1)}, u32[]{:S(2)}) copy-start(bf16[1,1024,768]{2,1,0:T(8,128)(2,1)} %param.11) | copy-start | bytes 4718596
  68.2 23.8 %all-to-all-start.3 = ((bf16[16,16,1152]{2,1,0:T(8,128)(2,1)}), bf16[16,16,1152]{2,1,0:T(8,128)(2,1)S(1)}, u32[]{:S(2)}, u32[]{:S(2)}) async-start(bf16[16,16,1152]{2,1,0:T(8,128)(2,1)} %get-tuple-element.25), calls=%async_computation.3 | async-start | bytes 1179648 | tf_op jit(solution)/shard_map/all_to_all | solution.py:181
  74.3 10.7 %copy-start.7 = (s32[16]{0:T(128)S(1)}, s32[16]{0:T(128)}, u32[]{:S(2)}) copy-start(s32[16]{0:T(128)} %constant.37.clone) | copy-start | bytes 196
  76.1 12.6 %collective-permute-start.2 = (bf16[1024,768]{1,0:T(8,128)(2,1)}, bf16[1024,768]{1,0:T(8,128)(2,1)}, u32[]{:S(2)}, u32[]{:S(2)}) collective-permute-start(bf16[1024,768]{1,0:T(8,128)(2,1)} %convolution_convert_fusion), channel_id=1, source_target_pairs={{0,1},{1,0},{2,3},{3,2},{4,5},{5,4},{6,7},{7,6},{8,9},{9,8},{10,11... | collective-permute-start | bytes 4718600 | tf_op jit(solution)/shard_map/ppermute | solution.py:253
  83.0 3.9 %collective-permute-start.3 = (f32[1024]{0:T(1024)S(1)}, f32[1024]{0:T(1024)S(1)}, u32[]{:S(2)}, u32[]{:S(2)}) collective-permute-start(f32[1024]{0:T(1024)S(1)} %pad_maximum_fusion.4), channel_id=1, source_target_pairs={{0,1},{1,0},{2,3},{3,2},{4,5},{5,4},{6,7},{7,6},{8,9},{9,8},{10,11... | collective-permute-start | bytes 12296 | tf_op jit(solution)/shard_map/ppermute | solution.py:264
